TPU v7x, 32 devices: a whole 2x2x4 slice. The times are simulated.
32 devices in a mesh: seq: 8 (over z, y), dp: 4 (over x, core).
Axes of the slice: x: 2, y: 2, z: 4, core: 2. Of those that a mesh axis runs over, the one named last changes fastest.
Arguments:
- queries: bfloat16 [4, 1024, 1024], P('dp', 'seq'), may hold values from -150 to 150
- key_states: bfloat16 [4, 1024, 1024], P('dp', 'seq'), may hold values from -6 to 6
- values: bfloat16 [4, 1024, 1024], P('dp', 'seq'), may hold values from -6 to 6
- w_out: bfloat16 [1024, 1024], replicated, may hold values from -0.1875 to 0.1875
- cotangent: bfloat16 [4, 1024, 1024], P('dp', 'seq'), may hold values from -6 to 6
- neighbours: int32 [4, 8, 2], P('dp', 'seq'), may hold values from 0 to 7, as said below
- counts: int32 [4, 8], P('dp', 'seq'), may hold values from 1 to 2
Outputs:
- output: bfloat16 [4, 1024, 1024], P('dp', 'seq')
- grad_queries: bfloat16 [4, 1024, 1024], P('dp', 'seq')
- grad_keys: bfloat16 [4, 1024, 1024], P('dp', 'seq')
- grad_values: bfloat16 [4, 1024, 1024], P('dp', 'seq')
- grad_w_out: float32 [1024, 1024], P(('seq', 'dp'))
Inputs may be any that keep to these rules, and one draw needn't show every extreme that they name: `neighbours`: entries j < counts[s, p] of patch p's list are distinct patches other than p, at most 1 patches away from p; the later entries equal p.
All inputs are finite; a program needn't handle non-finite values.
Results may differ from a plain program's by a relative error of at most 0.029.
Values may be sent and summed in bfloat16 or wider, within the bound.
No kernel may reach another device: no remote copies, remote signals or barrier semaphores. Data moves between devices by JAX's collectives and lax.ppermute only.
A program may use at most 64 MiB of HBM per device.

v0:
```python
import functools
import math

import jax
import jax.numpy as jnp
from jax import lax
from jax.experimental import pallas as pl
from jax.experimental.pallas import tpu as pltpu
from jax.sharding import PartitionSpec as P

HD = 128
VMEM_LIMIT = 12 * 1024 * 1024
F32 = jnp.float32
BF16 = jnp.bfloat16
VMEM = pl.BlockSpec(memory_space=pltpu.VMEM)
HBM = pl.BlockSpec(memory_space=pltpu.HBM)
ANY = pl.BlockSpec(memory_space=pl.ANY)
FLAG_ROWS = 16


def dot(a, b, ca, cb):
    return lax.dot_general(a, b, (((ca,), (cb,)), ((), ())), preferred_element_type=F32)


def bit_reversed(index, bits):
    out = 0
    for b in range(bits):
        out = out * 2 + ((index >> b) & 1)
    return out


def shape_of(*dims, dtype=BF16):
    return jax.ShapeDtypeStruct(dims, dtype)


def call(body, out_shape, in_specs, name, scratch=()):
    return pl.pallas_call(
        body,
        out_shape=out_shape,
        in_specs=in_specs,
        out_specs=(VMEM,) * len(out_shape),
        scratch_shapes=list(scratch),
        compiler_params=pltpu.CompilerParams(vmem_limit_bytes=VMEM_LIMIT),
        cost_estimate=pl.CostEstimate(flops=0, bytes_accessed=0, transcendentals=0),
        name=name,
    )


def head_cols(pair, parity):
    return pl.ds(pl.multiple_of((2 * pair + parity) * HD, HD), HD)


def listed_flags(me, listed):
    far_patch = jnp.where(me % 2 == 0, me - 1, me + 1)
    near, far = jnp.int32(0), jnp.int32(0)
    for slot in range(listed.shape[1]):
        near = jnp.where(listed[0, slot] == (me ^ 1), 1, near)
        far = jnp.where(listed[0, slot] == far_patch, 1, far)
    return near, far


def in_hbm(x):
    return pltpu.with_memory_space_constraint(x, pltpu.HBM)


def pack_kernel(listed, q, k, v, kv_send, kv_keep, q_send, q_keep, listed_in, sems):
    mine = lax.axis_index("seq") & 1
    tokens, half = q_keep.shape[0] - FLAG_ROWS, q_keep.shape[1]
    copies = []

    def copy(source, target):
        copies.append(pltpu.make_async_copy(source, target, sems.at[len(copies)]))
        copies[-1].start()

    copy(listed, listed_in)
    for kv, q_to, parity in ((kv_send, q_send, 1 - mine), (kv_keep, q_keep, mine)):
        for source, target, row in ((k, kv, 0), (v, kv, tokens), (q, q_to, 0)):
            for j in range(half // HD):
                copy(
                    source.at[:, head_cols(j, parity)],
                    target.at[row : row + tokens, j * HD : (j + 1) * HD],
                )
    copies[0].wait()
    near, far = listed_flags(lax.axis_index("seq"), listed_in)
    left = lax.broadcasted_iota(jnp.int32, (FLAG_ROWS, half), 1) < half // 2
    flags = jnp.where(left, near, far).astype(F32).astype(BF16)
    q_send[tokens : tokens + FLAG_ROWS, :] = flags
    q_keep[tokens : tokens + FLAG_ROWS, :] = flags
    for item in copies[1:]:
        item.wait()


def pack(listed, q, k, v):
    tokens, features = k.shape
    half = features // 2
    kv = shape_of(2 * tokens, half)
    return call(
        pack_kernel,
        (kv, kv) + (shape_of(tokens + FLAG_ROWS, half),) * 2,
        [HBM] * 4,
        "pack_heads",
        scratch=[
            pltpu.SMEM(listed.shape, jnp.int32),
            pltpu.SemaphoreType.DMA((3 * features // HD + 1,)),
        ],
    )(*[in_hbm(x) for x in (listed, q, k, v)])


def turn_kernel(cot, cot_par, w, ga, cot_in, w_in, sems):
    tokens = cot.shape[0]
    pairs = ga.shape[1] // HD
    copies = [pltpu.make_async_copy(cot, cot_in, sems.at[pairs])]
    for j in range(pairs):
        rows = w.at[head_cols(j, lax.axis_index("seq") & 1), :]
        copies.append(pltpu.make_async_copy(rows, w_in.at[j], sems.at[j]))
    for item in copies:
        item.start()
    copies[0].wait()
    for j in range(pairs):
        cols = slice(j * HD, (j + 1) * HD)
        copies[j + 1].wait()
        ga[:tokens, cols] = dot(cot_in[...], w_in[j], 1, 1).astype(BF16)
        ga[tokens:, cols] = dot(cot_par[...], w_in[j], 1, 1).astype(BF16)


def grad_attended(cot, cot_par, w):
    tokens, width = cot.shape
    pairs = w.shape[0] // (2 * HD)
    return call(
        turn_kernel,
        (shape_of(2 * tokens, pairs * HD),),
        [HBM, VMEM, HBM],
        "grad_attended",
        scratch=[
            pltpu.VMEM((tokens, width), BF16),
            pltpu.VMEM((pairs, HD, width), BF16),
            pltpu.SemaphoreType.DMA((pairs + 1,)),
        ],
    )(in_hbm(cot), cot_par, in_hbm(w))[0]


def far_slot(me):
    return (me & 1) ^ ((me >> 1) & 1)


def forward_kernel(
    direct, n_dp, q_own, q_par, own, par, far_own, far_par, after,
    probs, att_own, att_back, att_t,
):
    rate = math.log2(math.e) / math.sqrt(HD)
    tokens, half = q_own.shape[0] - FLAG_ROWS, q_own.shape[1]
    pairs = half // HD
    me = lax.axis_index("seq")
    left = lax.broadcasted_iota(jnp.int32, (1, 2 * tokens), 1) < tokens

    def barred(x, place):
        flag = x[tokens : tokens + FLAG_ROWS, :].astype(F32)[:1, place : place + 1]
        return jnp.where(jnp.broadcast_to(flag, (1, 2 * tokens)) > 0, 0.0, -jnp.inf)

    bias = (
        jnp.where(left, 0.0, barred(q_par, 0)),
        jnp.where(left, barred(q_own, 0), 0.0),
        jnp.where(left, barred(q_own, half - 1), barred(q_par, half - 1)),
    )
    for j in range(pairs):
        cols = slice(j * HD, (j + 1) * HD)
        qo, qp = q_own[:tokens, cols], q_par[:tokens, cols]
        q = jnp.concatenate([qo, qp], axis=0)
        k = jnp.concatenate([own[:tokens, cols], par[:tokens, cols]], axis=0)
        v = jnp.concatenate([own[tokens:, cols], par[tokens:, cols]], axis=0)
        near = dot(k, q, 1, 1)
        far = jnp.concatenate(
            [dot(far_own[:tokens, cols], qo, 1, 1), dot(far_par[:tokens, cols], qp, 1, 1)], axis=1
        )
        s = [near[:tokens] + bias[0], near[tokens:] + bias[1], far + bias[2]]
        top = jnp.max(jnp.maximum(jnp.maximum(s[0], s[1]), s[2]), axis=0, keepdims=True)
        e = [jnp.exp2((x - top) * rate) for x in s]
        inv = 1.0 / jnp.sum(e[0] + e[1] + e[2], axis=0, keepdims=True)
        low = [(x * inv).astype(BF16) for x in e]
        for i in range(3):
            probs[j, i * tokens : (i + 1) * tokens, :] = low[i]
        vfo, vfp = far_own[tokens:, cols], far_par[tokens:, cols]
        o_t = dot(v, jnp.concatenate(low[:2], axis=0), 0, 0)
        o_t += jnp.concatenate(
            [dot(vfo, low[2][:, :tokens], 0, 0), dot(vfp, low[2][:, tokens:], 0, 0)], axis=1
        )
        o = o_t.T.astype(BF16)
        att_own[:, cols] = o[:tokens]
        att_back[:, cols] = o[tokens:]
        o_low = o_t.astype(BF16)
        if direct:
            rows = HD // n_dp
            place = bit_reversed(j ^ (me >> 1), (pairs - 1).bit_length())
            for d in range(n_dp):
                block = bit_reversed((d ^ lax.axis_index("dp")) >> 1, (n_dp // 2 - 1).bit_length())
                start = pl.multiple_of((block * pairs + place) * rows, rows)
                att_t[(d ^ lax.axis_index("dp")) & 1, pl.ds(start, rows), :] = o_low[d * rows : (d + 1) * rows, :]
        else:
            att_t[cols, :] = o_low


def forward(inputs, after, n_seq, n_dp):
    tokens, half = inputs[0].shape[0] - FLAG_ROWS, inputs[0].shape[1]
    features = 2 * half
    heads, pairs = features // HD, half // HD
    direct = n_seq == heads and HD % n_dp == 0 and (HD // n_dp) % 16 == 0
    one = shape_of(tokens, half)
    turned = shape_of(2, half // 2, 2 * tokens) if direct else shape_of(half, 2 * tokens)
    probs, att_own, att_back, turned = call(
        functools.partial(forward_kernel, direct, n_dp),
        (shape_of(pairs, 3 * tokens, 2 * tokens), one, one, turned),
        [VMEM] * 6 + [ANY],
        "patch_forward",
    )(*inputs, after)
    if not direct:
        here = lax.axis_index("seq")
        bits, d_bits = (n_seq - 1).bit_length(), (n_dp // 2 - 1).bit_length()
        order = jnp.array([bit_reversed(i, bits) for i in range(n_seq)], jnp.int32) ^ here
        d_order = [bit_reversed(i, d_bits) * 2 + c for c in range(2) for i in range(n_dp // 2)]
        full = jnp.zeros((heads // 2, 2, HD, 2 * tokens), BF16)
        full = lax.dynamic_update_slice(
            full, turned.reshape(heads // 2, 1, HD, 2 * tokens), (0, here & 1, 0, 0)
        )
        full = full.reshape(n_seq, n_dp, features // (n_seq * n_dp), 2 * tokens)
        full = jnp.take(full, order, axis=0)
        full = jnp.take(full, jnp.array(d_order, jnp.int32) ^ lax.axis_index("dp"), axis=1).transpose(1, 0, 2, 3)
        turned = full.reshape(2, features // 2, 2 * tokens)
    return probs, att_own, att_back, turned, 2 if direct else 1


def backward_kernel(
    q_own, q_par, own, par, far_own, far_par, ga, probs, _after, grads, edge_a, edge_b
):
    scale = 1.0 / math.sqrt(HD)
    tokens, half = q_own.shape[0] - FLAG_ROWS, q_own.shape[1]
    slot = far_slot(lax.axis_index("seq"))
    last = slice(2 * tokens, 3 * tokens)
    for j in range(half // HD):
        cols = slice(j * HD, (j + 1) * HD)
        g_both = ga[:, cols]
        go, gp = g_both[:tokens], g_both[tokens:]
        qo, qp = q_own[:tokens, cols], q_par[:tokens, cols]
        v = jnp.concatenate([own[tokens:, cols], par[tokens:, cols]], axis=0)
        vfo, vfp = far_own[tokens:, cols], far_par[tokens:, cols]
        gn = dot(v, g_both, 1, 1)
        g = [
            gn[:tokens],
            gn[tokens:],
            jnp.concatenate([dot(vfo, go, 1, 1), dot(vfp, gp, 1, 1)], axis=1),
        ]
        p = [probs[j, i * tokens : (i + 1) * tokens, :].astype(F32) for i in range(3)]
        delta = jnp.sum(p[0] * g[0] + p[1] * g[1] + p[2] * g[2], axis=0, keepdims=True)
        ds = [(p[i] * (g[i] - delta)).astype(BF16) for i in range(3)]
        for i in range(3):
            grads[j, i * tokens : (i + 1) * tokens, :] = ds[i]
        dfo, dfp = ds[2][:, :tokens], ds[2][:, tokens:]
        own_far = jnp.concatenate(
            [dot(dfo, qo, 1, 0) * scale, dot(probs[j, last, :tokens], go, 1, 0)], axis=0
        ).astype(BF16)
        par_far = jnp.concatenate(
            [dot(dfp, qp, 1, 0) * scale, dot(probs[j, last, tokens:], gp, 1, 0)], axis=0
        ).astype(BF16)
        edge_a[:, cols] = jnp.where(slot == 0, own_far, par_far)
        edge_b[:, cols] = jnp.where(slot == 0, par_far, own_far)


def backward(inputs, ga, probs, after):
    tokens, half = inputs[0].shape[0] - FLAG_ROWS, inputs[0].shape[1]
    return call(
        backward_kernel,
        (shape_of(*probs.shape),) + (shape_of(2 * tokens, half),) * 2,
        [VMEM] * 8 + [ANY],
        "patch_backward",
    )(*inputs, ga, probs, after)


def gradient_kernel(
    q_own, q_par, own, par, far_own, far_par, ga, probs, grads, dq_own, dq_back, d_own, d_par
):
    scale = 1.0 / math.sqrt(HD)
    tokens, half = q_own.shape[0] - FLAG_ROWS, q_own.shape[1]
    near, last = slice(0, 2 * tokens), slice(2 * tokens, 3 * tokens)
    for j in range(half // HD):
        cols = slice(j * HD, (j + 1) * HD)
        q = jnp.concatenate([q_own[:tokens, cols], q_par[:tokens, cols]], axis=0)
        k = jnp.concatenate([own[:tokens, cols], par[:tokens, cols]], axis=0)
        kfo, kfp = far_own[:tokens, cols], far_par[:tokens, cols]
        low, dsn = probs[j, near, :], grads[j, near, :]
        dfo, dfp = grads[j, last, :tokens], grads[j, last, tokens:]
        dq = dot(dsn, k, 0, 0) + jnp.concatenate([dot(dfo, kfo, 0, 0), dot(dfp, kfp, 0, 0)], axis=0)
        dq = (dq * scale).astype(BF16)
        dq_own[:, cols] = dq[:tokens]
        dq_back[:, cols] = dq[tokens:]
        dk = (dot(dsn, q, 1, 0) * scale).astype(BF16)
        dv = dot(low, ga[:, cols], 1, 0).astype(BF16)
        d_own[:tokens, cols] = dk[:tokens]
        d_par[:tokens, cols] = dk[tokens:]
        d_own[tokens:, cols] = dv[:tokens]
        d_par[tokens:, cols] = dv[tokens:]


def gradients(inputs, ga, probs, grads):
    tokens, half = inputs[0].shape[0] - FLAG_ROWS, inputs[0].shape[1]
    one, kv = shape_of(tokens, half), shape_of(2 * tokens, half)
    return call(
        gradient_kernel, (one, one, kv, kv), [VMEM] * 9, "patch_gradients"
    )(*inputs, ga, probs, grads)


def weight_kernel(att_keep, att_core, own, par, core_own, core_par, keep, send):
    size = keep.shape[0]
    tokens = own.shape[0]
    for target, start in ((send, size), (keep, 0)):
        rows = slice(start, start + size)
        total = dot(att_keep[rows, :tokens], own[...], 1, 0)
        total += dot(att_keep[rows, tokens:], par[...], 1, 0)
        total += dot(att_core[rows, :tokens], core_own[...], 1, 0)
        total += dot(att_core[rows, tokens:], core_par[...], 1, 0)
        target[...] = total.astype(target.dtype)


def weight_terms(*operands):
    rows = operands[0].shape[0]
    tokens, width = operands[2].shape
    return call(
        weight_kernel,
        (shape_of(rows // 2, width, dtype=F32), shape_of(rows // 2, width)),
        [VMEM] * 6,
        "weight_terms",
    )(*operands)


def query_kernel(att_own, att_back, dq_own, dq_back, w, out, dq, att):
    mine = lax.axis_index("seq") & 1
    for j in range(att_own.shape[1] // HD):
        cols = slice(j * HD, (j + 1) * HD)
        att[:, head_cols(j, mine)] = att_own[:, cols]
        att[:, head_cols(j, 1 - mine)] = att_back[:, cols]
        dq[:, head_cols(j, mine)] = dq_own[:, cols]
        dq[:, head_cols(j, 1 - mine)] = dq_back[:, cols]
    out[...] = dot(att[...], w[...], 1, 0).astype(BF16)


def finish_queries(att_own, att_back, dq_own, dq_back, w):
    tokens = att_own.shape[0]
    return call(
        query_kernel,
        (shape_of(tokens, w.shape[1]), shape_of(tokens, w.shape[0])),
        [VMEM] * 5,
        "finish_queries",
        scratch=[pltpu.VMEM((tokens, w.shape[0]), BF16)],
    )(att_own, att_back, dq_own, dq_back, w)


def returned_kernel(d_par, far_a, far_b, total):
    slot = far_slot(lax.axis_index("seq"))
    returned = jnp.where(slot == 0, far_b[...].astype(F32), far_a[...].astype(F32))
    total[...] = (d_par[...].astype(F32) + returned).astype(BF16)


def add_returned(d_par, far):
    return call(
        returned_kernel, (shape_of(*d_par.shape),), [VMEM] * 3, "add_returned"
    )(d_par, *far)[0]


def key_kernel(own, far_a, far_b, home, keep, out, dk, dv, total):
    mine = lax.axis_index("seq") & 1
    slot = far_slot(lax.axis_index("seq"))
    tokens = dk.shape[0]
    for i, target in ((0, dk), (1, dv)):
        rows = slice(i * tokens, (i + 1) * tokens)
        for j in range(own.shape[1] // HD):
            cols = slice(j * HD, (j + 1) * HD)
            far = jnp.where(slot == 0, far_a[rows, cols].astype(F32), far_b[rows, cols].astype(F32))
            target[:, head_cols(j, mine)] = (own[rows, cols].astype(F32) + far).astype(BF16)
            target[:, head_cols(j, 1 - mine)] = home[rows, cols]
    total[...] = keep[...] + out[...].astype(F32)


def finish_keys(own, far, home, keep, out):
    tokens, half = own.shape[0] // 2, own.shape[1]
    return call(
        key_kernel,
        (shape_of(tokens, 2 * half),) * 2 + (shape_of(*keep.shape, dtype=F32),),
        [VMEM] * 6,
        "finish_keys",
    )(own, *far, home, keep, out)


def on_device(queries, key_states, values, w_out, cotangent, neighbours, counts):
    n_seq, n_dp = lax.axis_size("seq"), lax.axis_size("dp")
    cot = cotangent[0]

    swap = [(i, i ^ 1) for i in range(n_seq)]
    relay = [(i, i + 2) for i in range(0, n_seq, 2) if i + 2 < n_seq]
    relay += [(i, i - 2) for i in range(1, n_seq, 2) if i - 2 >= 0]
    outer = [(b, a) for a, b in relay]
    edges = [[], []]
    for i in range(n_seq):
        edges[1].append((i, i ^ 2))
        other = i + 2 if (i >> 1) & 1 else i - 2
        if 0 <= other < n_seq:
            edges[0].append((i, other))
    send = lambda x, pairs: lax.ppermute(x, "seq", pairs)
    across = lambda x, k: lax.ppermute(x, "dp", [(i, i ^ k) for i in range(n_dp)])

    kv_send, own, q_send, q_own = pack(
        neighbours[0], queries[0], key_states[0], values[0]
    )
    par = send(kv_send, swap)
    q_par = send(q_send, swap)
    far_par = send(own, outer)
    cot_par = send(cot, swap)
    far_own = send(par, relay)
    core_own, core_par = across(cot, 1), across(cot_par, 1)
    ga = grad_attended(cot, cot_par, w_out)

    inputs = (q_own, q_par, own, par, far_own, far_par)
    probs, att_own, att_back, att_t, step = forward(
        inputs, ga, n_seq, n_dp
    )
    att_core = across(att_t[1], 1)
    att_back = send(att_back, swap)
    keep, out = weight_terms(att_t[0], att_core, cot, cot_par, core_own, core_par)
    grads, *leaving = backward(inputs, ga, probs, keep)
    far = [send(leaving[i], edges[i]) for i in range(2)]
    dq_own, dq_back, d_own, d_par = gradients(inputs, ga, probs, grads)
    dq_back = send(dq_back, swap)
    home = send(add_returned(d_par, far), swap)

    hops = []
    bit = 2
    while bit < n_dp:
        hops.append(("dp", n_dp, bit))
        bit *= 2
    while step < n_seq:
        hops.append(("seq", n_seq, step))
        step *= 2
    for place, (axis, count, bit) in enumerate(hops):
        out = lax.ppermute(out, axis, [(i, i ^ bit) for i in range(count)])
        if place + 1 < len(hops):
            total = keep + out.astype(F32)
            rows = total.shape[0] // 2
            keep, out = total[:rows], total[rows:].astype(BF16)

    output, dq = finish_queries(att_own, att_back, dq_own, dq_back, w_out)
    dk, dv, total = finish_keys(d_own, far, home, keep, out)
    return (output[None], dq[None], dk[None], dv[None], total)


def solution(mesh):
    placed = (
        P("dp", "seq", None),
        P("dp", "seq", None),
        P("dp", "seq", None),
        P(),
        P("dp", "seq", None),
        P("dp", "seq", None),
        P("dp", "seq"),
    )
    return jax.shard_map(
        on_device,
        mesh=mesh,
        in_specs=placed,
        out_specs=(
            P("dp", "seq", None),
            P("dp", "seq", None),
            P("dp", "seq", None),
            P("dp", "seq", None),
            P(("seq", "dp"), None),
        ),
        check_vma=False,
    )
```

profile of v0, /device:TPU:0, one launch (start us, length us, event | category | flops | bytes accessed | tf_op | source)
XLA Modules:
  0.0 49.4 jit_solution(11124141598123809144)
XLA Ops:
  0.6 1.3 %pack_heads.1 = (bf16[256,512]{1,0:T(8,128)(2,1)S(1)}, bf16[256,512]{1,0:T(8,128)(2,1)S(1)}, bf16[144,512]{1,0:T(8,128)(2,1)S(1)}, bf16[144,512]{1,0:T(8,128)(2,1)S(1)}) custom-call(s32[1,2]{1,0:T(1,128)} %bitcast.20, bf16[128,1024]{1,0:T(8,128)(2,1)} %bitcast.17, bf16[128,1024]{1,0:T(8,128)(2,1)} %bitcast.18, bf16[128,1024]{1,0:T(8,128)(2,1)} %bitcast.19), custom_call_target="tpu_custom_call" | custom-call | tf_op jit(solution)/shard_map/pack_heads/pallas_call | solution.py:97
  2.0 3.0 %collective-permute-start.1 = (bf16[256,512]{1,0:T(8,128)(2,1)S(1)}, bf16[256,512]{1,0:T(8,128)(2,1)S(1)}, u32[]{:S(2)}, u32[]{:S(2)}) collective-permute-start(bf16[256,512]{1,0:T(8,128)(2,1)S(1)} %get-tuple-element.30), channel_id=1, source_target_pairs={{0,4},{4,0},{8,12},{12,8},{16,20},{20,16},{24,28},{28,24},{1,5},{5... | collective-permute-start | bytes 786440 | tf_op jit(solution)/shard_map/ppermute | solution.py:405
  5.0 0.1 collective-permute-start.4
  5.1 1.3 %collective-permute-start.3 = (bf16[256,512]{1,0:T(8,128)(2,1)S(1)}, bf16[256,512]{1,0:T(8,128)(2,1)S(1)}, u32[]{:S(2)}, u32[]{:S(2)}) collective-permute-start(bf16[256,512]{1,0:T(8,128)(2,1)S(1)} %get-tuple-element.29.own), channel_id=1, source_target_pairs={{8,0},{16,8},{24,16},{4,12},{12,20},{20,28},{9,1},{17,9},{25,17},{... | collective-permute-start | bytes 786440 | tf_op jit(solution)/shard_map/ppermute | solution.py:405
  6.4 5.8 %collective-permute-done.1.par = bf16[256,512]{1,0:T(8,128)(2,1)S(1)} collective-permute-done((bf16[256,512]{1,0:T(8,128)(2,1)S(1)}, bf16[256,512]{1,0:T(8,128)(2,1)S(1)}, u32[]{:S(2)}, u32[]{:S(2)}) %collective-permute-start.1) | collective-permute-done | bytes 262176 | tf_op jit(solution)/shard_map/ppermute | solution.py:405
  12.1 4.0 %collective-permute-start.2 = (bf16[256,512]{1,0:T(8,128)(2,1)S(1)}, bf16[256,512]{1,0:T(8,128)(2,1)S(1)}, u32[]{:S(2)}, u32[]{:S(2)}) collective-permute-start(bf16[256,512]{1,0:T(8,128)(2,1)S(1)} %collective-permute-done.1.par), channel_id=1, source_target_pairs={{0,8},{8,16},{16,24},{12,4},{20,12},{28,20},{1,9},{9,17},{17,25},{... | collective-permute-start | bytes 786440 | tf_op jit(solution)/shard_map/ppermute | solution.py:405
  16.2 0.0 copy-start.1
  16.2 0.1 collective-permute-start
  16.3 0.1 collective-permute-start.7
  16.3 1.1 %collective-permute-done.4.cot_par.par = bf16[128,1024]{1,0:T(8,128)(2,1)S(1)} collective-permute-done((bf16[128,1024]{1,0:T(8,128)(2,1)}, bf16[128,1024]{1,0:T(8,128)(2,1)S(1)}, u32[]{:S(2)}, u32[]{:S(2)}) %collective-permute-start.4) | collective-permute-done | bytes 262176 | tf_op jit(solution)/shard_map/ppermute | solution.py:405
  17.4 0.0 collective-permute-start.8
  17.4 2.3 %grad_attended.1.after.ga = bf16[256,512]{1,0:T(8,128)(2,1)S(1)} custom-call(bf16[128,1024]{1,0:T(8,128)(2,1)} %bitcast.15, bf16[128,1024]{1,0:T(8,128)(2,1)S(1)} %collective-permute-done.4.cot_par.par, bf16[1024,1024]{1,0:T(8,128)(2,1)} %w.3), custom_call_target="tpu_custom_call" | custom-call | tf_op jit(solution)/shard_map/grad_attended/pallas_call | solution.py:129
  19.8 1.6 %collective-permute-done.q_par = bf16[144,512]{1,0:T(8,128)(2,1)S(1)} collective-permute-done((bf16[144,512]{1,0:T(8,128)(2,1)S(1)}, bf16[144,512]{1,0:T(8,128)(2,1)S(1)}, u32[]{:S(2)}, u32[]{:S(2)}) %collective-permute-start) | collective-permute-done | bytes 147488 | tf_op jit(solution)/shard_map/ppermute | solution.py:405
  21.4 0.0 collective-permute-done.3.far_par
  21.4 0.0 collective-permute-done.2.far_own
  21.4 1.6 %patch_forward.1 = (bf16[4,384,256]{2,1,0:T(8,128)(2,1)S(1)}, bf16[128,512]{1,0:T(8,128)(2,1)S(1)}, bf16[128,512]{1,0:T(8,128)(2,1)S(1)}, bf16[2,256,256]{2,1,0:T(8,128)(2,1)S(1)}) custom-call(bf16[144,512]{1,0:T(8,128)(2,1)S(1)} %get-tuple-element.27.q_own, bf16[144,512]{1,0:T(8,128)(2,1)S(1)} %collective-permute-done.q_par, ...), custom_call_target="tpu_custom_call" | custom-call | tf_op jit(solution)/shard_map/patch_forward/pallas_call | solution.py:209
  23.0 0.1 collective-permute-start.6
  23.1 0.0 collective-permute-done.7.core_own
  23.1 0.0 collective-permute-done.8.core_par
  23.1 1.3 %collective-permute-done.6.att_core = bf16[256,256]{1,0:T(8,128)(2,1)S(1)} collective-permute-done((bf16[256,256]{1,0:T(8,128)(2,1)S(1)}, bf16[256,256]{1,0:T(8,128)(2,1)S(1)}, u32[]{:S(2)}, u32[]{:S(2)}) %collective-permute-start.6) | collective-permute-done | bytes 131104 | tf_op jit(solution)/shard_map/ppermute | solution.py:406
  24.4 0.0 copy-done.1
  24.4 0.7 %weight_terms.1 = (f32[128,1024]{1,0:T(8,128)S(1)}, bf16[128,1024]{1,0:T(8,128)(2,1)S(1)}) custom-call(bf16[256,256]{1,0:T(8,128)(2,1)S(1)} %get-tuple-element.50.att_keep, bf16[256,256]{1,0:T(8,128)(2,1)S(1)} %collective-permute-done.6.att_core, bf16[128,1024]{1,0:T(8,128)(2,1)S(1)} %bitcast.16, bf16[128,1024]{1,0:T(8,128)(2,1)S(1)} %collective-permute-done.4.cot_par.par, ...), custom_call_target="tpu_custom_call" | custom-call | tf_op jit(solution)/shard_map/weight_terms/pallas_call | solution.py:325
  25.1 1.6 %collective-permute-start.13 = (bf16[128,1024]{1,0:T(8,128)(2,1)S(1)}, bf16[128,1024]{1,0:T(8,128)(2,1)S(1)}, u32[]{:S(2)}, u32[]{:S(2)}) collective-permute-start(bf16[128,1024]{1,0:T(8,128)(2,1)S(1)} %get-tuple-element.45), channel_id=1, source_target_pairs={{0,2},{1,3},{2,0},{3,1},{4,6},{5,7},{6,4},{7,5},{8,10},{9,11},{10,... | collective-permute-start | bytes 786440 | tf_op jit(solution)/shard_map/ppermute | solution.py:441
  26.7 1.3 %patch_backward.1 = (bf16[4,384,256]{2,1,0:T(8,128)(2,1)S(1)}, bf16[256,512]{1,0:T(8,128)(2,1)S(1)}, bf16[256,512]{1,0:T(8,128)(2,1)S(1)}) custom-call(bf16[144,512]{1,0:T(8,128)(2,1)S(1)} %get-tuple-element.27.q_own, bf16[144,512]{1,0:T(8,128)(2,1)S(1)} %collective-permute-done.q_par, bf16[256,512]{1,0:T(8,128)(2,1)S(1)} %get-tuple-element.29.own, ...), custom_call_target="tpu_custom_call" | custom-call | tf_op jit(solution)/shard_map/patch_backward/pallas_call | solution.py:269
  28.0 0.7 %collective-permute-start.10 = (bf16[256,512]{1,0:T(8,128)(2,1)S(1)}, bf16[256,512]{1,0:T(8,128)(2,1)S(1)}, u32[]{:S(2)}, u32[]{:S(2)}) collective-permute-start(bf16[256,512]{1,0:T(8,128)(2,1)S(1)} %get-tuple-element.42), channel_id=1, source_target_pairs={{8,16},{12,20},{16,8},{20,12},{9,17},{13,21},{17,9},{21,13},{10,18... | collective-permute-start | bytes 786440 | tf_op jit(solution)/shard_map/ppermute | solution.py:405
  28.7 4.4 %collective-permute-start.11 = (bf16[256,512]{1,0:T(8,128)(2,1)S(1)}, bf16[256,512]{1,0:T(8,128)(2,1)S(1)}, u32[]{:S(2)}, u32[]{:S(2)}) collective-permute-start(bf16[256,512]{1,0:T(8,128)(2,1)S(1)} %get-tuple-element.43), channel_id=1, source_target_pairs={{0,8},{4,12},{8,0},{12,4},{16,24},{20,28},{24,16},{28,20},{1,9},{5... | collective-permute-start | bytes 786440 | tf_op jit(solution)/shard_map/ppermute | solution.py:405
  33.2 0.4 collective-permute-done.13
  33.6 0.1 convert_add_fusion
  33.6 1.6 %collective-permute-start.14 = (bf16[64,1024]{1,0:T(8,128)(2,1)S(1)}, bf16[64,1024]{1,0:T(8,128)(2,1)S(1)}, u32[]{:S(2)}, u32[]{:S(2)}) collective-permute-start(bf16[64,1024]{1,0:T(8,128)(2,1)S(1)} %slice.35), channel_id=1, source_target_pairs={{0,8},{4,12},{8,0},{12,4},{16,24},{20,28},{24,16},{28,20},{1,9},{5... | collective-permute-start | bytes 393224 | tf_op jit(solution)/shard_map/ppermute | solution.py:441
  35.3 1.2 %collective-permute-start.5 = (bf16[128,512]{1,0:T(8,128)(2,1)S(1)}, bf16[128,512]{1,0:T(8,128)(2,1)S(1)}, u32[]{:S(2)}, u32[]{:S(2)}) collective-permute-start(bf16[128,512]{1,0:T(8,128)(2,1)S(1)} %get-tuple-element.32), channel_id=1, source_target_pairs={{0,4},{4,0},{8,12},{12,8},{16,20},{20,16},{24,28},{28,24},{1,5},{5... | collective-permute-start | bytes 393224 | tf_op jit(solution)/shard_map/ppermute | solution.py:405
  36.4 0.0 copy-start
  36.4 0.7 %patch_gradients.1 = (bf16[128,512]{1,0:T(8,128)(2,1)S(1)}, bf16[128,512]{1,0:T(8,128)(2,1)S(1)}, bf16[256,512]{1,0:T(8,128)(2,1)S(1)}, bf16[256,512]{1,0:T(8,128)(2,1)S(1)}) custom-call(bf16[144,512]{1,0:T(8,128)(2,1)S(1)} %get-tuple-element.27.q_own, bf16[144,512]{1,0:T(8,128)(2,1)S(1)} %collective-permute-done.q_par, ...), custom_call_target="tpu_custom_call" | custom-call | tf_op jit(solution)/shard_map/patch_gradients/pallas_call | solution.py:305
  37.1 0.9 %collective-permute-start.9 = (bf16[128,512]{1,0:T(8,128)(2,1)S(1)}, bf16[128,512]{1,0:T(8,128)(2,1)S(1)}, u32[]{:S(2)}, u32[]{:S(2)}) collective-permute-start(bf16[128,512]{1,0:T(8,128)(2,1)S(1)} %get-tuple-element.38), channel_id=1, source_target_pairs={{0,4},{4,0},{8,12},{12,8},{16,20},{20,16},{24,28},{28,24},{1,5},{5... | collective-permute-start | bytes 393224 | tf_op jit(solution)/shard_map/ppermute | solution.py:405
  38.0 0.0 collective-permute-done.10.far_a
  38.0 2.3 %collective-permute-done.11.far_b = bf16[256,512]{1,0:T(8,128)(2,1)S(1)} collective-permute-done((bf16[256,512]{1,0:T(8,128)(2,1)S(1)}, bf16[256,512]{1,0:T(8,128)(2,1)S(1)}, u32[]{:S(2)}, u32[]{:S(2)}) %collective-permute-start.11) | collective-permute-done | bytes 262176 | tf_op jit(solution)/shard_map/ppermute | solution.py:405
  40.3 0.1 add_returned.1
  40.4 1.1 %collective-permute-start.12 = (bf16[256,512]{1,0:T(8,128)(2,1)S(1)}, bf16[256,512]{1,0:T(8,128)(2,1)S(1)}, u32[]{:S(2)}, u32[]{:S(2)}) collective-permute-start(bf16[256,512]{1,0:T(8,128)(2,1)S(1)} %add_returned.1), channel_id=1, source_target_pairs={{0,4},{4,0},{8,12},{12,8},{16,20},{20,16},{24,28},{28,24},{1,5},{5... | collective-permute-start | bytes 786440 | tf_op jit(solution)/shard_map/ppermute | solution.py:405
  41.6 0.5 collective-permute-done.14
  42.1 1.7 %collective-permute-start.15 = (bf16[32,1024]{1,0:T(8,128)(2,1)S(1)}, bf16[32,1024]{1,0:T(8,128)(2,1)S(1)}, u32[]{:S(2)}, u32[]{:S(2)}) collective-permute-start(bf16[32,1024]{1,0:T(8,128)(2,1)S(1)} %slice.36), channel_id=1, source_target_pairs={{0,16},{4,20},{8,24},{12,28},{16,0},{20,4},{24,8},{28,12},{1,17},{... | collective-permute-start | bytes 196616 | tf_op jit(solution)/shard_map/ppermute | solution.py:441
  43.8 0.0 collective-permute-done.5.att_back
  43.8 0.7 %collective-permute-done.9.dq_back = bf16[128,512]{1,0:T(8,128)(2,1)S(1)} collective-permute-done((bf16[128,512]{1,0:T(8,128)(2,1)S(1)}, bf16[128,512]{1,0:T(8,128)(2,1)S(1)}, u32[]{:S(2)}, u32[]{:S(2)}) %collective-permute-start.9) | collective-permute-done | bytes 131104 | tf_op jit(solution)/shard_map/ppermute | solution.py:405
  44.4 0.0 copy-done
  44.5 1.2 %finish_queries.1 = (bf16[128,1024]{1,0:T(8,128)(2,1)}, bf16[128,1024]{1,0:T(8,128)(2,1)}) custom-call(bf16[128,512]{1,0:T(8,128)(2,1)S(1)} %get-tuple-element.31.att_own, bf16[128,512]{1,0:T(8,128)(2,1)S(1)} %collective-permute-done.5.att_back, bf16[128,512]{1,0:T(8,128)(2,1)S(1)} %get-tuple-element.37.dq_own, ...), custom_call_target="tpu_custom_call" | custom-call | tf_op jit(solution)/shard_map/finish_queries/pallas_call | solution.py:346
  45.7 1.7 %collective-permute-done.15.out = bf16[32,1024]{1,0:T(8,128)(2,1)S(1)} collective-permute-done((bf16[32,1024]{1,0:T(8,128)(2,1)S(1)}, bf16[32,1024]{1,0:T(8,128)(2,1)S(1)}, u32[]{:S(2)}, u32[]{:S(2)}) %collective-permute-start.15) | collective-permute-done | bytes 65568 | tf_op jit(solution)/shard_map/ppermute | solution.py:441
  47.3 1.1 %collective-permute-done.12.home = bf16[256,512]{1,0:T(8,128)(2,1)S(1)} collective-permute-done((bf16[256,512]{1,0:T(8,128)(2,1)S(1)}, bf16[256,512]{1,0:T(8,128)(2,1)S(1)}, u32[]{:S(2)}, u32[]{:S(2)}) %collective-permute-start.12) | collective-permute-done | bytes 262176 | tf_op jit(solution)/shard_map/ppermute | solution.py:405
  48.4 0.9 %finish_keys.1 = (bf16[128,1024]{1,0:T(8,128)(2,1)}, bf16[128,1024]{1,0:T(8,128)(2,1)}, f32[32,1024]{1,0:T(8,128)}) custom-call(bf16[256,512]{1,0:T(8,128)(2,1)S(1)} %get-tuple-element.41.own, bf16[256,512]{1,0:T(8,128)(2,1)S(1)} %collective-permute-done.10.far_a, bf16[256,512]{1,0:T(8,128)(2,1)S(1)} %collective-permute-done.11.far_b, ...), custom_call_target="tpu_custom_call" | custom-call | tf_op jit(solution)/shard_map/finish_keys/pallas_call | solution.py:383
  (5 shorter events, 0.1 us)
Async XLA Ops:
  2.0 10.2 %collective-permute-start.1 = (bf16[256,512]{1,0:T(8,128)(2,1)S(1)}, bf16[256,512]{1,0:T(8,128)(2,1)S(1)}, u32[]{:S(2)}, u32[]{:S(2)}) collective-permute-start(bf16[256,512]{1,0:T(8,128)(2,1)S(1)} %get-tuple-element.30), channel_id=1, source_target_pairs={{0,4},{4,0},{8,12},{12,8},{16,20},{20,16},{24,28},{28,24},{1,5},{5... | collective-permute-start | bytes 786440 | tf_op jit(solution)/shard_map/ppermute | solution.py:405
  5.0 12.4 %collective-permute-start.4 = (bf16[128,1024]{1,0:T(8,128)(2,1)}, bf16[128,1024]{1,0:T(8,128)(2,1)S(1)}, u32[]{:S(2)}, u32[]{:S(2)}) collective-permute-start(bf16[128,1024]{1,0:T(8,128)(2,1)} %bitcast.13), channel_id=1, source_target_pairs={{0,4},{4,0},{8,12},{12,8},{16,20},{20,16},{24,28},{28,24},{1,5},{5... | collective-permute-start | bytes 786440 | tf_op jit(solution)/shard_map/ppermute | solution.py:405
  5.1 16.3 %collective-permute-start.3 = (bf16[256,512]{1,0:T(8,128)(2,1)S(1)}, bf16[256,512]{1,0:T(8,128)(2,1)S(1)}, u32[]{:S(2)}, u32[]{:S(2)}) collective-permute-start(bf16[256,512]{1,0:T(8,128)(2,1)S(1)} %get-tuple-element.29.own), channel_id=1, source_target_pairs={{8,0},{16,8},{24,16},{4,12},{12,20},{20,28},{9,1},{17,9},{25,17},{... | collective-permute-start | bytes 786440 | tf_op jit(solution)/shard_map/ppermute | solution.py:405
  12.1 9.3 %collective-permute-start.2 = (bf16[256,512]{1,0:T(8,128)(2,1)S(1)}, bf16[256,512]{1,0:T(8,128)(2,1)S(1)}, u32[]{:S(2)}, u32[]{:S(2)}) collective-permute-start(bf16[256,512]{1,0:T(8,128)(2,1)S(1)} %collective-permute-done.1.par), channel_id=1, source_target_pairs={{0,8},{8,16},{16,24},{12,4},{20,12},{28,20},{1,9},{9,17},{17,25},{... | collective-permute-start | bytes 786440 | tf_op jit(solution)/shard_map/ppermute | solution.py:405
  16.2 8.3 %copy-start.1 = (bf16[1,128,1024]{2,1,0:T(8,128)(2,1)S(1)}, bf16[1,128,1024]{2,1,0:T(8,128)(2,1)}, u32[]{:S(2)}) copy-start(bf16[1,128,1024]{2,1,0:T(8,128)(2,1)} %param.11) | copy-start | bytes 786436
  16.2 5.2 %collective-permute-start = (bf16[144,512]{1,0:T(8,128)(2,1)S(1)}, bf16[144,512]{1,0:T(8,128)(2,1)S(1)}, u32[]{:S(2)}, u32[]{:S(2)}) collective-permute-start(bf16[144,512]{1,0:T(8,128)(2,1)S(1)} %get-tuple-element.28), channel_id=1, source_target_pairs={{0,4},{4,0},{8,12},{12,8},{16,20},{20,16},{24,28},{28,24},{1,5},{5... | collective-permute-start | bytes 442376 | tf_op jit(solution)/shard_map/ppermute | solution.py:405
  16.3 6.8 %collective-permute-start.7 = (bf16[128,1024]{1,0:T(8,128)(2,1)}, bf16[128,1024]{1,0:T(8,128)(2,1)S(1)}, u32[]{:S(2)}, u32[]{:S(2)}) collective-permute-start(bf16[128,1024]{1,0:T(8,128)(2,1)} %bitcast.14), channel_id=1, source_target_pairs={{0,1},{1,0},{2,3},{3,2},{4,5},{5,4},{6,7},{7,6},{8,9},{9,8},{10,11... | collective-permute-start | bytes 786440 | tf_op jit(solution)/shard_map/ppermute | solution.py:406
  17.4 5.7 %collective-permute-start.8 = (bf16[128,1024]{1,0:T(8,128)(2,1)S(1)}, bf16[128,1024]{1,0:T(8,128)(2,1)S(1)}, u32[]{:S(2)}, u32[]{:S(2)}) collective-permute-start(bf16[128,1024]{1,0:T(8,128)(2,1)S(1)} %collective-permute-done.4.cot_par.par), channel_id=1, source_target_pairs={{0,1},{1,0},{2,3},{3,2},{4,5},{5,4},{6,7},{7,6},{8,9},{9,8},{10,11... | collective-permute-start | bytes 786440 | tf_op jit(solution)/shard_map/ppermute | solution.py:406
  23.0 1.4 %collective-permute-start.6 = (bf16[256,256]{1,0:T(8,128)(2,1)S(1)}, bf16[256,256]{1,0:T(8,128)(2,1)S(1)}, u32[]{:S(2)}, u32[]{:S(2)}) collective-permute-start(bf16[256,256]{1,0:T(8,128)(2,1)S(1)} %get-tuple-element.49), channel_id=1, source_target_pairs={{0,1},{1,0},{2,3},{3,2},{4,5},{5,4},{6,7},{7,6},{8,9},{9,8},{10,11... | collective-permute-start | bytes 393224 | tf_op jit(solution)/shard_map/ppermute | solution.py:406
  25.1 8.4 %collective-permute-start.13 = (bf16[128,1024]{1,0:T(8,128)(2,1)S(1)}, bf16[128,1024]{1,0:T(8,128)(2,1)S(1)}, u32[]{:S(2)}, u32[]{:S(2)}) collective-permute-start(bf16[128,1024]{1,0:T(8,128)(2,1)S(1)} %get-tuple-element.45), channel_id=1, source_target_pairs={{0,2},{1,3},{2,0},{3,1},{4,6},{5,7},{6,4},{7,5},{8,10},{9,11},{10,... | collective-permute-start | bytes 786440 | tf_op jit(solution)/shard_map/ppermute | solution.py:441
  28.0 10.0 %collective-permute-start.10 = (bf16[256,512]{1,0:T(8,128)(2,1)S(1)}, bf16[256,512]{1,0:T(8,128)(2,1)S(1)}, u32[]{:S(2)}, u32[]{:S(2)}) collective-permute-start(bf16[256,512]{1,0:T(8,128)(2,1)S(1)} %get-tuple-element.42), channel_id=1, source_target_pairs={{8,16},{12,20},{16,8},{20,12},{9,17},{13,21},{17,9},{21,13},{10,18... | collective-permute-start | bytes 786440 | tf_op jit(solution)/shard_map/ppermute | solution.py:405
  28.7 11.6 %collective-permute-start.11 = (bf16[256,512]{1,0:T(8,128)(2,1)S(1)}, bf16[256,512]{1,0:T(8,128)(2,1)S(1)}, u32[]{:S(2)}, u32[]{:S(2)}) collective-permute-start(bf16[256,512]{1,0:T(8,128)(2,1)S(1)} %get-tuple-element.43), channel_id=1, source_target_pairs={{0,8},{4,12},{8,0},{12,4},{16,24},{20,28},{24,16},{28,20},{1,9},{5... | collective-permute-start | bytes 786440 | tf_op jit(solution)/shard_map/ppermute | solution.py:405
  33.6 8.4 %collective-permute-start.14 = (bf16[64,1024]{1,0:T(8,128)(2,1)S(1)}, bf16[64,1024]{1,0:T(8,128)(2,1)S(1)}, u32[]{:S(2)}, u32[]{:S(2)}) collective-permute-start(bf16[64,1024]{1,0:T(8,128)(2,1)S(1)} %slice.35), channel_id=1, source_target_pairs={{0,8},{4,12},{8,0},{12,4},{16,24},{20,28},{24,16},{28,20},{1,9},{5... | collective-permute-start | bytes 393224 | tf_op jit(solution)/shard_map/ppermute | solution.py:441
  35.3 8.5 %collective-permute-start.5 = (bf16[128,512]{1,0:T(8,128)(2,1)S(1)}, bf16[128,512]{1,0:T(8,128)(2,1)S(1)}, u32[]{:S(2)}, u32[]{:S(2)}) collective-permute-start(bf16[128,512]{1,0:T(8,128)(2,1)S(1)} %get-tuple-element.32), channel_id=1, source_target_pairs={{0,4},{4,0},{8,12},{12,8},{16,20},{20,16},{24,28},{28,24},{1,5},{5... | collective-permute-start | bytes 393224 | tf_op jit(solution)/shard_map/ppermute | solution.py:405
  36.4 8.0 %copy-start = (bf16[1024,1024]{1,0:T(8,128)(2,1)S(1)}, bf16[1024,1024]{1,0:T(8,128)(2,1)}, u32[]{:S(2)}) copy-start(bf16[1024,1024]{1,0:T(8,128)(2,1)} %w.3) | copy-start | bytes 6291460
  37.1 7.4 %collective-permute-start.9 = (bf16[128,512]{1,0:T(8,128)(2,1)S(1)}, bf16[128,512]{1,0:T(8,128)(2,1)S(1)}, u32[]{:S(2)}, u32[]{:S(2)}) collective-permute-start(bf16[128,512]{1,0:T(8,128)(2,1)S(1)} %get-tuple-element.38), channel_id=1, source_target_pairs={{0,4},{4,0},{8,12},{12,8},{16,20},{20,16},{24,28},{28,24},{1,5},{5... | collective-permute-start | bytes 393224 | tf_op jit(solution)/shard_map/ppermute | solution.py:405
  40.4 8.0 %collective-permute-start.12 = (bf16[256,512]{1,0:T(8,128)(2,1)S(1)}, bf16[256,512]{1,0:T(8,128)(2,1)S(1)}, u32[]{:S(2)}, u32[]{:S(2)}) collective-permute-start(bf16[256,512]{1,0:T(8,128)(2,1)S(1)} %add_returned.1), channel_id=1, source_target_pairs={{0,4},{4,0},{8,12},{12,8},{16,20},{20,16},{24,28},{28,24},{1,5},{5... | collective-permute-start | bytes 786440 | tf_op jit(solution)/shard_map/ppermute | solution.py:405
  42.1 5.2 %collective-permute-start.15 = (bf16[32,1024]{1,0:T(8,128)(2,1)S(1)}, bf16[32,1024]{1,0:T(8,128)(2,1)S(1)}, u32[]{:S(2)}, u32[]{:S(2)}) collective-permute-start(bf16[32,1024]{1,0:T(8,128)(2,1)S(1)} %slice.36), channel_id=1, source_target_pairs={{0,16},{4,20},{8,24},{12,28},{16,0},{20,4},{24,8},{28,12},{1,17},{... | collective-permute-start | bytes 196616 | tf_op jit(solution)/shard_map/ppermute | solution.py:441
where the time goes:
time: 49.6 us; the launch traced here: 49.4 us
  starting transfers between devices  21.8 us (44%)
  waiting for transfers between devices  16.4 us (33%)
  Pallas kernels  10.2 us (21%)
  between operations  0.8 us (2%)
    ppermute x10, starting transfers between devices, on_device(): send = lambda x, pairs: lax.ppermute(x, 'seq', pairs)  16.8 us
    ppermute x10, waiting for transfers between devices, on_device(): send = lambda x, pairs: lax.ppermute(x, 'seq', pairs)  12.6 us
    ppermute x3, starting transfers between devices, on_device(): out = lax.ppermute(out, axis, [(i, i ^ bit) for i in range(count)])  4.86 us
    ppermute x3, waiting for transfers between devices, on_device(): out = lax.ppermute(out, axis, [(i, i ^ bit) for i in range(count)])  2.52 us
    pallas_call x1, Pallas kernels, grad_attended(): call(turn_kernel, (shape_of(2 * tokens, pairs * HD),), [HBM, VMEM, HBM],...  2.32 us
    pallas_call x1, Pallas kernels, forward(): call(functools.partial(forward_kernel, direct, n_dp), (shape_of(pairs, 3...  1.59 us
    pallas_call x1, Pallas kernels, backward(): call(backward_kernel, (shape_of(*probs.shape),) + (shape_of(2 * tokens, h...  1.34 us
    pallas_call x1, Pallas kernels, pack(): call(pack_kernel, (kv, kv) + (shape_of(tokens + FLAG_ROWS, half),) * 2, [...  1.34 us
  transfers between devices with their start and end apart: 16, of which 10 were waited for; matrix products, arithmetic and copies ran while one was open for 0% of the time, Pallas kernels for 15%

commit v1 on v0

--- a/solution.py
+++ b/solution.py
@@ -229,7 +229,7 @@
 
 
 def backward_kernel(
-    q_own, q_par, own, par, far_own, far_par, ga, probs, _after, grads, edge_a, edge_b
+    q_own, q_par, own, par, far_own, far_par, ga, probs, grads, edge_a, edge_b
 ):
     scale = 1.0 / math.sqrt(HD)
     tokens, half = q_own.shape[0] - FLAG_ROWS, q_own.shape[1]
@@ -264,14 +264,14 @@
         edge_b[:, cols] = jnp.where(slot == 0, par_far, own_far)
 
 
-def backward(inputs, ga, probs, after):
+def backward(inputs, ga, probs):
     tokens, half = inputs[0].shape[0] - FLAG_ROWS, inputs[0].shape[1]
     return call(
         backward_kernel,
         (shape_of(*probs.shape),) + (shape_of(2 * tokens, half),) * 2,
-        [VMEM] * 8 + [ANY],
+        [VMEM] * 8,
         "patch_backward",
-    )(*inputs, ga, probs, after)
+    )(*inputs, ga, probs)
 
 
 def gradient_kernel(
@@ -307,27 +307,25 @@
     )(*inputs, ga, probs, grads)
 
 
-def weight_kernel(att_keep, att_core, own, par, core_own, core_par, keep, send):
-    size = keep.shape[0]
+def weight_kernel(kept, att_keep, att_core, own, par, core_own, core_par, _after, target):
+    size = target.shape[0]
     tokens = own.shape[0]
-    for target, start in ((send, size), (keep, 0)):
-        rows = slice(start, start + size)
-        total = dot(att_keep[rows, :tokens], own[...], 1, 0)
-        total += dot(att_keep[rows, tokens:], par[...], 1, 0)
-        total += dot(att_core[rows, :tokens], core_own[...], 1, 0)
-        total += dot(att_core[rows, tokens:], core_par[...], 1, 0)
-        target[...] = total.astype(target.dtype)
-
-
-def weight_terms(*operands):
-    rows = operands[0].shape[0]
-    tokens, width = operands[2].shape
-    return call(
-        weight_kernel,
-        (shape_of(rows // 2, width, dtype=F32), shape_of(rows // 2, width)),
-        [VMEM] * 6,
-        "weight_terms",
-    )(*operands)
+    rows = slice(0, size) if kept else slice(size, 2 * size)
+    total = dot(att_keep[rows, :tokens], own[...], 1, 0)
+    total += dot(att_keep[rows, tokens:], par[...], 1, 0)
+    total += dot(att_core[rows, :tokens], core_own[...], 1, 0)
+    total += dot(att_core[rows, tokens:], core_par[...], 1, 0)
+    target[...] = total.astype(target.dtype)
+
+
+def weight_terms(kept, operands, after):
+    rows, width = operands[0].shape[0] // 2, operands[2].shape[1]
+    return call(
+        functools.partial(weight_kernel, kept),
+        (shape_of(rows, width, dtype=F32 if kept else BF16),),
+        [VMEM] * 6 + [ANY],
+        "weight_terms_kept" if kept else "weight_terms_sent",
+    )(*operands, after)[0]
 
 
 def query_kernel(att_own, att_back, dq_own, dq_back, w, out, dq, att):
@@ -422,8 +420,10 @@
     )
     att_core = across(att_t[1], 1)
     att_back = send(att_back, swap)
-    keep, out = weight_terms(att_t[0], att_core, cot, cot_par, core_own, core_par)
-    grads, *leaving = backward(inputs, ga, probs, keep)
+    grads, *leaving = backward(inputs, ga, probs)
+    operands = (att_t[0], att_core, cot, cot_par, core_own, core_par)
+    out = weight_terms(False, operands, leaving[0])
+    keep = weight_terms(True, operands, out)
     far = [send(leaving[i], edges[i]) for i in range(2)]
     dq_own, dq_back, d_own, d_par = gradients(inputs, ga, probs, grads)
     dq_back = send(dq_back, swap)

time: 49.6 us -> 49.9 us (level)
    ppermute x10, waiting for transfers between devices: 12.6 us -> 14 us  [on_device(): send = lambda x, pairs: lax.ppermute(x, 'seq', pairs)]
    ppermute x3, waiting for transfers between devices: 1.32 us -> 0.01 us  [on_device(): lax.ppermute(x, 'dp', [(i, i ^ k) for i in range(n_dp)])]
  transfers between devices with their start and end apart: 16 -> 16, of which waited for: 10 -> 8; matrix products, arithmetic and copies ran while one was open for 0% -> 0% of each run, Pallas kernels for 15% -> 15%
where the time goes in v1:
time: 49.9 us; the launch traced here: 49.6 us
  starting transfers between devices  22.1 us (44%)
  waiting for transfers between devices  16.2 us (32%)
  Pallas kernels  10.3 us (21%)
  between operations  0.82 us (2%)
    ppermute x10, starting transfers between devices, on_device(): send = lambda x, pairs: lax.ppermute(x, 'seq', pairs)  17.1 us
    ppermute x10, waiting for transfers between devices, on_device(): send = lambda x, pairs: lax.ppermute(x, 'seq', pairs)  14 us
    ppermute x3, starting transfers between devices, on_device(): out = lax.ppermute(out, axis, [(i, i ^ bit) for i in range(count)])  4.89 us
    pallas_call x1, Pallas kernels, grad_attended(): call(turn_kernel, (shape_of(2 * tokens, pairs * HD),), [HBM, VMEM, HBM],...  2.32 us
    ppermute x3, waiting for transfers between devices, on_device(): out = lax.ppermute(out, axis, [(i, i ^ bit) for i in range(count)])  2.26 us
    pallas_call x1, Pallas kernels, forward(): call(functools.partial(forward_kernel, direct, n_dp), (shape_of(pairs, 3...  1.59 us
    pallas_call x1, Pallas kernels, backward(): call(backward_kernel, (shape_of(*probs.shape),) + (shape_of(2 * tokens, h...  1.35 us
    pallas_call x1, Pallas kernels, pack(): call(pack_kernel, (kv, kv) + (shape_of(tokens + FLAG_ROWS, half),) * 2, [...  1.34 us
  transfers between devices with their start and end apart: 16, of which 8 were waited for; matrix products, arithmetic and copies ran while one was open for 0% of the time, Pallas kernels for 15%

profile of v1, /device:TPU:0, one launch (start us, length us, event | category | flops | bytes accessed | tf_op | source)
XLA Modules:
  0.0 49.6 jit_solution(412469415964209023)
XLA Ops:
  0.6 1.3 %pack_heads.1 = (bf16[256,512]{1,0:T(8,128)(2,1)S(1)}, bf16[256,512]{1,0:T(8,128)(2,1)S(1)}, bf16[144,512]{1,0:T(8,128)(2,1)S(1)}, bf16[144,512]{1,0:T(8,128)(2,1)S(1)}) custom-call(s32[1,2]{1,0:T(1,128)} %bitcast.21, bf16[128,1024]{1,0:T(8,128)(2,1)} %bitcast.18, bf16[128,1024]{1,0:T(8,128)(2,1)} %bitcast.19, bf16[128,1024]{1,0:T(8,128)(2,1)} %bitcast.20), custom_call_target="tpu_custom_call" | custom-call | tf_op jit(solution)/shard_map/pack_heads/pallas_call | solution.py:97
  2.0 3.0 %collective-permute-start.1 = (bf16[256,512]{1,0:T(8,128)(2,1)S(1)}, bf16[256,512]{1,0:T(8,128)(2,1)S(1)}, u32[]{:S(2)}, u32[]{:S(2)}) collective-permute-start(bf16[256,512]{1,0:T(8,128)(2,1)S(1)} %get-tuple-element.28), channel_id=1, source_target_pairs={{0,4},{4,0},{8,12},{12,8},{16,20},{20,16},{24,28},{28,24},{1,5},{5... | collective-permute-start | bytes 786440 | tf_op jit(solution)/shard_map/ppermute | solution.py:403
  5.0 0.1 collective-permute-start.4
  5.1 1.3 %collective-permute-start.3 = (bf16[256,512]{1,0:T(8,128)(2,1)S(1)}, bf16[256,512]{1,0:T(8,128)(2,1)S(1)}, u32[]{:S(2)}, u32[]{:S(2)}) collective-permute-start(bf16[256,512]{1,0:T(8,128)(2,1)S(1)} %get-tuple-element.27.own), channel_id=1, source_target_pairs={{8,0},{16,8},{24,16},{4,12},{12,20},{20,28},{9,1},{17,9},{25,17},{... | collective-permute-start | bytes 786440 | tf_op jit(solution)/shard_map/ppermute | solution.py:403
  6.4 5.8 %collective-permute-done.1.par = bf16[256,512]{1,0:T(8,128)(2,1)S(1)} collective-permute-done((bf16[256,512]{1,0:T(8,128)(2,1)S(1)}, bf16[256,512]{1,0:T(8,128)(2,1)S(1)}, u32[]{:S(2)}, u32[]{:S(2)}) %collective-permute-start.1) | collective-permute-done | bytes 262176 | tf_op jit(solution)/shard_map/ppermute | solution.py:403
  12.1 4.0 %collective-permute-start.2 = (bf16[256,512]{1,0:T(8,128)(2,1)S(1)}, bf16[256,512]{1,0:T(8,128)(2,1)S(1)}, u32[]{:S(2)}, u32[]{:S(2)}) collective-permute-start(bf16[256,512]{1,0:T(8,128)(2,1)S(1)} %collective-permute-done.1.par), channel_id=1, source_target_pairs={{0,8},{8,16},{16,24},{12,4},{20,12},{28,20},{1,9},{9,17},{17,25},{... | collective-permute-start | bytes 786440 | tf_op jit(solution)/shard_map/ppermute | solution.py:403
  16.2 0.1 collective-permute-start
  16.3 0.1 collective-permute-start.11
  16.3 1.1 %collective-permute-done.4.cot_par.par = bf16[128,1024]{1,0:T(8,128)(2,1)S(1)} collective-permute-done((bf16[128,1024]{1,0:T(8,128)(2,1)}, bf16[128,1024]{1,0:T(8,128)(2,1)S(1)}, u32[]{:S(2)}, u32[]{:S(2)}) %collective-permute-start.4) | collective-permute-done | bytes 262176 | tf_op jit(solution)/shard_map/ppermute | solution.py:403
  17.4 0.0 collective-permute-start.12
  17.4 2.3 %grad_attended.1.after.ga = bf16[256,512]{1,0:T(8,128)(2,1)S(1)} custom-call(bf16[128,1024]{1,0:T(8,128)(2,1)} %bitcast.15, bf16[128,1024]{1,0:T(8,128)(2,1)S(1)} %collective-permute-done.4.cot_par.par, bf16[1024,1024]{1,0:T(8,128)(2,1)} %w.3), custom_call_target="tpu_custom_call" | custom-call | tf_op jit(solution)/shard_map/grad_attended/pallas_call | solution.py:129
  19.8 1.6 %collective-permute-done.q_par = bf16[144,512]{1,0:T(8,128)(2,1)S(1)} collective-permute-done((bf16[144,512]{1,0:T(8,128)(2,1)S(1)}, bf16[144,512]{1,0:T(8,128)(2,1)S(1)}, u32[]{:S(2)}, u32[]{:S(2)}) %collective-permute-start) | collective-permute-done | bytes 147488 | tf_op jit(solution)/shard_map/ppermute | solution.py:403
  21.4 0.0 collective-permute-done.3.far_par
  21.4 0.0 collective-permute-done.2.far_own
  21.4 0.0 copy-start.1
  21.4 1.6 %patch_forward.1 = (bf16[4,384,256]{2,1,0:T(8,128)(2,1)S(1)}, bf16[128,512]{1,0:T(8,128)(2,1)S(1)}, bf16[128,512]{1,0:T(8,128)(2,1)S(1)}, bf16[2,256,256]{2,1,0:T(8,128)(2,1)S(1)}) custom-call(bf16[144,512]{1,0:T(8,128)(2,1)S(1)} %get-tuple-element.25.q_own, bf16[144,512]{1,0:T(8,128)(2,1)S(1)} %collective-permute-done.q_par, ...), custom_call_target="tpu_custom_call" | custom-call | tf_op jit(solution)/shard_map/patch_forward/pallas_call | solution.py:209
  23.0 0.1 collective-permute-start.10
  23.1 1.3 %patch_backward.1 = (bf16[4,384,256]{2,1,0:T(8,128)(2,1)S(1)}, bf16[256,512]{1,0:T(8,128)(2,1)S(1)}, bf16[256,512]{1,0:T(8,128)(2,1)S(1)}) custom-call(bf16[144,512]{1,0:T(8,128)(2,1)S(1)} %get-tuple-element.25.q_own, bf16[144,512]{1,0:T(8,128)(2,1)S(1)} %collective-permute-done.q_par, bf16[256,512]{1,0:T(8,128)(2,1)S(1)} %get-tuple-element.27.own, ...), custom_call_target="tpu_custom_call" | custom-call | tf_op jit(solution)/shard_map/patch_backward/pallas_call | solution.py:269
  24.5 0.0 collective-permute-done.11.core_own
  24.5 0.0 collective-permute-done.12.core_par
  24.5 0.0 collective-permute-done.10.att_core
  24.5 0.0 copy-done.1
  24.5 0.4 weight_terms_sent.1._after
  24.9 1.6 %collective-permute-start.13 = (bf16[128,1024]{1,0:T(8,128)(2,1)S(1)}, bf16[128,1024]{1,0:T(8,128)(2,1)S(1)}, u32[]{:S(2)}, u32[]{:S(2)}) collective-permute-start(bf16[128,1024]{1,0:T(8,128)(2,1)S(1)} %weight_terms_sent.1._after), channel_id=1, source_target_pairs={{0,2},{1,3},{2,0},{3,1},{4,6},{5,7},{6,4},{7,5},{8,10},{9,11},{10,... | collective-permute-start | bytes 786440 | tf_op jit(solution)/shard_map/ppermute | solution.py:441
  26.5 0.7 %collective-permute-start.7 = (bf16[256,512]{1,0:T(8,128)(2,1)S(1)}, bf16[256,512]{1,0:T(8,128)(2,1)S(1)}, u32[]{:S(2)}, u32[]{:S(2)}) collective-permute-start(bf16[256,512]{1,0:T(8,128)(2,1)S(1)} %get-tuple-element.38._after), channel_id=1, source_target_pairs={{8,16},{12,20},{16,8},{20,12},{9,17},{13,21},{17,9},{21,13},{10,18... | collective-permute-start | bytes 786440 | tf_op jit(solution)/shard_map/ppermute | solution.py:403
  27.2 4.4 %collective-permute-start.8 = (bf16[256,512]{1,0:T(8,128)(2,1)S(1)}, bf16[256,512]{1,0:T(8,128)(2,1)S(1)}, u32[]{:S(2)}, u32[]{:S(2)}) collective-permute-start(bf16[256,512]{1,0:T(8,128)(2,1)S(1)} %get-tuple-element.39), channel_id=1, source_target_pairs={{0,8},{4,12},{8,0},{12,4},{16,24},{20,28},{24,16},{28,20},{1,9},{5... | collective-permute-start | bytes 786440 | tf_op jit(solution)/shard_map/ppermute | solution.py:403
  31.6 0.4 weight_terms_kept.1
  32.0 1.7 %collective-permute-done.13 = bf16[128,1024]{1,0:T(8,128)(2,1)S(1)} collective-permute-done((bf16[128,1024]{1,0:T(8,128)(2,1)S(1)}, bf16[128,1024]{1,0:T(8,128)(2,1)S(1)}, u32[]{:S(2)}, u32[]{:S(2)}) %collective-permute-start.13) | collective-permute-done | bytes 262176 | tf_op jit(solution)/shard_map/ppermute | solution.py:441
  33.7 0.1 convert_add_fusion
  33.8 1.6 %collective-permute-start.14 = (bf16[64,1024]{1,0:T(8,128)(2,1)S(1)}, bf16[64,1024]{1,0:T(8,128)(2,1)S(1)}, u32[]{:S(2)}, u32[]{:S(2)}) collective-permute-start(bf16[64,1024]{1,0:T(8,128)(2,1)S(1)} %slice.35), channel_id=1, source_target_pairs={{0,8},{4,12},{8,0},{12,4},{16,24},{20,28},{24,16},{28,20},{1,9},{5... | collective-permute-start | bytes 393224 | tf_op jit(solution)/shard_map/ppermute | solution.py:441
  35.4 1.1 %collective-permute-start.5 = (bf16[128,512]{1,0:T(8,128)(2,1)S(1)}, bf16[128,512]{1,0:T(8,128)(2,1)S(1)}, u32[]{:S(2)}, u32[]{:S(2)}) collective-permute-start(bf16[128,512]{1,0:T(8,128)(2,1)S(1)} %get-tuple-element.30), channel_id=1, source_target_pairs={{0,4},{4,0},{8,12},{12,8},{16,20},{20,16},{24,28},{28,24},{1,5},{5... | collective-permute-start | bytes 393224 | tf_op jit(solution)/shard_map/ppermute | solution.py:403
  36.5 0.0 copy-start
  36.5 0.7 %patch_gradients.1 = (bf16[128,512]{1,0:T(8,128)(2,1)S(1)}, bf16[128,512]{1,0:T(8,128)(2,1)S(1)}, bf16[256,512]{1,0:T(8,128)(2,1)S(1)}, bf16[256,512]{1,0:T(8,128)(2,1)S(1)}) custom-call(bf16[144,512]{1,0:T(8,128)(2,1)S(1)} %get-tuple-element.25.q_own, bf16[144,512]{1,0:T(8,128)(2,1)S(1)} %collective-permute-done.q_par, ...), custom_call_target="tpu_custom_call" | custom-call | tf_op jit(solution)/shard_map/patch_gradients/pallas_call | solution.py:305
  37.1 1.0 %collective-permute-start.6 = (bf16[128,512]{1,0:T(8,128)(2,1)S(1)}, bf16[128,512]{1,0:T(8,128)(2,1)S(1)}, u32[]{:S(2)}, u32[]{:S(2)}) collective-permute-start(bf16[128,512]{1,0:T(8,128)(2,1)S(1)} %get-tuple-element.34), channel_id=1, source_target_pairs={{0,4},{4,0},{8,12},{12,8},{16,20},{20,16},{24,28},{28,24},{1,5},{5... | collective-permute-start | bytes 393224 | tf_op jit(solution)/shard_map/ppermute | solution.py:403
  38.2 0.0 collective-permute-done.7.far_a
  38.2 0.5 %collective-permute-done.8.far_b = bf16[256,512]{1,0:T(8,128)(2,1)S(1)} collective-permute-done((bf16[256,512]{1,0:T(8,128)(2,1)S(1)}, bf16[256,512]{1,0:T(8,128)(2,1)S(1)}, u32[]{:S(2)}, u32[]{:S(2)}) %collective-permute-start.8) | collective-permute-done | bytes 262176 | tf_op jit(solution)/shard_map/ppermute | solution.py:403
  38.7 0.1 add_returned.1
  38.8 1.4 %collective-permute-start.9 = (bf16[256,512]{1,0:T(8,128)(2,1)S(1)}, bf16[256,512]{1,0:T(8,128)(2,1)S(1)}, u32[]{:S(2)}, u32[]{:S(2)}) collective-permute-start(bf16[256,512]{1,0:T(8,128)(2,1)S(1)} %add_returned.1), channel_id=1, source_target_pairs={{0,4},{4,0},{8,12},{12,8},{16,20},{20,16},{24,28},{28,24},{1,5},{5... | collective-permute-start | bytes 786440 | tf_op jit(solution)/shard_map/ppermute | solution.py:403
  40.2 0.6 %collective-permute-done.14 = bf16[64,1024]{1,0:T(8,128)(2,1)S(1)} collective-permute-done((bf16[64,1024]{1,0:T(8,128)(2,1)S(1)}, bf16[64,1024]{1,0:T(8,128)(2,1)S(1)}, u32[]{:S(2)}, u32[]{:S(2)}) %collective-permute-start.14) | collective-permute-done | bytes 131104 | tf_op jit(solution)/shard_map/ppermute | solution.py:441
  40.9 1.7 %collective-permute-start.15 = (bf16[32,1024]{1,0:T(8,128)(2,1)S(1)}, bf16[32,1024]{1,0:T(8,128)(2,1)S(1)}, u32[]{:S(2)}, u32[]{:S(2)}) collective-permute-start(bf16[32,1024]{1,0:T(8,128)(2,1)S(1)} %slice.36), channel_id=1, source_target_pairs={{0,16},{4,20},{8,24},{12,28},{16,0},{20,4},{24,8},{28,12},{1,17},{... | collective-permute-start | bytes 196616 | tf_op jit(solution)/shard_map/ppermute | solution.py:441
  42.5 0.0 collective-permute-done.5.att_back
  42.6 2.1 %collective-permute-done.6.dq_back = bf16[128,512]{1,0:T(8,128)(2,1)S(1)} collective-permute-done((bf16[128,512]{1,0:T(8,128)(2,1)S(1)}, bf16[128,512]{1,0:T(8,128)(2,1)S(1)}, u32[]{:S(2)}, u32[]{:S(2)}) %collective-permute-start.6) | collective-permute-done | bytes 131104 | tf_op jit(solution)/shard_map/ppermute | solution.py:403
  44.7 0.0 copy-done
  44.7 1.2 %finish_queries.1 = (bf16[128,1024]{1,0:T(8,128)(2,1)}, bf16[128,1024]{1,0:T(8,128)(2,1)}) custom-call(bf16[128,512]{1,0:T(8,128)(2,1)S(1)} %get-tuple-element.29.att_own, bf16[128,512]{1,0:T(8,128)(2,1)S(1)} %collective-permute-done.5.att_back, bf16[128,512]{1,0:T(8,128)(2,1)S(1)} %get-tuple-element.33.dq_own, ...), custom_call_target="tpu_custom_call" | custom-call | tf_op jit(solution)/shard_map/finish_queries/pallas_call | solution.py:344
  45.9 2.8 %collective-permute-done.9.home = bf16[256,512]{1,0:T(8,128)(2,1)S(1)} collective-permute-done((bf16[256,512]{1,0:T(8,128)(2,1)S(1)}, bf16[256,512]{1,0:T(8,128)(2,1)S(1)}, u32[]{:S(2)}, u32[]{:S(2)}) %collective-permute-start.9) | collective-permute-done | bytes 262176 | tf_op jit(solution)/shard_map/ppermute | solution.py:403
  48.7 0.0 collective-permute-done.15.out
  48.7 0.9 %finish_keys.1 = (bf16[128,1024]{1,0:T(8,128)(2,1)}, bf16[128,1024]{1,0:T(8,128)(2,1)}, f32[32,1024]{1,0:T(8,128)}) custom-call(bf16[256,512]{1,0:T(8,128)(2,1)S(1)} %get-tuple-element.37.own, bf16[256,512]{1,0:T(8,128)(2,1)S(1)} %collective-permute-done.7.far_a, bf16[256,512]{1,0:T(8,128)(2,1)S(1)} %collective-permute-done.8.far_b, ...), custom_call_target="tpu_custom_call" | custom-call | tf_op jit(solution)/shard_map/finish_keys/pallas_call | solution.py:381
  (5 shorter events, 0.1 us)
Async XLA Ops:
  2.0 10.2 %collective-permute-start.1 = (bf16[256,512]{1,0:T(8,128)(2,1)S(1)}, bf16[256,512]{1,0:T(8,128)(2,1)S(1)}, u32[]{:S(2)}, u32[]{:S(2)}) collective-permute-start(bf16[256,512]{1,0:T(8,128)(2,1)S(1)} %get-tuple-element.28), channel_id=1, source_target_pairs={{0,4},{4,0},{8,12},{12,8},{16,20},{20,16},{24,28},{28,24},{1,5},{5... | collective-permute-start | bytes 786440 | tf_op jit(solution)/shard_map/ppermute | solution.py:403
  5.0 12.4 %collective-permute-start.4 = (bf16[128,1024]{1,0:T(8,128)(2,1)}, bf16[128,1024]{1,0:T(8,128)(2,1)S(1)}, u32[]{:S(2)}, u32[]{:S(2)}) collective-permute-start(bf16[128,1024]{1,0:T(8,128)(2,1)} %bitcast.13), channel_id=1, source_target_pairs={{0,4},{4,0},{8,12},{12,8},{16,20},{20,16},{24,28},{28,24},{1,5},{5... | collective-permute-start | bytes 786440 | tf_op jit(solution)/shard_map/ppermute | solution.py:403
  5.1 16.3 %collective-permute-start.3 = (bf16[256,512]{1,0:T(8,128)(2,1)S(1)}, bf16[256,512]{1,0:T(8,128)(2,1)S(1)}, u32[]{:S(2)}, u32[]{:S(2)}) collective-permute-start(bf16[256,512]{1,0:T(8,128)(2,1)S(1)} %get-tuple-element.27.own), channel_id=1, source_target_pairs={{8,0},{16,8},{24,16},{4,12},{12,20},{20,28},{9,1},{17,9},{25,17},{... | collective-permute-start | bytes 786440 | tf_op jit(solution)/shard_map/ppermute | solution.py:403
  12.1 9.2 %collective-permute-start.2 = (bf16[256,512]{1,0:T(8,128)(2,1)S(1)}, bf16[256,512]{1,0:T(8,128)(2,1)S(1)}, u32[]{:S(2)}, u32[]{:S(2)}) collective-permute-start(bf16[256,512]{1,0:T(8,128)(2,1)S(1)} %collective-permute-done.1.par), channel_id=1, source_target_pairs={{0,8},{8,16},{16,24},{12,4},{20,12},{28,20},{1,9},{9,17},{17,25},{... | collective-permute-start | bytes 786440 | tf_op jit(solution)/shard_map/ppermute | solution.py:403
  16.2 5.2 %collective-permute-start = (bf16[144,512]{1,0:T(8,128)(2,1)S(1)}, bf16[144,512]{1,0:T(8,128)(2,1)S(1)}, u32[]{:S(2)}, u32[]{:S(2)}) collective-permute-start(bf16[144,512]{1,0:T(8,128)(2,1)S(1)} %get-tuple-element.26), channel_id=1, source_target_pairs={{0,4},{4,0},{8,12},{12,8},{16,20},{20,16},{24,28},{28,24},{1,5},{5... | collective-permute-start | bytes 442376 | tf_op jit(solution)/shard_map/ppermute | solution.py:403
  16.3 8.2 %collective-permute-start.11 = (bf16[128,1024]{1,0:T(8,128)(2,1)}, bf16[128,1024]{1,0:T(8,128)(2,1)S(1)}, u32[]{:S(2)}, u32[]{:S(2)}) collective-permute-start(bf16[128,1024]{1,0:T(8,128)(2,1)} %bitcast.14), channel_id=1, source_target_pairs={{0,1},{1,0},{2,3},{3,2},{4,5},{5,4},{6,7},{7,6},{8,9},{9,8},{10,11... | collective-permute-start | bytes 786440 | tf_op jit(solution)/shard_map/ppermute | solution.py:404
  17.4 7.0 %collective-permute-start.12 = (bf16[128,1024]{1,0:T(8,128)(2,1)S(1)}, bf16[128,1024]{1,0:T(8,128)(2,1)S(1)}, u32[]{:S(2)}, u32[]{:S(2)}) collective-permute-start(bf16[128,1024]{1,0:T(8,128)(2,1)S(1)} %collective-permute-done.4.cot_par.par), channel_id=1, source_target_pairs={{0,1},{1,0},{2,3},{3,2},{4,5},{5,4},{6,7},{7,6},{8,9},{9,8},{10,11... | collective-permute-start | bytes 786440 | tf_op jit(solution)/shard_map/ppermute | solution.py:404
  21.4 3.1 %copy-start.1 = (bf16[1,128,1024]{2,1,0:T(8,128)(2,1)S(1)}, bf16[1,128,1024]{2,1,0:T(8,128)(2,1)}, u32[]{:S(2)}) copy-start(bf16[1,128,1024]{2,1,0:T(8,128)(2,1)} %param.11) | copy-start | bytes 786436
  23.0 1.5 %collective-permute-start.10 = (bf16[256,256]{1,0:T(8,128)(2,1)S(1)}, bf16[256,256]{1,0:T(8,128)(2,1)S(1)}, u32[]{:S(2)}, u32[]{:S(2)}) collective-permute-start(bf16[256,256]{1,0:T(8,128)(2,1)S(1)} %get-tuple-element.45), channel_id=1, source_target_pairs={{0,1},{1,0},{2,3},{3,2},{4,5},{5,4},{6,7},{7,6},{8,9},{9,8},{10,11... | collective-permute-start | bytes 393224 | tf_op jit(solution)/shard_map/ppermute | solution.py:404
  24.9 8.8 %collective-permute-start.13 = (bf16[128,1024]{1,0:T(8,128)(2,1)S(1)}, bf16[128,1024]{1,0:T(8,128)(2,1)S(1)}, u32[]{:S(2)}, u32[]{:S(2)}) collective-permute-start(bf16[128,1024]{1,0:T(8,128)(2,1)S(1)} %weight_terms_sent.1._after), channel_id=1, source_target_pairs={{0,2},{1,3},{2,0},{3,1},{4,6},{5,7},{6,4},{7,5},{8,10},{9,11},{10,... | collective-permute-start | bytes 786440 | tf_op jit(solution)/shard_map/ppermute | solution.py:441
  26.5 11.7 %collective-permute-start.7 = (bf16[256,512]{1,0:T(8,128)(2,1)S(1)}, bf16[256,512]{1,0:T(8,128)(2,1)S(1)}, u32[]{:S(2)}, u32[]{:S(2)}) collective-permute-start(bf16[256,512]{1,0:T(8,128)(2,1)S(1)} %get-tuple-element.38._after), channel_id=1, source_target_pairs={{8,16},{12,20},{16,8},{20,12},{9,17},{13,21},{17,9},{21,13},{10,18... | collective-permute-start | bytes 786440 | tf_op jit(solution)/shard_map/ppermute | solution.py:403
  27.2 11.6 %collective-permute-start.8 = (bf16[256,512]{1,0:T(8,128)(2,1)S(1)}, bf16[256,512]{1,0:T(8,128)(2,1)S(1)}, u32[]{:S(2)}, u32[]{:S(2)}) collective-permute-start(bf16[256,512]{1,0:T(8,128)(2,1)S(1)} %get-tuple-element.39), channel_id=1, source_target_pairs={{0,8},{4,12},{8,0},{12,4},{16,24},{20,28},{24,16},{28,20},{1,9},{5... | collective-permute-start | bytes 786440 | tf_op jit(solution)/shard_map/ppermute | solution.py:403
  33.8 7.0 %collective-permute-start.14 = (bf16[64,1024]{1,0:T(8,128)(2,1)S(1)}, bf16[64,1024]{1,0:T(8,128)(2,1)S(1)}, u32[]{:S(2)}, u32[]{:S(2)}) collective-permute-start(bf16[64,1024]{1,0:T(8,128)(2,1)S(1)} %slice.35), channel_id=1, source_target_pairs={{0,8},{4,12},{8,0},{12,4},{16,24},{20,28},{24,16},{28,20},{1,9},{5... | collective-permute-start | bytes 393224 | tf_op jit(solution)/shard_map/ppermute | solution.py:441
  35.4 7.1 %collective-permute-start.5 = (bf16[128,512]{1,0:T(8,128)(2,1)S(1)}, bf16[128,512]{1,0:T(8,128)(2,1)S(1)}, u32[]{:S(2)}, u32[]{:S(2)}) collective-permute-start(bf16[128,512]{1,0:T(8,128)(2,1)S(1)} %get-tuple-element.30), channel_id=1, source_target_pairs={{0,4},{4,0},{8,12},{12,8},{16,20},{20,16},{24,28},{28,24},{1,5},{5... | collective-permute-start | bytes 393224 | tf_op jit(solution)/shard_map/ppermute | solution.py:403
  36.5 8.2 %copy-start = (bf16[1024,1024]{1,0:T(8,128)(2,1)S(1)}, bf16[1024,1024]{1,0:T(8,128)(2,1)}, u32[]{:S(2)}) copy-start(bf16[1024,1024]{1,0:T(8,128)(2,1)} %w.3) | copy-start | bytes 6291460
  37.1 7.5 %collective-permute-start.6 = (bf16[128,512]{1,0:T(8,128)(2,1)S(1)}, bf16[128,512]{1,0:T(8,128)(2,1)S(1)}, u32[]{:S(2)}, u32[]{:S(2)}) collective-permute-start(bf16[128,512]{1,0:T(8,128)(2,1)S(1)} %get-tuple-element.34), channel_id=1, source_target_pairs={{0,4},{4,0},{8,12},{12,8},{16,20},{20,16},{24,28},{28,24},{1,5},{5... | collective-permute-start | bytes 393224 | tf_op jit(solution)/shard_map/ppermute | solution.py:403
  38.8 9.9 %collective-permute-start.9 = (bf16[256,512]{1,0:T(8,128)(2,1)S(1)}, bf16[256,512]{1,0:T(8,128)(2,1)S(1)}, u32[]{:S(2)}, u32[]{:S(2)}) collective-permute-start(bf16[256,512]{1,0:T(8,128)(2,1)S(1)} %add_returned.1), channel_id=1, source_target_pairs={{0,4},{4,0},{8,12},{12,8},{16,20},{20,16},{24,28},{28,24},{1,5},{5... | collective-permute-start | bytes 786440 | tf_op jit(solution)/shard_map/ppermute | solution.py:403
  40.9 7.8 %collective-permute-start.15 = (bf16[32,1024]{1,0:T(8,128)(2,1)S(1)}, bf16[32,1024]{1,0:T(8,128)(2,1)S(1)}, u32[]{:S(2)}, u32[]{:S(2)}) collective-permute-start(bf16[32,1024]{1,0:T(8,128)(2,1)S(1)} %slice.36), channel_id=1, source_target_pairs={{0,16},{4,20},{8,24},{12,28},{16,0},{20,4},{24,8},{28,12},{1,17},{... | collective-permute-start | bytes 196616 | tf_op jit(solution)/shard_map/ppermute | solution.py:441

commit v2 on v1

--- a/solution.py
+++ b/solution.py
@@ -439,6 +439,8 @@
         step *= 2
     for place, (axis, count, bit) in enumerate(hops):
         out = lax.ppermute(out, axis, [(i, i ^ bit) for i in range(count)])
+        if place == 0:
+            out, d_own, att_back = lax.optimization_barrier((out, d_own, att_back))
         if place + 1 < len(hops):
             total = keep + out.astype(F32)
             rows = total.shape[0] // 2

time: 49.9 us -> 48.1 us (0.964)
  waiting for transfers between devices: 16.2 us -> 15.1 us
  starting transfers between devices: 22.1 us -> 21.4 us
    ppermute x3, waiting for transfers between devices: 2.26 us -> 0.88 us  [on_device(): out = lax.ppermute(out, axis, [(i, i ^ bit) for i in range(count)])]
  transfers between devices with their start and end apart: 16 -> 16, of which waited for: 8 -> 7; matrix products, arithmetic and copies ran while one was open for 0% -> 0% of each run, Pallas kernels for 15% -> 16%
where the time goes in v2:
time: 48.1 us; the launch traced here: 47.8 us
  starting transfers between devices  21.4 us (44%)
  waiting for transfers between devices  15.1 us (31%)
  Pallas kernels  10.3 us (21%)
  between operations  0.84 us (2%)
    ppermute x10, starting transfers between devices, on_device(): send = lambda x, pairs: lax.ppermute(x, 'seq', pairs)  16.7 us
    ppermute x10, waiting for transfers between devices, on_device(): send = lambda x, pairs: lax.ppermute(x, 'seq', pairs)  14.2 us
    ppermute x3, starting transfers between devices, on_device(): out = lax.ppermute(out, axis, [(i, i ^ bit) for i in range(count)])  4.56 us
    pallas_call x1, Pallas kernels, grad_attended(): call(turn_kernel, (shape_of(2 * tokens, pairs * HD),), [HBM, VMEM, HBM],...  2.32 us
    pallas_call x1, Pallas kernels, forward(): call(functools.partial(forward_kernel, direct, n_dp), (shape_of(pairs, 3...  1.59 us
    pallas_call x1, Pallas kernels, backward(): call(backward_kernel, (shape_of(*probs.shape),) + (shape_of(2 * tokens, h...  1.35 us
    pallas_call x1, Pallas kernels, pack(): call(pack_kernel, (kv, kv) + (shape_of(tokens + FLAG_ROWS, half),) * 2, [...  1.34 us
    pallas_call x1, Pallas kernels, finish_queries(): call(query_kernel, (shape_of(tokens, w.shape[1]), shape_of(tokens, w.shap...  1.19 us
  transfers between devices with their start and end apart: 16, of which 7 were waited for; matrix products, arithmetic and copies ran while one was open for 0% of the time, Pallas kernels for 16%

profile of v2, /device:TPU:0, one launch (start us, length us, event | category | flops | bytes accessed | tf_op | source)
XLA Modules:
  0.0 47.8 jit_solution(3638068620316748142)
XLA Ops:
  0.6 1.3 %pack_heads.1 = (bf16[256,512]{1,0:T(8,128)(2,1)S(1)}, bf16[256,512]{1,0:T(8,128)(2,1)S(1)}, bf16[144,512]{1,0:T(8,128)(2,1)S(1)}, bf16[144,512]{1,0:T(8,128)(2,1)S(1)}) custom-call(s32[1,2]{1,0:T(1,128)} %bitcast.21, bf16[128,1024]{1,0:T(8,128)(2,1)} %bitcast.18, bf16[128,1024]{1,0:T(8,128)(2,1)} %bitcast.19, bf16[128,1024]{1,0:T(8,128)(2,1)} %bitcast.20), custom_call_target="tpu_custom_call" | custom-call | tf_op jit(solution)/shard_map/pack_heads/pallas_call | solution.py:97
  2.0 3.0 %collective-permute-start.1 = (bf16[256,512]{1,0:T(8,128)(2,1)S(1)}, bf16[256,512]{1,0:T(8,128)(2,1)S(1)}, u32[]{:S(2)}, u32[]{:S(2)}) collective-permute-start(bf16[256,512]{1,0:T(8,128)(2,1)S(1)} %get-tuple-element.31), channel_id=1, source_target_pairs={{0,4},{4,0},{8,12},{12,8},{16,20},{20,16},{24,28},{28,24},{1,5},{5... | collective-permute-start | bytes 786440 | tf_op jit(solution)/shard_map/ppermute | solution.py:403
  5.0 0.1 collective-permute-start.4
  5.1 1.3 %collective-permute-start.3 = (bf16[256,512]{1,0:T(8,128)(2,1)S(1)}, bf16[256,512]{1,0:T(8,128)(2,1)S(1)}, u32[]{:S(2)}, u32[]{:S(2)}) collective-permute-start(bf16[256,512]{1,0:T(8,128)(2,1)S(1)} %get-tuple-element.30.own), channel_id=1, source_target_pairs={{8,0},{16,8},{24,16},{4,12},{12,20},{20,28},{9,1},{17,9},{25,17},{... | collective-permute-start | bytes 786440 | tf_op jit(solution)/shard_map/ppermute | solution.py:403
  6.4 5.8 %collective-permute-done.1.par = bf16[256,512]{1,0:T(8,128)(2,1)S(1)} collective-permute-done((bf16[256,512]{1,0:T(8,128)(2,1)S(1)}, bf16[256,512]{1,0:T(8,128)(2,1)S(1)}, u32[]{:S(2)}, u32[]{:S(2)}) %collective-permute-start.1) | collective-permute-done | bytes 262176 | tf_op jit(solution)/shard_map/ppermute | solution.py:403
  12.1 4.0 %collective-permute-start.2 = (bf16[256,512]{1,0:T(8,128)(2,1)S(1)}, bf16[256,512]{1,0:T(8,128)(2,1)S(1)}, u32[]{:S(2)}, u32[]{:S(2)}) collective-permute-start(bf16[256,512]{1,0:T(8,128)(2,1)S(1)} %collective-permute-done.1.par), channel_id=1, source_target_pairs={{0,8},{8,16},{16,24},{12,4},{20,12},{28,20},{1,9},{9,17},{17,25},{... | collective-permute-start | bytes 786440 | tf_op jit(solution)/shard_map/ppermute | solution.py:403
  16.2 0.1 collective-permute-start
  16.3 0.1 collective-permute-start.6
  16.3 1.1 %collective-permute-done.4.cot_par.par = bf16[128,1024]{1,0:T(8,128)(2,1)S(1)} collective-permute-done((bf16[128,1024]{1,0:T(8,128)(2,1)}, bf16[128,1024]{1,0:T(8,128)(2,1)S(1)}, u32[]{:S(2)}, u32[]{:S(2)}) %collective-permute-start.4) | collective-permute-done | bytes 262176 | tf_op jit(solution)/shard_map/ppermute | solution.py:403
  17.4 0.0 collective-permute-start.7
  17.4 2.3 %grad_attended.1.after.ga = bf16[256,512]{1,0:T(8,128)(2,1)S(1)} custom-call(bf16[128,1024]{1,0:T(8,128)(2,1)} %bitcast.15, bf16[128,1024]{1,0:T(8,128)(2,1)S(1)} %collective-permute-done.4.cot_par.par, bf16[1024,1024]{1,0:T(8,128)(2,1)} %w.3), custom_call_target="tpu_custom_call" | custom-call | tf_op jit(solution)/shard_map/grad_attended/pallas_call | solution.py:129
  19.8 1.6 %collective-permute-done.q_par = bf16[144,512]{1,0:T(8,128)(2,1)S(1)} collective-permute-done((bf16[144,512]{1,0:T(8,128)(2,1)S(1)}, bf16[144,512]{1,0:T(8,128)(2,1)S(1)}, u32[]{:S(2)}, u32[]{:S(2)}) %collective-permute-start) | collective-permute-done | bytes 147488 | tf_op jit(solution)/shard_map/ppermute | solution.py:403
  21.4 0.0 collective-permute-done.3.far_par
  21.4 0.0 collective-permute-done.2.far_own
  21.4 0.0 copy-start.1
  21.4 1.6 %patch_forward.1 = (bf16[4,384,256]{2,1,0:T(8,128)(2,1)S(1)}, bf16[128,512]{1,0:T(8,128)(2,1)S(1)}, bf16[128,512]{1,0:T(8,128)(2,1)S(1)}, bf16[2,256,256]{2,1,0:T(8,128)(2,1)S(1)}) custom-call(bf16[144,512]{1,0:T(8,128)(2,1)S(1)} %get-tuple-element.28.q_own, bf16[144,512]{1,0:T(8,128)(2,1)S(1)} %collective-permute-done.q_par, ...), custom_call_target="tpu_custom_call" | custom-call | tf_op jit(solution)/shard_map/patch_forward/pallas_call | solution.py:209
  23.0 0.1 collective-permute-start.5
  23.1 1.4 %patch_backward.1 = (bf16[4,384,256]{2,1,0:T(8,128)(2,1)S(1)}, bf16[256,512]{1,0:T(8,128)(2,1)S(1)}, bf16[256,512]{1,0:T(8,128)(2,1)S(1)}) custom-call(bf16[144,512]{1,0:T(8,128)(2,1)S(1)} %get-tuple-element.28.q_own, bf16[144,512]{1,0:T(8,128)(2,1)S(1)} %collective-permute-done.q_par, bf16[256,512]{1,0:T(8,128)(2,1)S(1)} %get-tuple-element.30.own, ...), custom_call_target="tpu_custom_call" | custom-call | tf_op jit(solution)/shard_map/patch_backward/pallas_call | solution.py:269
  24.5 0.0 collective-permute-done.6.core_own
  24.5 0.0 collective-permute-done.7.core_par
  24.5 0.0 collective-permute-done.5.att_core
  24.5 0.0 copy-done.1
  24.5 0.4 weight_terms_sent.1._after
  24.9 1.6 %collective-permute-start.8 = (bf16[128,1024]{1,0:T(8,128)(2,1)S(1)}, bf16[128,1024]{1,0:T(8,128)(2,1)S(1)}, u32[]{:S(2)}, u32[]{:S(2)}) collective-permute-start(bf16[128,1024]{1,0:T(8,128)(2,1)S(1)} %weight_terms_sent.1._after), channel_id=1, source_target_pairs={{0,2},{1,3},{2,0},{3,1},{4,6},{5,7},{6,4},{7,5},{8,10},{9,11},{10,... | collective-permute-start | bytes 786440 | tf_op jit(solution)/shard_map/ppermute | solution.py:441
  26.5 1.3 %collective-permute-start.9 = (bf16[128,512]{1,0:T(8,128)(2,1)S(1)}, bf16[128,512]{1,0:T(8,128)(2,1)S(1)}, u32[]{:S(2)}, u32[]{:S(2)}) collective-permute-start(bf16[128,512]{1,0:T(8,128)(2,1)S(1)} %get-tuple-element.38), channel_id=1, source_target_pairs={{0,4},{4,0},{8,12},{12,8},{16,20},{20,16},{24,28},{28,24},{1,5},{5... | collective-permute-start | bytes 393224 | tf_op jit(solution)/shard_map/ppermute | solution.py:403
  27.8 0.7 %collective-permute-start.11 = (bf16[256,512]{1,0:T(8,128)(2,1)S(1)}, bf16[256,512]{1,0:T(8,128)(2,1)S(1)}, u32[]{:S(2)}, u32[]{:S(2)}) collective-permute-start(bf16[256,512]{1,0:T(8,128)(2,1)S(1)} %get-tuple-element.35._after), channel_id=1, source_target_pairs={{8,16},{12,20},{16,8},{20,12},{9,17},{13,21},{17,9},{21,13},{10,18... | collective-permute-start | bytes 786440 | tf_op jit(solution)/shard_map/ppermute | solution.py:403
  28.4 4.5 %collective-permute-start.12 = (bf16[256,512]{1,0:T(8,128)(2,1)S(1)}, bf16[256,512]{1,0:T(8,128)(2,1)S(1)}, u32[]{:S(2)}, u32[]{:S(2)}) collective-permute-start(bf16[256,512]{1,0:T(8,128)(2,1)S(1)} %get-tuple-element.45), channel_id=1, source_target_pairs={{0,8},{4,12},{8,0},{12,4},{16,24},{20,28},{24,16},{28,20},{1,9},{5... | collective-permute-start | bytes 786440 | tf_op jit(solution)/shard_map/ppermute | solution.py:403
  32.9 0.7 %patch_gradients.1 = (bf16[128,512]{1,0:T(8,128)(2,1)S(1)}, bf16[128,512]{1,0:T(8,128)(2,1)S(1)}, bf16[256,512]{1,0:T(8,128)(2,1)S(1)}, bf16[256,512]{1,0:T(8,128)(2,1)S(1)}) custom-call(bf16[144,512]{1,0:T(8,128)(2,1)S(1)} %get-tuple-element.28.q_own, bf16[144,512]{1,0:T(8,128)(2,1)S(1)} %collective-permute-done.q_par, ...), custom_call_target="tpu_custom_call" | custom-call | tf_op jit(solution)/shard_map/patch_gradients/pallas_call | solution.py:305
  33.5 0.4 weight_terms_kept.1
  34.0 0.0 copy-start
  34.0 0.0 collective-permute-done.9.att_back
  34.0 0.0 collective-permute-done.8
  34.0 0.1 convert_add_fusion
  34.1 1.3 %collective-permute-start.14 = (bf16[64,1024]{1,0:T(8,128)(2,1)S(1)}, bf16[64,1024]{1,0:T(8,128)(2,1)S(1)}, u32[]{:S(2)}, u32[]{:S(2)}) collective-permute-start(bf16[64,1024]{1,0:T(8,128)(2,1)S(1)} %slice.35), channel_id=1, source_target_pairs={{0,8},{4,12},{8,0},{12,4},{16,24},{20,28},{24,16},{28,20},{1,9},{5... | collective-permute-start | bytes 393224 | tf_op jit(solution)/shard_map/ppermute | solution.py:441
  35.4 1.1 %collective-permute-start.10 = (bf16[128,512]{1,0:T(8,128)(2,1)S(1)}, bf16[128,512]{1,0:T(8,128)(2,1)S(1)}, u32[]{:S(2)}, u32[]{:S(2)}) collective-permute-start(bf16[128,512]{1,0:T(8,128)(2,1)S(1)} %get-tuple-element.41), channel_id=1, source_target_pairs={{0,4},{4,0},{8,12},{12,8},{16,20},{20,16},{24,28},{28,24},{1,5},{5... | collective-permute-start | bytes 393224 | tf_op jit(solution)/shard_map/ppermute | solution.py:403
  36.5 3.6 %collective-permute-done.12.far_b = bf16[256,512]{1,0:T(8,128)(2,1)S(1)} collective-permute-done((bf16[256,512]{1,0:T(8,128)(2,1)S(1)}, bf16[256,512]{1,0:T(8,128)(2,1)S(1)}, u32[]{:S(2)}, u32[]{:S(2)}) %collective-permute-start.12) | collective-permute-done | bytes 262176 | tf_op jit(solution)/shard_map/ppermute | solution.py:403
  40.1 0.0 collective-permute-done.11.far_a
  40.1 0.1 add_returned.1
  40.2 0.8 %collective-permute-start.13 = (bf16[256,512]{1,0:T(8,128)(2,1)S(1)}, bf16[256,512]{1,0:T(8,128)(2,1)S(1)}, u32[]{:S(2)}, u32[]{:S(2)}) collective-permute-start(bf16[256,512]{1,0:T(8,128)(2,1)S(1)} %add_returned.1), channel_id=1, source_target_pairs={{0,4},{4,0},{8,12},{12,8},{16,20},{20,16},{24,28},{28,24},{1,5},{5... | collective-permute-start | bytes 786440 | tf_op jit(solution)/shard_map/ppermute | solution.py:403
  41.0 0.6 %collective-permute-done.14 = bf16[64,1024]{1,0:T(8,128)(2,1)S(1)} collective-permute-done((bf16[64,1024]{1,0:T(8,128)(2,1)S(1)}, bf16[64,1024]{1,0:T(8,128)(2,1)S(1)}, u32[]{:S(2)}, u32[]{:S(2)}) %collective-permute-start.14) | collective-permute-done | bytes 131104 | tf_op jit(solution)/shard_map/ppermute | solution.py:441
  41.6 1.7 %collective-permute-start.15 = (bf16[32,1024]{1,0:T(8,128)(2,1)S(1)}, bf16[32,1024]{1,0:T(8,128)(2,1)S(1)}, u32[]{:S(2)}, u32[]{:S(2)}) collective-permute-start(bf16[32,1024]{1,0:T(8,128)(2,1)S(1)} %slice.36), channel_id=1, source_target_pairs={{0,16},{4,20},{8,24},{12,28},{16,0},{20,4},{24,8},{28,12},{1,17},{... | collective-permute-start | bytes 196616 | tf_op jit(solution)/shard_map/ppermute | solution.py:441
  43.3 0.0 collective-permute-done.10.dq_back
  43.3 0.0 copy-done
  43.3 1.2 %finish_queries.1 = (bf16[128,1024]{1,0:T(8,128)(2,1)}, bf16[128,1024]{1,0:T(8,128)(2,1)}) custom-call(bf16[128,512]{1,0:T(8,128)(2,1)S(1)} %get-tuple-element.32.att_own, bf16[128,512]{1,0:T(8,128)(2,1)S(1)} %collective-permute-done.9.att_back, bf16[128,512]{1,0:T(8,128)(2,1)S(1)} %get-tuple-element.40.dq_own, ...), custom_call_target="tpu_custom_call" | custom-call | tf_op jit(solution)/shard_map/finish_queries/pallas_call | solution.py:344
  44.5 2.1 %collective-permute-done.13.home = bf16[256,512]{1,0:T(8,128)(2,1)S(1)} collective-permute-done((bf16[256,512]{1,0:T(8,128)(2,1)S(1)}, bf16[256,512]{1,0:T(8,128)(2,1)S(1)}, u32[]{:S(2)}, u32[]{:S(2)}) %collective-permute-start.13) | collective-permute-done | bytes 262176 | tf_op jit(solution)/shard_map/ppermute | solution.py:403
  46.6 0.2 collective-permute-done.15.out
  46.9 0.9 %finish_keys.1 = (bf16[128,1024]{1,0:T(8,128)(2,1)}, bf16[128,1024]{1,0:T(8,128)(2,1)}, f32[32,1024]{1,0:T(8,128)}) custom-call(bf16[256,512]{1,0:T(8,128)(2,1)S(1)} %get-tuple-element.44.own, bf16[256,512]{1,0:T(8,128)(2,1)S(1)} %collective-permute-done.11.far_a, bf16[256,512]{1,0:T(8,128)(2,1)S(1)} %collective-permute-done.12.far_b, ...), custom_call_target="tpu_custom_call" | custom-call | tf_op jit(solution)/shard_map/finish_keys/pallas_call | solution.py:381
  (5 shorter events, 0.1 us)
Async XLA Ops:
  2.0 10.2 %collective-permute-start.1 = (bf16[256,512]{1,0:T(8,128)(2,1)S(1)}, bf16[256,512]{1,0:T(8,128)(2,1)S(1)}, u32[]{:S(2)}, u32[]{:S(2)}) collective-permute-start(bf16[256,512]{1,0:T(8,128)(2,1)S(1)} %get-tuple-element.31), channel_id=1, source_target_pairs={{0,4},{4,0},{8,12},{12,8},{16,20},{20,16},{24,28},{28,24},{1,5},{5... | collective-permute-start | bytes 786440 | tf_op jit(solution)/shard_map/ppermute | solution.py:403
  5.0 12.4 %collective-permute-start.4 = (bf16[128,1024]{1,0:T(8,128)(2,1)}, bf16[128,1024]{1,0:T(8,128)(2,1)S(1)}, u32[]{:S(2)}, u32[]{:S(2)}) collective-permute-start(bf16[128,1024]{1,0:T(8,128)(2,1)} %bitcast.13), channel_id=1, source_target_pairs={{0,4},{4,0},{8,12},{12,8},{16,20},{20,16},{24,28},{28,24},{1,5},{5... | collective-permute-start | bytes 786440 | tf_op jit(solution)/shard_map/ppermute | solution.py:403
  5.1 16.3 %collective-permute-start.3 = (bf16[256,512]{1,0:T(8,128)(2,1)S(1)}, bf16[256,512]{1,0:T(8,128)(2,1)S(1)}, u32[]{:S(2)}, u32[]{:S(2)}) collective-permute-start(bf16[256,512]{1,0:T(8,128)(2,1)S(1)} %get-tuple-element.30.own), channel_id=1, source_target_pairs={{8,0},{16,8},{24,16},{4,12},{12,20},{20,28},{9,1},{17,9},{25,17},{... | collective-permute-start | bytes 786440 | tf_op jit(solution)/shard_map/ppermute | solution.py:403
  12.1 9.2 %collective-permute-start.2 = (bf16[256,512]{1,0:T(8,128)(2,1)S(1)}, bf16[256,512]{1,0:T(8,128)(2,1)S(1)}, u32[]{:S(2)}, u32[]{:S(2)}) collective-permute-start(bf16[256,512]{1,0:T(8,128)(2,1)S(1)} %collective-permute-done.1.par), channel_id=1, source_target_pairs={{0,8},{8,16},{16,24},{12,4},{20,12},{28,20},{1,9},{9,17},{17,25},{... | collective-permute-start | bytes 786440 | tf_op jit(solution)/shard_map/ppermute | solution.py:403
  16.2 5.2 %collective-permute-start = (bf16[144,512]{1,0:T(8,128)(2,1)S(1)}, bf16[144,512]{1,0:T(8,128)(2,1)S(1)}, u32[]{:S(2)}, u32[]{:S(2)}) collective-permute-start(bf16[144,512]{1,0:T(8,128)(2,1)S(1)} %get-tuple-element.29), channel_id=1, source_target_pairs={{0,4},{4,0},{8,12},{12,8},{16,20},{20,16},{24,28},{28,24},{1,5},{5... | collective-permute-start | bytes 442376 | tf_op jit(solution)/shard_map/ppermute | solution.py:403
  16.3 8.2 %collective-permute-start.6 = (bf16[128,1024]{1,0:T(8,128)(2,1)}, bf16[128,1024]{1,0:T(8,128)(2,1)S(1)}, u32[]{:S(2)}, u32[]{:S(2)}) collective-permute-start(bf16[128,1024]{1,0:T(8,128)(2,1)} %bitcast.14), channel_id=1, source_target_pairs={{0,1},{1,0},{2,3},{3,2},{4,5},{5,4},{6,7},{7,6},{8,9},{9,8},{10,11... | collective-permute-start | bytes 786440 | tf_op jit(solution)/shard_map/ppermute | solution.py:404
  17.4 7.0 %collective-permute-start.7 = (bf16[128,1024]{1,0:T(8,128)(2,1)S(1)}, bf16[128,1024]{1,0:T(8,128)(2,1)S(1)}, u32[]{:S(2)}, u32[]{:S(2)}) collective-permute-start(bf16[128,1024]{1,0:T(8,128)(2,1)S(1)} %collective-permute-done.4.cot_par.par), channel_id=1, source_target_pairs={{0,1},{1,0},{2,3},{3,2},{4,5},{5,4},{6,7},{7,6},{8,9},{9,8},{10,11... | collective-permute-start | bytes 786440 | tf_op jit(solution)/shard_map/ppermute | solution.py:404
  21.4 3.1 %copy-start.1 = (bf16[1,128,1024]{2,1,0:T(8,128)(2,1)S(1)}, bf16[1,128,1024]{2,1,0:T(8,128)(2,1)}, u32[]{:S(2)}) copy-start(bf16[1,128,1024]{2,1,0:T(8,128)(2,1)} %param.11) | copy-start | bytes 786436
  23.0 1.5 %collective-permute-start.5 = (bf16[256,256]{1,0:T(8,128)(2,1)S(1)}, bf16[256,256]{1,0:T(8,128)(2,1)S(1)}, u32[]{:S(2)}, u32[]{:S(2)}) collective-permute-start(bf16[256,256]{1,0:T(8,128)(2,1)S(1)} %get-tuple-element.51), channel_id=1, source_target_pairs={{0,1},{1,0},{2,3},{3,2},{4,5},{5,4},{6,7},{7,6},{8,9},{9,8},{10,11... | collective-permute-start | bytes 393224 | tf_op jit(solution)/shard_map/ppermute | solution.py:404
  24.9 9.1 %collective-permute-start.8 = (bf16[128,1024]{1,0:T(8,128)(2,1)S(1)}, bf16[128,1024]{1,0:T(8,128)(2,1)S(1)}, u32[]{:S(2)}, u32[]{:S(2)}) collective-permute-start(bf16[128,1024]{1,0:T(8,128)(2,1)S(1)} %weight_terms_sent.1._after), channel_id=1, source_target_pairs={{0,2},{1,3},{2,0},{3,1},{4,6},{5,7},{6,4},{7,5},{8,10},{9,11},{10,... | collective-permute-start | bytes 786440 | tf_op jit(solution)/shard_map/ppermute | solution.py:441
  26.5 7.5 %collective-permute-start.9 = (bf16[128,512]{1,0:T(8,128)(2,1)S(1)}, bf16[128,512]{1,0:T(8,128)(2,1)S(1)}, u32[]{:S(2)}, u32[]{:S(2)}) collective-permute-start(bf16[128,512]{1,0:T(8,128)(2,1)S(1)} %get-tuple-element.38), channel_id=1, source_target_pairs={{0,4},{4,0},{8,12},{12,8},{16,20},{20,16},{24,28},{28,24},{1,5},{5... | collective-permute-start | bytes 393224 | tf_op jit(solution)/shard_map/ppermute | solution.py:403
  27.8 12.3 %collective-permute-start.11 = (bf16[256,512]{1,0:T(8,128)(2,1)S(1)}, bf16[256,512]{1,0:T(8,128)(2,1)S(1)}, u32[]{:S(2)}, u32[]{:S(2)}) collective-permute-start(bf16[256,512]{1,0:T(8,128)(2,1)S(1)} %get-tuple-element.35._after), channel_id=1, source_target_pairs={{8,16},{12,20},{16,8},{20,12},{9,17},{13,21},{17,9},{21,13},{10,18... | collective-permute-start | bytes 786440 | tf_op jit(solution)/shard_map/ppermute | solution.py:403
  28.4 11.6 %collective-permute-start.12 = (bf16[256,512]{1,0:T(8,128)(2,1)S(1)}, bf16[256,512]{1,0:T(8,128)(2,1)S(1)}, u32[]{:S(2)}, u32[]{:S(2)}) collective-permute-start(bf16[256,512]{1,0:T(8,128)(2,1)S(1)} %get-tuple-element.45), channel_id=1, source_target_pairs={{0,8},{4,12},{8,0},{12,4},{16,24},{20,28},{24,16},{28,20},{1,9},{5... | collective-permute-start | bytes 786440 | tf_op jit(solution)/shard_map/ppermute | solution.py:403
  34.0 9.4 %copy-start = (bf16[1024,1024]{1,0:T(8,128)(2,1)S(1)}, bf16[1024,1024]{1,0:T(8,128)(2,1)}, u32[]{:S(2)}) copy-start(bf16[1024,1024]{1,0:T(8,128)(2,1)} %w.3) | copy-start | bytes 6291460
  34.1 7.5 %collective-permute-start.14 = (bf16[64,1024]{1,0:T(8,128)(2,1)S(1)}, bf16[64,1024]{1,0:T(8,128)(2,1)S(1)}, u32[]{:S(2)}, u32[]{:S(2)}) collective-permute-start(bf16[64,1024]{1,0:T(8,128)(2,1)S(1)} %slice.35), channel_id=1, source_target_pairs={{0,8},{4,12},{8,0},{12,4},{16,24},{20,28},{24,16},{28,20},{1,9},{5... | collective-permute-start | bytes 393224 | tf_op jit(solution)/shard_map/ppermute | solution.py:441
  35.4 7.9 %collective-permute-start.10 = (bf16[128,512]{1,0:T(8,128)(2,1)S(1)}, bf16[128,512]{1,0:T(8,128)(2,1)S(1)}, u32[]{:S(2)}, u32[]{:S(2)}) collective-permute-start(bf16[128,512]{1,0:T(8,128)(2,1)S(1)} %get-tuple-element.41), channel_id=1, source_target_pairs={{0,4},{4,0},{8,12},{12,8},{16,20},{20,16},{24,28},{28,24},{1,5},{5... | collective-permute-start | bytes 393224 | tf_op jit(solution)/shard_map/ppermute | solution.py:403
  40.2 6.4 %collective-permute-start.13 = (bf16[256,512]{1,0:T(8,128)(2,1)S(1)}, bf16[256,512]{1,0:T(8,128)(2,1)S(1)}, u32[]{:S(2)}, u32[]{:S(2)}) collective-permute-start(bf16[256,512]{1,0:T(8,128)(2,1)S(1)} %add_returned.1), channel_id=1, source_target_pairs={{0,4},{4,0},{8,12},{12,8},{16,20},{20,16},{24,28},{28,24},{1,5},{5... | collective-permute-start | bytes 786440 | tf_op jit(solution)/shard_map/ppermute | solution.py:403
  41.6 5.2 %collective-permute-start.15 = (bf16[32,1024]{1,0:T(8,128)(2,1)S(1)}, bf16[32,1024]{1,0:T(8,128)(2,1)S(1)}, u32[]{:S(2)}, u32[]{:S(2)}) collective-permute-start(bf16[32,1024]{1,0:T(8,128)(2,1)S(1)} %slice.36), channel_id=1, source_target_pairs={{0,16},{4,20},{8,24},{12,28},{16,0},{20,4},{24,8},{28,12},{1,17},{... | collective-permute-start | bytes 196616 | tf_op jit(solution)/shard_map/ppermute | solution.py:441

commit v3 on v2

--- a/solution.py
+++ b/solution.py
@@ -362,28 +362,61 @@
     )(d_par, *far)[0]
 
 
-def key_kernel(own, far_a, far_b, home, keep, out, dk, dv, total):
-    mine = lax.axis_index("seq") & 1
-    slot = far_slot(lax.axis_index("seq"))
-    tokens = dk.shape[0]
-    for i, target in ((0, dk), (1, dv)):
-        rows = slice(i * tokens, (i + 1) * tokens)
-        for j in range(own.shape[1] // HD):
-            cols = slice(j * HD, (j + 1) * HD)
-            far = jnp.where(slot == 0, far_a[rows, cols].astype(F32), far_b[rows, cols].astype(F32))
-            target[:, head_cols(j, mine)] = (own[rows, cols].astype(F32) + far).astype(BF16)
-            target[:, head_cols(j, 1 - mine)] = home[rows, cols]
+def column_copies(source, targets, parity, sems):
+    tokens = targets[0].shape[0]
+    copies = []
+    for i, target in enumerate(targets):
+        for j in range(source.shape[1] // HD):
+            copies.append(
+                pltpu.make_async_copy(
+                    source.at[i * tokens : (i + 1) * tokens, j * HD : (j + 1) * HD],
+                    target.at[:, head_cols(j, parity)],
+                    sems.at[len(copies)],
+                )
+            )
+            copies[-1].start()
+    return copies
+
+
+def own_kernel(own, far_a, far_b, dk, dv, total, sems):
+    me = lax.axis_index("seq")
+    far = jnp.where(far_slot(me) == 0, far_a[...].astype(F32), far_b[...].astype(F32))
+    total[...] = (own[...].astype(F32) + far).astype(BF16)
+    for item in column_copies(total, (dk, dv), me & 1, sems):
+        item.wait()
+
+
+def home_kernel(_dk, _dv, home, keep, out, dk, dv, total, sems):
+    copies = column_copies(home, (dk, dv), 1 - (lax.axis_index("seq") & 1), sems)
     total[...] = keep[...] + out[...].astype(F32)
+    for item in copies:
+        item.wait()
 
 
 def finish_keys(own, far, home, keep, out):
     tokens, half = own.shape[0] // 2, own.shape[1]
-    return call(
-        key_kernel,
-        (shape_of(tokens, 2 * half),) * 2 + (shape_of(*keep.shape, dtype=F32),),
-        [VMEM] * 6,
-        "finish_keys",
-    )(own, *far, home, keep, out)
+    params = pltpu.CompilerParams(vmem_limit_bytes=VMEM_LIMIT)
+    sems = pltpu.SemaphoreType.DMA((2 * half // HD,))
+    shapes = (shape_of(tokens, 2 * half),) * 2
+    begun = pl.pallas_call(
+        own_kernel,
+        out_shape=shapes,
+        in_specs=[VMEM] * 3,
+        out_specs=(HBM, HBM),
+        scratch_shapes=[pltpu.VMEM(own.shape, BF16), sems],
+        compiler_params=params,
+        name="finish_own_heads",
+    )(own, *far)
+    return pl.pallas_call(
+        home_kernel,
+        out_shape=shapes + (shape_of(*keep.shape, dtype=F32),),
+        in_specs=[HBM, HBM] + [VMEM] * 3,
+        out_specs=(HBM, HBM, VMEM),
+        input_output_aliases={0: 0, 1: 1},
+        scratch_shapes=[sems],
+        compiler_params=params,
+        name="finish_home_heads",
+    )(*begun, home, keep, out)
 
 
 def on_device(queries, key_states, values, w_out, cotangent, neighbours, counts):

time: 48.1 us -> 48.6 us (1.010)
  Pallas kernels: 10.3 us -> 11.7 us
  waiting for transfers between devices: 15.1 us -> 14.2 us
    pallas_call x1 -> x2, Pallas kernels: 0.92 us -> 2.29 us  [the longest x1 1.43 us: finish_keys(): pl.pallas_call(home_kernel, out_shape=shapes + (shape_of(*keep.shape, dty...]
    ppermute x10, waiting for transfers between devices: 14.2 us -> 13.3 us  [on_device(): send = lambda x, pairs: lax.ppermute(x, 'seq', pairs)]
  transfers between devices with their start and end apart: 16 -> 16, of which waited for: 7 -> 7; matrix products, arithmetic and copies ran while one was open for 0% -> 0% of each run, Pallas kernels for 16% -> 18%
where the time goes in v3:
time: 48.6 us; the launch traced here: 48.3 us
  starting transfers between devices  21.4 us (44%)
  waiting for transfers between devices  14.2 us (29%)
  Pallas kernels  11.7 us (24%)
  between operations  0.86 us (2%)
    ppermute x10, starting transfers between devices, on_device(): send = lambda x, pairs: lax.ppermute(x, 'seq', pairs)  16.7 us
    ppermute x10, waiting for transfers between devices, on_device(): send = lambda x, pairs: lax.ppermute(x, 'seq', pairs)  13.3 us
    ppermute x3, starting transfers between devices, on_device(): out = lax.ppermute(out, axis, [(i, i ^ bit) for i in range(count)])  4.56 us
    pallas_call x1, Pallas kernels, grad_attended(): call(turn_kernel, (shape_of(2 * tokens, pairs * HD),), [HBM, VMEM, HBM],...  2.32 us
    pallas_call x1, Pallas kernels, forward(): call(functools.partial(forward_kernel, direct, n_dp), (shape_of(pairs, 3...  1.59 us
    pallas_call x1, Pallas kernels, finish_keys(): pl.pallas_call(home_kernel, out_shape=shapes + (shape_of(*keep.shape, dty...  1.43 us
    pallas_call x1, Pallas kernels, backward(): call(backward_kernel, (shape_of(*probs.shape),) + (shape_of(2 * tokens, h...  1.35 us
    pallas_call x1, Pallas kernels, pack(): call(pack_kernel, (kv, kv) + (shape_of(tokens + FLAG_ROWS, half),) * 2, [...  1.34 us
  transfers between devices with their start and end apart: 16, of which 7 were waited for; matrix products, arithmetic and copies ran while one was open for 0% of the time, Pallas kernels for 18%

profile of v3, /device:TPU:0, one launch (start us, length us, event | category | flops | bytes accessed | tf_op | source)
XLA Modules:
  0.0 48.3 jit_solution(14037182784010582347)
XLA Ops:
  0.6 1.3 %pack_heads.1 = (bf16[256,512]{1,0:T(8,128)(2,1)S(1)}, bf16[256,512]{1,0:T(8,128)(2,1)S(1)}, bf16[144,512]{1,0:T(8,128)(2,1)S(1)}, bf16[144,512]{1,0:T(8,128)(2,1)S(1)}) custom-call(s32[1,2]{1,0:T(1,128)} %bitcast.23, bf16[128,1024]{1,0:T(8,128)(2,1)} %bitcast.18, bf16[128,1024]{1,0:T(8,128)(2,1)} %bitcast.19, bf16[128,1024]{1,0:T(8,128)(2,1)} %bitcast.20), custom_call_target="tpu_custom_call" | custom-call | tf_op jit(solution)/shard_map/pack_heads/pallas_call | solution.py:97
  2.0 3.0 %collective-permute-start.1 = (bf16[256,512]{1,0:T(8,128)(2,1)S(1)}, bf16[256,512]{1,0:T(8,128)(2,1)S(1)}, u32[]{:S(2)}, u32[]{:S(2)}) collective-permute-start(bf16[256,512]{1,0:T(8,128)(2,1)S(1)} %get-tuple-element.33), channel_id=1, source_target_pairs={{0,4},{4,0},{8,12},{12,8},{16,20},{20,16},{24,28},{28,24},{1,5},{5... | collective-permute-start | bytes 786440 | tf_op jit(solution)/shard_map/ppermute | solution.py:436
  5.0 0.1 collective-permute-start.4
  5.1 1.3 %collective-permute-start.3 = (bf16[256,512]{1,0:T(8,128)(2,1)S(1)}, bf16[256,512]{1,0:T(8,128)(2,1)S(1)}, u32[]{:S(2)}, u32[]{:S(2)}) collective-permute-start(bf16[256,512]{1,0:T(8,128)(2,1)S(1)} %get-tuple-element.32.own), channel_id=1, source_target_pairs={{8,0},{16,8},{24,16},{4,12},{12,20},{20,28},{9,1},{17,9},{25,17},{... | collective-permute-start | bytes 786440 | tf_op jit(solution)/shard_map/ppermute | solution.py:436
  6.4 5.8 %collective-permute-done.1.par = bf16[256,512]{1,0:T(8,128)(2,1)S(1)} collective-permute-done((bf16[256,512]{1,0:T(8,128)(2,1)S(1)}, bf16[256,512]{1,0:T(8,128)(2,1)S(1)}, u32[]{:S(2)}, u32[]{:S(2)}) %collective-permute-start.1) | collective-permute-done | bytes 262176 | tf_op jit(solution)/shard_map/ppermute | solution.py:436
  12.1 4.0 %collective-permute-start.2 = (bf16[256,512]{1,0:T(8,128)(2,1)S(1)}, bf16[256,512]{1,0:T(8,128)(2,1)S(1)}, u32[]{:S(2)}, u32[]{:S(2)}) collective-permute-start(bf16[256,512]{1,0:T(8,128)(2,1)S(1)} %collective-permute-done.1.par), channel_id=1, source_target_pairs={{0,8},{8,16},{16,24},{12,4},{20,12},{28,20},{1,9},{9,17},{17,25},{... | collective-permute-start | bytes 786440 | tf_op jit(solution)/shard_map/ppermute | solution.py:436
  16.2 0.1 collective-permute-start
  16.3 0.1 collective-permute-start.6
  16.3 1.1 %collective-permute-done.4.cot_par.par = bf16[128,1024]{1,0:T(8,128)(2,1)S(1)} collective-permute-done((bf16[128,1024]{1,0:T(8,128)(2,1)}, bf16[128,1024]{1,0:T(8,128)(2,1)S(1)}, u32[]{:S(2)}, u32[]{:S(2)}) %collective-permute-start.4) | collective-permute-done | bytes 262176 | tf_op jit(solution)/shard_map/ppermute | solution.py:436
  17.4 0.0 collective-permute-start.7
  17.4 2.3 %grad_attended.1.after.ga = bf16[256,512]{1,0:T(8,128)(2,1)S(1)} custom-call(bf16[128,1024]{1,0:T(8,128)(2,1)} %bitcast.15, bf16[128,1024]{1,0:T(8,128)(2,1)S(1)} %collective-permute-done.4.cot_par.par, bf16[1024,1024]{1,0:T(8,128)(2,1)} %w.3), custom_call_target="tpu_custom_call" | custom-call | tf_op jit(solution)/shard_map/grad_attended/pallas_call | solution.py:129
  19.8 1.6 %collective-permute-done.q_par = bf16[144,512]{1,0:T(8,128)(2,1)S(1)} collective-permute-done((bf16[144,512]{1,0:T(8,128)(2,1)S(1)}, bf16[144,512]{1,0:T(8,128)(2,1)S(1)}, u32[]{:S(2)}, u32[]{:S(2)}) %collective-permute-start) | collective-permute-done | bytes 147488 | tf_op jit(solution)/shard_map/ppermute | solution.py:436
  21.4 0.0 collective-permute-done.3.far_par
  21.4 0.0 collective-permute-done.2.far_own
  21.4 0.0 copy-start.1
  21.4 1.6 %patch_forward.1 = (bf16[4,384,256]{2,1,0:T(8,128)(2,1)S(1)}, bf16[128,512]{1,0:T(8,128)(2,1)S(1)}, bf16[128,512]{1,0:T(8,128)(2,1)S(1)}, bf16[2,256,256]{2,1,0:T(8,128)(2,1)S(1)}) custom-call(bf16[144,512]{1,0:T(8,128)(2,1)S(1)} %get-tuple-element.30.q_own, bf16[144,512]{1,0:T(8,128)(2,1)S(1)} %collective-permute-done.q_par, ...), custom_call_target="tpu_custom_call" | custom-call | tf_op jit(solution)/shard_map/patch_forward/pallas_call | solution.py:209
  23.0 0.1 collective-permute-start.5
  23.1 1.4 %patch_backward.1 = (bf16[4,384,256]{2,1,0:T(8,128)(2,1)S(1)}, bf16[256,512]{1,0:T(8,128)(2,1)S(1)}, bf16[256,512]{1,0:T(8,128)(2,1)S(1)}) custom-call(bf16[144,512]{1,0:T(8,128)(2,1)S(1)} %get-tuple-element.30.q_own, bf16[144,512]{1,0:T(8,128)(2,1)S(1)} %collective-permute-done.q_par, bf16[256,512]{1,0:T(8,128)(2,1)S(1)} %get-tuple-element.32.own, ...), custom_call_target="tpu_custom_call" | custom-call | tf_op jit(solution)/shard_map/patch_backward/pallas_call | solution.py:269
  24.5 0.0 collective-permute-done.6.core_own
  24.5 0.0 collective-permute-done.7.core_par
  24.5 0.0 collective-permute-done.5.att_core
  24.5 0.0 copy-done.1
  24.5 0.4 weight_terms_sent.1._after
  24.9 1.6 %collective-permute-start.8 = (bf16[128,1024]{1,0:T(8,128)(2,1)S(1)}, bf16[128,1024]{1,0:T(8,128)(2,1)S(1)}, u32[]{:S(2)}, u32[]{:S(2)}) collective-permute-start(bf16[128,1024]{1,0:T(8,128)(2,1)S(1)} %weight_terms_sent.1._after), channel_id=1, source_target_pairs={{0,2},{1,3},{2,0},{3,1},{4,6},{5,7},{6,4},{7,5},{8,10},{9,11},{10,... | collective-permute-start | bytes 786440 | tf_op jit(solution)/shard_map/ppermute | solution.py:474
  26.5 1.3 %collective-permute-start.9 = (bf16[128,512]{1,0:T(8,128)(2,1)S(1)}, bf16[128,512]{1,0:T(8,128)(2,1)S(1)}, u32[]{:S(2)}, u32[]{:S(2)}) collective-permute-start(bf16[128,512]{1,0:T(8,128)(2,1)S(1)} %get-tuple-element.40), channel_id=1, source_target_pairs={{0,4},{4,0},{8,12},{12,8},{16,20},{20,16},{24,28},{28,24},{1,5},{5... | collective-permute-start | bytes 393224 | tf_op jit(solution)/shard_map/ppermute | solution.py:436
  27.8 0.7 %collective-permute-start.11 = (bf16[256,512]{1,0:T(8,128)(2,1)S(1)}, bf16[256,512]{1,0:T(8,128)(2,1)S(1)}, u32[]{:S(2)}, u32[]{:S(2)}) collective-permute-start(bf16[256,512]{1,0:T(8,128)(2,1)S(1)} %get-tuple-element.37._after), channel_id=1, source_target_pairs={{8,16},{12,20},{16,8},{20,12},{9,17},{13,21},{17,9},{21,13},{10,18... | collective-permute-start | bytes 786440 | tf_op jit(solution)/shard_map/ppermute | solution.py:436
  28.4 4.5 %collective-permute-start.12 = (bf16[256,512]{1,0:T(8,128)(2,1)S(1)}, bf16[256,512]{1,0:T(8,128)(2,1)S(1)}, u32[]{:S(2)}, u32[]{:S(2)}) collective-permute-start(bf16[256,512]{1,0:T(8,128)(2,1)S(1)} %get-tuple-element.47), channel_id=1, source_target_pairs={{0,8},{4,12},{8,0},{12,4},{16,24},{20,28},{24,16},{28,20},{1,9},{5... | collective-permute-start | bytes 786440 | tf_op jit(solution)/shard_map/ppermute | solution.py:436
  32.9 0.7 %patch_gradients.1 = (bf16[128,512]{1,0:T(8,128)(2,1)S(1)}, bf16[128,512]{1,0:T(8,128)(2,1)S(1)}, bf16[256,512]{1,0:T(8,128)(2,1)S(1)}, bf16[256,512]{1,0:T(8,128)(2,1)S(1)}) custom-call(bf16[144,512]{1,0:T(8,128)(2,1)S(1)} %get-tuple-element.30.q_own, bf16[144,512]{1,0:T(8,128)(2,1)S(1)} %collective-permute-done.q_par, ...), custom_call_target="tpu_custom_call" | custom-call | tf_op jit(solution)/shard_map/patch_gradients/pallas_call | solution.py:305
  33.5 0.4 weight_terms_kept.1
  34.0 0.0 collective-permute-done.9.att_back
  34.0 0.0 collective-permute-done.8
  34.0 0.0 copy-start
  34.0 0.1 convert_add_fusion
  34.1 1.3 %collective-permute-start.14 = (bf16[64,1024]{1,0:T(8,128)(2,1)S(1)}, bf16[64,1024]{1,0:T(8,128)(2,1)S(1)}, u32[]{:S(2)}, u32[]{:S(2)}) collective-permute-start(bf16[64,1024]{1,0:T(8,128)(2,1)S(1)} %slice.35), channel_id=1, source_target_pairs={{0,8},{4,12},{8,0},{12,4},{16,24},{20,28},{24,16},{28,20},{1,9},{5... | collective-permute-start | bytes 393224 | tf_op jit(solution)/shard_map/ppermute | solution.py:474
  35.4 1.1 %collective-permute-start.10 = (bf16[128,512]{1,0:T(8,128)(2,1)S(1)}, bf16[128,512]{1,0:T(8,128)(2,1)S(1)}, u32[]{:S(2)}, u32[]{:S(2)}) collective-permute-start(bf16[128,512]{1,0:T(8,128)(2,1)S(1)} %get-tuple-element.43), channel_id=1, source_target_pairs={{0,4},{4,0},{8,12},{12,8},{16,20},{20,16},{24,28},{28,24},{1,5},{5... | collective-permute-start | bytes 393224 | tf_op jit(solution)/shard_map/ppermute | solution.py:436
  36.5 3.6 %collective-permute-done.12.far_b = bf16[256,512]{1,0:T(8,128)(2,1)S(1)} collective-permute-done((bf16[256,512]{1,0:T(8,128)(2,1)S(1)}, bf16[256,512]{1,0:T(8,128)(2,1)S(1)}, u32[]{:S(2)}, u32[]{:S(2)}) %collective-permute-start.12) | collective-permute-done | bytes 262176 | tf_op jit(solution)/shard_map/ppermute | solution.py:436
  40.1 0.0 collective-permute-done.11.far_a
  40.1 0.1 add_returned.1
  40.2 0.8 %collective-permute-start.13 = (bf16[256,512]{1,0:T(8,128)(2,1)S(1)}, bf16[256,512]{1,0:T(8,128)(2,1)S(1)}, u32[]{:S(2)}, u32[]{:S(2)}) collective-permute-start(bf16[256,512]{1,0:T(8,128)(2,1)S(1)} %add_returned.1), channel_id=1, source_target_pairs={{0,4},{4,0},{8,12},{12,8},{16,20},{20,16},{24,28},{28,24},{1,5},{5... | collective-permute-start | bytes 786440 | tf_op jit(solution)/shard_map/ppermute | solution.py:436
  41.0 0.6 %collective-permute-done.14 = bf16[64,1024]{1,0:T(8,128)(2,1)S(1)} collective-permute-done((bf16[64,1024]{1,0:T(8,128)(2,1)S(1)}, bf16[64,1024]{1,0:T(8,128)(2,1)S(1)}, u32[]{:S(2)}, u32[]{:S(2)}) %collective-permute-start.14) | collective-permute-done | bytes 131104 | tf_op jit(solution)/shard_map/ppermute | solution.py:474
  41.6 1.7 %collective-permute-start.15 = (bf16[32,1024]{1,0:T(8,128)(2,1)S(1)}, bf16[32,1024]{1,0:T(8,128)(2,1)S(1)}, u32[]{:S(2)}, u32[]{:S(2)}) collective-permute-start(bf16[32,1024]{1,0:T(8,128)(2,1)S(1)} %slice.36), channel_id=1, source_target_pairs={{0,16},{4,20},{8,24},{12,28},{16,0},{20,4},{24,8},{28,12},{1,17},{... | collective-permute-start | bytes 196616 | tf_op jit(solution)/shard_map/ppermute | solution.py:474
  43.3 0.9 %finish_own_heads.1 = (bf16[128,1024]{1,0:T(8,128)(2,1)}, bf16[128,1024]{1,0:T(8,128)(2,1)}) custom-call(bf16[256,512]{1,0:T(8,128)(2,1)S(1)} %get-tuple-element.46.own, bf16[256,512]{1,0:T(8,128)(2,1)S(1)} %collective-permute-done.11.far_a, bf16[256,512]{1,0:T(8,128)(2,1)S(1)} %collective-permute-done.12.far_b), custom_call_target="tpu_custom_call" | custom-call | tf_op jit(solution)/shard_map/finish_own_heads/pallas_call | solution.py:401
  44.2 0.0 collective-permute-done.10.dq_back
  44.2 0.0 copy-done
  44.2 1.2 %finish_queries.1 = (bf16[128,1024]{1,0:T(8,128)(2,1)}, bf16[128,1024]{1,0:T(8,128)(2,1)}) custom-call(bf16[128,512]{1,0:T(8,128)(2,1)S(1)} %get-tuple-element.34.att_own, bf16[128,512]{1,0:T(8,128)(2,1)S(1)} %collective-permute-done.9.att_back, bf16[128,512]{1,0:T(8,128)(2,1)S(1)} %get-tuple-element.42.dq_own, ...), custom_call_target="tpu_custom_call" | custom-call | tf_op jit(solution)/shard_map/finish_queries/pallas_call | solution.py:344
  45.4 1.2 %collective-permute-done.13.home = bf16[256,512]{1,0:T(8,128)(2,1)S(1)} collective-permute-done((bf16[256,512]{1,0:T(8,128)(2,1)S(1)}, bf16[256,512]{1,0:T(8,128)(2,1)S(1)}, u32[]{:S(2)}, u32[]{:S(2)}) %collective-permute-start.13) | collective-permute-done | bytes 262176 | tf_op jit(solution)/shard_map/ppermute | solution.py:436
  46.6 0.2 collective-permute-done.15.out
  46.9 1.4 %finish_home_heads.1 = (bf16[128,1024]{1,0:T(8,128)(2,1)}, bf16[128,1024]{1,0:T(8,128)(2,1)}, f32[32,1024]{1,0:T(8,128)}) custom-call(bf16[128,1024]{1,0:T(8,128)(2,1)} %get-tuple-element.48._dk, bf16[128,1024]{1,0:T(8,128)(2,1)} %get-tuple-element.49._dv, ...), custom_call_target="tpu_custom_call", output_to_operand_aliasing={{0}: (0, {}), {1}: (1, {})} | custom-call | tf_op jit(solution)/shard_map/finish_home_heads/pallas_call | solution.py:410
  (5 shorter events, 0.1 us)
Async XLA Ops:
  2.0 10.2 %collective-permute-start.1 = (bf16[256,512]{1,0:T(8,128)(2,1)S(1)}, bf16[256,512]{1,0:T(8,128)(2,1)S(1)}, u32[]{:S(2)}, u32[]{:S(2)}) collective-permute-start(bf16[256,512]{1,0:T(8,128)(2,1)S(1)} %get-tuple-element.33), channel_id=1, source_target_pairs={{0,4},{4,0},{8,12},{12,8},{16,20},{20,16},{24,28},{28,24},{1,5},{5... | collective-permute-start | bytes 786440 | tf_op jit(solution)/shard_map/ppermute | solution.py:436
  5.0 12.4 %collective-permute-start.4 = (bf16[128,1024]{1,0:T(8,128)(2,1)}, bf16[128,1024]{1,0:T(8,128)(2,1)S(1)}, u32[]{:S(2)}, u32[]{:S(2)}) collective-permute-start(bf16[128,1024]{1,0:T(8,128)(2,1)} %bitcast.13), channel_id=1, source_target_pairs={{0,4},{4,0},{8,12},{12,8},{16,20},{20,16},{24,28},{28,24},{1,5},{5... | collective-permute-start | bytes 786440 | tf_op jit(solution)/shard_map/ppermute | solution.py:436
  5.1 16.3 %collective-permute-start.3 = (bf16[256,512]{1,0:T(8,128)(2,1)S(1)}, bf16[256,512]{1,0:T(8,128)(2,1)S(1)}, u32[]{:S(2)}, u32[]{:S(2)}) collective-permute-start(bf16[256,512]{1,0:T(8,128)(2,1)S(1)} %get-tuple-element.32.own), channel_id=1, source_target_pairs={{8,0},{16,8},{24,16},{4,12},{12,20},{20,28},{9,1},{17,9},{25,17},{... | collective-permute-start | bytes 786440 | tf_op jit(solution)/shard_map/ppermute | solution.py:436
  12.1 9.2 %collective-permute-start.2 = (bf16[256,512]{1,0:T(8,128)(2,1)S(1)}, bf16[256,512]{1,0:T(8,128)(2,1)S(1)}, u32[]{:S(2)}, u32[]{:S(2)}) collective-permute-start(bf16[256,512]{1,0:T(8,128)(2,1)S(1)} %collective-permute-done.1.par), channel_id=1, source_target_pairs={{0,8},{8,16},{16,24},{12,4},{20,12},{28,20},{1,9},{9,17},{17,25},{... | collective-permute-start | bytes 786440 | tf_op jit(solution)/shard_map/ppermute | solution.py:436
  16.2 5.2 %collective-permute-start = (bf16[144,512]{1,0:T(8,128)(2,1)S(1)}, bf16[144,512]{1,0:T(8,128)(2,1)S(1)}, u32[]{:S(2)}, u32[]{:S(2)}) collective-permute-start(bf16[144,512]{1,0:T(8,128)(2,1)S(1)} %get-tuple-element.31), channel_id=1, source_target_pairs={{0,4},{4,0},{8,12},{12,8},{16,20},{20,16},{24,28},{28,24},{1,5},{5... | collective-permute-start | bytes 442376 | tf_op jit(solution)/shard_map/ppermute | solution.py:436
  16.3 8.2 %collective-permute-start.6 = (bf16[128,1024]{1,0:T(8,128)(2,1)}, bf16[128,1024]{1,0:T(8,128)(2,1)S(1)}, u32[]{:S(2)}, u32[]{:S(2)}) collective-permute-start(bf16[128,1024]{1,0:T(8,128)(2,1)} %bitcast.14), channel_id=1, source_target_pairs={{0,1},{1,0},{2,3},{3,2},{4,5},{5,4},{6,7},{7,6},{8,9},{9,8},{10,11... | collective-permute-start | bytes 786440 | tf_op jit(solution)/shard_map/ppermute | solution.py:437
  17.4 7.0 %collective-permute-start.7 = (bf16[128,1024]{1,0:T(8,128)(2,1)S(1)}, bf16[128,1024]{1,0:T(8,128)(2,1)S(1)}, u32[]{:S(2)}, u32[]{:S(2)}) collective-permute-start(bf16[128,1024]{1,0:T(8,128)(2,1)S(1)} %collective-permute-done.4.cot_par.par), channel_id=1, source_target_pairs={{0,1},{1,0},{2,3},{3,2},{4,5},{5,4},{6,7},{7,6},{8,9},{9,8},{10,11... | collective-permute-start | bytes 786440 | tf_op jit(solution)/shard_map/ppermute | solution.py:437
  21.4 3.1 %copy-start.1 = (bf16[1,128,1024]{2,1,0:T(8,128)(2,1)S(1)}, bf16[1,128,1024]{2,1,0:T(8,128)(2,1)}, u32[]{:S(2)}) copy-start(bf16[1,128,1024]{2,1,0:T(8,128)(2,1)} %param.11) | copy-start | bytes 786436
  23.0 1.5 %collective-permute-start.5 = (bf16[256,256]{1,0:T(8,128)(2,1)S(1)}, bf16[256,256]{1,0:T(8,128)(2,1)S(1)}, u32[]{:S(2)}, u32[]{:S(2)}) collective-permute-start(bf16[256,256]{1,0:T(8,128)(2,1)S(1)} %get-tuple-element.55), channel_id=1, source_target_pairs={{0,1},{1,0},{2,3},{3,2},{4,5},{5,4},{6,7},{7,6},{8,9},{9,8},{10,11... | collective-permute-start | bytes 393224 | tf_op jit(solution)/shard_map/ppermute | solution.py:437
  24.9 9.1 %collective-permute-start.8 = (bf16[128,1024]{1,0:T(8,128)(2,1)S(1)}, bf16[128,1024]{1,0:T(8,128)(2,1)S(1)}, u32[]{:S(2)}, u32[]{:S(2)}) collective-permute-start(bf16[128,1024]{1,0:T(8,128)(2,1)S(1)} %weight_terms_sent.1._after), channel_id=1, source_target_pairs={{0,2},{1,3},{2,0},{3,1},{4,6},{5,7},{6,4},{7,5},{8,10},{9,11},{10,... | collective-permute-start | bytes 786440 | tf_op jit(solution)/shard_map/ppermute | solution.py:474
  26.5 7.5 %collective-permute-start.9 = (bf16[128,512]{1,0:T(8,128)(2,1)S(1)}, bf16[128,512]{1,0:T(8,128)(2,1)S(1)}, u32[]{:S(2)}, u32[]{:S(2)}) collective-permute-start(bf16[128,512]{1,0:T(8,128)(2,1)S(1)} %get-tuple-element.40), channel_id=1, source_target_pairs={{0,4},{4,0},{8,12},{12,8},{16,20},{20,16},{24,28},{28,24},{1,5},{5... | collective-permute-start | bytes 393224 | tf_op jit(solution)/shard_map/ppermute | solution.py:436
  27.8 12.3 %collective-permute-start.11 = (bf16[256,512]{1,0:T(8,128)(2,1)S(1)}, bf16[256,512]{1,0:T(8,128)(2,1)S(1)}, u32[]{:S(2)}, u32[]{:S(2)}) collective-permute-start(bf16[256,512]{1,0:T(8,128)(2,1)S(1)} %get-tuple-element.37._after), channel_id=1, source_target_pairs={{8,16},{12,20},{16,8},{20,12},{9,17},{13,21},{17,9},{21,13},{10,18... | collective-permute-start | bytes 786440 | tf_op jit(solution)/shard_map/ppermute | solution.py:436
  28.4 11.6 %collective-permute-start.12 = (bf16[256,512]{1,0:T(8,128)(2,1)S(1)}, bf16[256,512]{1,0:T(8,128)(2,1)S(1)}, u32[]{:S(2)}, u32[]{:S(2)}) collective-permute-start(bf16[256,512]{1,0:T(8,128)(2,1)S(1)} %get-tuple-element.47), channel_id=1, source_target_pairs={{0,8},{4,12},{8,0},{12,4},{16,24},{20,28},{24,16},{28,20},{1,9},{5... | collective-permute-start | bytes 786440 | tf_op jit(solution)/shard_map/ppermute | solution.py:436
  34.0 10.2 %copy-start = (bf16[1024,1024]{1,0:T(8,128)(2,1)S(1)}, bf16[1024,1024]{1,0:T(8,128)(2,1)}, u32[]{:S(2)}) copy-start(bf16[1024,1024]{1,0:T(8,128)(2,1)} %w.3) | copy-start | bytes 6291460
  34.1 7.5 %collective-permute-start.14 = (bf16[64,1024]{1,0:T(8,128)(2,1)S(1)}, bf16[64,1024]{1,0:T(8,128)(2,1)S(1)}, u32[]{:S(2)}, u32[]{:S(2)}) collective-permute-start(bf16[64,1024]{1,0:T(8,128)(2,1)S(1)} %slice.35), channel_id=1, source_target_pairs={{0,8},{4,12},{8,0},{12,4},{16,24},{20,28},{24,16},{28,20},{1,9},{5... | collective-permute-start | bytes 393224 | tf_op jit(solution)/shard_map/ppermute | solution.py:474
  35.4 8.8 %collective-permute-start.10 = (bf16[128,512]{1,0:T(8,128)(2,1)S(1)}, bf16[128,512]{1,0:T(8,128)(2,1)S(1)}, u32[]{:S(2)}, u32[]{:S(2)}) collective-permute-start(bf16[128,512]{1,0:T(8,128)(2,1)S(1)} %get-tuple-element.43), channel_id=1, source_target_pairs={{0,4},{4,0},{8,12},{12,8},{16,20},{20,16},{24,28},{28,24},{1,5},{5... | collective-permute-start | bytes 393224 | tf_op jit(solution)/shard_map/ppermute | solution.py:436
  40.2 6.4 %collective-permute-start.13 = (bf16[256,512]{1,0:T(8,128)(2,1)S(1)}, bf16[256,512]{1,0:T(8,128)(2,1)S(1)}, u32[]{:S(2)}, u32[]{:S(2)}) collective-permute-start(bf16[256,512]{1,0:T(8,128)(2,1)S(1)} %add_returned.1), channel_id=1, source_target_pairs={{0,4},{4,0},{8,12},{12,8},{16,20},{20,16},{24,28},{28,24},{1,5},{5... | collective-permute-start | bytes 786440 | tf_op jit(solution)/shard_map/ppermute | solution.py:436
  41.6 5.2 %collective-permute-start.15 = (bf16[32,1024]{1,0:T(8,128)(2,1)S(1)}, bf16[32,1024]{1,0:T(8,128)(2,1)S(1)}, u32[]{:S(2)}, u32[]{:S(2)}) collective-permute-start(bf16[32,1024]{1,0:T(8,128)(2,1)S(1)} %slice.36), channel_id=1, source_target_pairs={{0,16},{4,20},{8,24},{12,28},{16,0},{20,4},{24,8},{28,12},{1,17},{... | collective-permute-start | bytes 196616 | tf_op jit(solution)/shard_map/ppermute | solution.py:474

commit v4 on v2

--- a/solution.py
+++ b/solution.py
@@ -440,7 +440,7 @@
     for place, (axis, count, bit) in enumerate(hops):
         out = lax.ppermute(out, axis, [(i, i ^ bit) for i in range(count)])
         if place == 0:
-            out, d_own, att_back = lax.optimization_barrier((out, d_own, att_back))
+            out, d_own = lax.optimization_barrier((out, d_own))
         if place + 1 < len(hops):
             total = keep + out.astype(F32)
             rows = total.shape[0] // 2

time: 48.1 us -> 49.9 us (1.037)
  waiting for transfers between devices: 15.1 us -> 16.3 us
  starting transfers between devices: 21.4 us -> 22 us
    ppermute x3, waiting for transfers between devices: 0.88 us -> 1.6 us  [on_device(): out = lax.ppermute(out, axis, [(i, i ^ bit) for i in range(count)])]
    ppermute x10, waiting for transfers between devices: 14.2 us -> 14.7 us  [on_device(): send = lambda x, pairs: lax.ppermute(x, 'seq', pairs)]
  transfers between devices with their start and end apart: 16 -> 16, of which waited for: 7 -> 8; matrix products, arithmetic and copies ran while one was open for 0% -> 0% of each run, Pallas kernels for 16% -> 15%
where the time goes in v4:
time: 49.9 us; the launch traced here: 49.6 us
  starting transfers between devices  22 us (44%)
  waiting for transfers between devices  16.3 us (33%)
  Pallas kernels  10.3 us (21%)
  between operations  0.83 us (2%)
    ppermute x10, starting transfers between devices, on_device(): send = lambda x, pairs: lax.ppermute(x, 'seq', pairs)  17 us
    ppermute x10, waiting for transfers between devices, on_device(): send = lambda x, pairs: lax.ppermute(x, 'seq', pairs)  14.7 us
    ppermute x3, starting transfers between devices, on_device(): out = lax.ppermute(out, axis, [(i, i ^ bit) for i in range(count)])  4.87 us
    pallas_call x1, Pallas kernels, grad_attended(): call(turn_kernel, (shape_of(2 * tokens, pairs * HD),), [HBM, VMEM, HBM],...  2.32 us
    ppermute x3, waiting for transfers between devices, on_device(): out = lax.ppermute(out, axis, [(i, i ^ bit) for i in range(count)])  1.6 us
    pallas_call x1, Pallas kernels, forward(): call(functools.partial(forward_kernel, direct, n_dp), (shape_of(pairs, 3...  1.59 us
    pallas_call x1, Pallas kernels, backward(): call(backward_kernel, (shape_of(*probs.shape),) + (shape_of(2 * tokens, h...  1.35 us
    pallas_call x1, Pallas kernels, pack(): call(pack_kernel, (kv, kv) + (shape_of(tokens + FLAG_ROWS, half),) * 2, [...  1.34 us
  transfers between devices with their start and end apart: 16, of which 8 were waited for; matrix products, arithmetic and copies ran while one was open for 0% of the time, Pallas kernels for 15%

profile of v4, /device:TPU:0, one launch (start us, length us, event | category | flops | bytes accessed | tf_op | source)
XLA Modules:
  0.0 49.6 jit_solution(7846775465580987824)
XLA Ops:
  0.6 1.3 %pack_heads.1 = (bf16[256,512]{1,0:T(8,128)(2,1)S(1)}, bf16[256,512]{1,0:T(8,128)(2,1)S(1)}, bf16[144,512]{1,0:T(8,128)(2,1)S(1)}, bf16[144,512]{1,0:T(8,128)(2,1)S(1)}) custom-call(s32[1,2]{1,0:T(1,128)} %bitcast.21, bf16[128,1024]{1,0:T(8,128)(2,1)} %bitcast.18, bf16[128,1024]{1,0:T(8,128)(2,1)} %bitcast.19, bf16[128,1024]{1,0:T(8,128)(2,1)} %bitcast.20), custom_call_target="tpu_custom_call" | custom-call | tf_op jit(solution)/shard_map/pack_heads/pallas_call | solution.py:97
  2.0 3.0 %collective-permute-start.1 = (bf16[256,512]{1,0:T(8,128)(2,1)S(1)}, bf16[256,512]{1,0:T(8,128)(2,1)S(1)}, u32[]{:S(2)}, u32[]{:S(2)}) collective-permute-start(bf16[256,512]{1,0:T(8,128)(2,1)S(1)} %get-tuple-element.30), channel_id=1, source_target_pairs={{0,4},{4,0},{8,12},{12,8},{16,20},{20,16},{24,28},{28,24},{1,5},{5... | collective-permute-start | bytes 786440 | tf_op jit(solution)/shard_map/ppermute | solution.py:403
  5.0 0.1 collective-permute-start.4
  5.1 1.3 %collective-permute-start.3 = (bf16[256,512]{1,0:T(8,128)(2,1)S(1)}, bf16[256,512]{1,0:T(8,128)(2,1)S(1)}, u32[]{:S(2)}, u32[]{:S(2)}) collective-permute-start(bf16[256,512]{1,0:T(8,128)(2,1)S(1)} %get-tuple-element.29.own), channel_id=1, source_target_pairs={{8,0},{16,8},{24,16},{4,12},{12,20},{20,28},{9,1},{17,9},{25,17},{... | collective-permute-start | bytes 786440 | tf_op jit(solution)/shard_map/ppermute | solution.py:403
  6.4 5.8 %collective-permute-done.1.par = bf16[256,512]{1,0:T(8,128)(2,1)S(1)} collective-permute-done((bf16[256,512]{1,0:T(8,128)(2,1)S(1)}, bf16[256,512]{1,0:T(8,128)(2,1)S(1)}, u32[]{:S(2)}, u32[]{:S(2)}) %collective-permute-start.1) | collective-permute-done | bytes 262176 | tf_op jit(solution)/shard_map/ppermute | solution.py:403
  12.1 4.0 %collective-permute-start.2 = (bf16[256,512]{1,0:T(8,128)(2,1)S(1)}, bf16[256,512]{1,0:T(8,128)(2,1)S(1)}, u32[]{:S(2)}, u32[]{:S(2)}) collective-permute-start(bf16[256,512]{1,0:T(8,128)(2,1)S(1)} %collective-permute-done.1.par), channel_id=1, source_target_pairs={{0,8},{8,16},{16,24},{12,4},{20,12},{28,20},{1,9},{9,17},{17,25},{... | collective-permute-start | bytes 786440 | tf_op jit(solution)/shard_map/ppermute | solution.py:403
  16.2 0.1 collective-permute-start
  16.3 0.1 collective-permute-start.8
  16.3 1.1 %collective-permute-done.4.cot_par.par = bf16[128,1024]{1,0:T(8,128)(2,1)S(1)} collective-permute-done((bf16[128,1024]{1,0:T(8,128)(2,1)}, bf16[128,1024]{1,0:T(8,128)(2,1)S(1)}, u32[]{:S(2)}, u32[]{:S(2)}) %collective-permute-start.4) | collective-permute-done | bytes 262176 | tf_op jit(solution)/shard_map/ppermute | solution.py:403
  17.4 0.0 collective-permute-start.9
  17.4 2.3 %grad_attended.1.after.ga = bf16[256,512]{1,0:T(8,128)(2,1)S(1)} custom-call(bf16[128,1024]{1,0:T(8,128)(2,1)} %bitcast.15, bf16[128,1024]{1,0:T(8,128)(2,1)S(1)} %collective-permute-done.4.cot_par.par, bf16[1024,1024]{1,0:T(8,128)(2,1)} %w.3), custom_call_target="tpu_custom_call" | custom-call | tf_op jit(solution)/shard_map/grad_attended/pallas_call | solution.py:129
  19.8 1.6 %collective-permute-done.q_par = bf16[144,512]{1,0:T(8,128)(2,1)S(1)} collective-permute-done((bf16[144,512]{1,0:T(8,128)(2,1)S(1)}, bf16[144,512]{1,0:T(8,128)(2,1)S(1)}, u32[]{:S(2)}, u32[]{:S(2)}) %collective-permute-start) | collective-permute-done | bytes 147488 | tf_op jit(solution)/shard_map/ppermute | solution.py:403
  21.4 0.0 collective-permute-done.3.far_par
  21.4 0.0 collective-permute-done.2.far_own
  21.4 0.0 copy-start.1
  21.4 1.6 %patch_forward.1 = (bf16[4,384,256]{2,1,0:T(8,128)(2,1)S(1)}, bf16[128,512]{1,0:T(8,128)(2,1)S(1)}, bf16[128,512]{1,0:T(8,128)(2,1)S(1)}, bf16[2,256,256]{2,1,0:T(8,128)(2,1)S(1)}) custom-call(bf16[144,512]{1,0:T(8,128)(2,1)S(1)} %get-tuple-element.27.q_own, bf16[144,512]{1,0:T(8,128)(2,1)S(1)} %collective-permute-done.q_par, ...), custom_call_target="tpu_custom_call" | custom-call | tf_op jit(solution)/shard_map/patch_forward/pallas_call | solution.py:209
  23.0 0.1 collective-permute-start.7
  23.1 1.4 %patch_backward.1 = (bf16[4,384,256]{2,1,0:T(8,128)(2,1)S(1)}, bf16[256,512]{1,0:T(8,128)(2,1)S(1)}, bf16[256,512]{1,0:T(8,128)(2,1)S(1)}) custom-call(bf16[144,512]{1,0:T(8,128)(2,1)S(1)} %get-tuple-element.27.q_own, bf16[144,512]{1,0:T(8,128)(2,1)S(1)} %collective-permute-done.q_par, bf16[256,512]{1,0:T(8,128)(2,1)S(1)} %get-tuple-element.29.own, ...), custom_call_target="tpu_custom_call" | custom-call | tf_op jit(solution)/shard_map/patch_backward/pallas_call | solution.py:269
  24.5 0.0 collective-permute-done.8.core_own
  24.5 0.0 collective-permute-done.9.core_par
  24.5 0.0 collective-permute-done.7.att_core
  24.5 0.0 copy-done.1
  24.5 0.4 weight_terms_sent.1._after
  24.9 1.6 %collective-permute-start.10 = (bf16[128,1024]{1,0:T(8,128)(2,1)S(1)}, bf16[128,1024]{1,0:T(8,128)(2,1)S(1)}, u32[]{:S(2)}, u32[]{:S(2)}) collective-permute-start(bf16[128,1024]{1,0:T(8,128)(2,1)S(1)} %weight_terms_sent.1._after), channel_id=1, source_target_pairs={{0,2},{1,3},{2,0},{3,1},{4,6},{5,7},{6,4},{7,5},{8,10},{9,11},{10,... | collective-permute-start | bytes 786440 | tf_op jit(solution)/shard_map/ppermute | solution.py:441
  26.5 0.7 %collective-permute-start.11 = (bf16[256,512]{1,0:T(8,128)(2,1)S(1)}, bf16[256,512]{1,0:T(8,128)(2,1)S(1)}, u32[]{:S(2)}, u32[]{:S(2)}) collective-permute-start(bf16[256,512]{1,0:T(8,128)(2,1)S(1)} %get-tuple-element.40._after), channel_id=1, source_target_pairs={{8,16},{12,20},{16,8},{20,12},{9,17},{13,21},{17,9},{21,13},{10,18... | collective-permute-start | bytes 786440 | tf_op jit(solution)/shard_map/ppermute | solution.py:403
  27.2 4.4 %collective-permute-start.12 = (bf16[256,512]{1,0:T(8,128)(2,1)S(1)}, bf16[256,512]{1,0:T(8,128)(2,1)S(1)}, u32[]{:S(2)}, u32[]{:S(2)}) collective-permute-start(bf16[256,512]{1,0:T(8,128)(2,1)S(1)} %get-tuple-element.43), channel_id=1, source_target_pairs={{0,8},{4,12},{8,0},{12,4},{16,24},{20,28},{24,16},{28,20},{1,9},{5... | collective-permute-start | bytes 786440 | tf_op jit(solution)/shard_map/ppermute | solution.py:403
  31.6 0.7 %patch_gradients.1 = (bf16[128,512]{1,0:T(8,128)(2,1)S(1)}, bf16[128,512]{1,0:T(8,128)(2,1)S(1)}, bf16[256,512]{1,0:T(8,128)(2,1)S(1)}, bf16[256,512]{1,0:T(8,128)(2,1)S(1)}) custom-call(bf16[144,512]{1,0:T(8,128)(2,1)S(1)} %get-tuple-element.27.q_own, bf16[144,512]{1,0:T(8,128)(2,1)S(1)} %collective-permute-done.q_par, ...), custom_call_target="tpu_custom_call" | custom-call | tf_op jit(solution)/shard_map/patch_gradients/pallas_call | solution.py:305
  32.2 0.4 weight_terms_kept.1
  32.7 0.0 copy-start
  32.7 1.0 %collective-permute-done.10 = bf16[128,1024]{1,0:T(8,128)(2,1)S(1)} collective-permute-done((bf16[128,1024]{1,0:T(8,128)(2,1)S(1)}, bf16[128,1024]{1,0:T(8,128)(2,1)S(1)}, u32[]{:S(2)}, u32[]{:S(2)}) %collective-permute-start.10) | collective-permute-done | bytes 262176 | tf_op jit(solution)/shard_map/ppermute | solution.py:441
  33.7 0.1 convert_add_fusion
  33.8 1.6 %collective-permute-start.14 = (bf16[64,1024]{1,0:T(8,128)(2,1)S(1)}, bf16[64,1024]{1,0:T(8,128)(2,1)S(1)}, u32[]{:S(2)}, u32[]{:S(2)}) collective-permute-start(bf16[64,1024]{1,0:T(8,128)(2,1)S(1)} %slice.35), channel_id=1, source_target_pairs={{0,8},{4,12},{8,0},{12,4},{16,24},{20,28},{24,16},{28,20},{1,9},{5... | collective-permute-start | bytes 393224 | tf_op jit(solution)/shard_map/ppermute | solution.py:441
  35.4 1.1 %collective-permute-start.5 = (bf16[128,512]{1,0:T(8,128)(2,1)S(1)}, bf16[128,512]{1,0:T(8,128)(2,1)S(1)}, u32[]{:S(2)}, u32[]{:S(2)}) collective-permute-start(bf16[128,512]{1,0:T(8,128)(2,1)S(1)} %get-tuple-element.32), channel_id=1, source_target_pairs={{0,4},{4,0},{8,12},{12,8},{16,20},{20,16},{24,28},{28,24},{1,5},{5... | collective-permute-start | bytes 393224 | tf_op jit(solution)/shard_map/ppermute | solution.py:403
  36.5 1.0 %collective-permute-start.6 = (bf16[128,512]{1,0:T(8,128)(2,1)S(1)}, bf16[128,512]{1,0:T(8,128)(2,1)S(1)}, u32[]{:S(2)}, u32[]{:S(2)}) collective-permute-start(bf16[128,512]{1,0:T(8,128)(2,1)S(1)} %get-tuple-element.36), channel_id=1, source_target_pairs={{0,4},{4,0},{8,12},{12,8},{16,20},{20,16},{24,28},{28,24},{1,5},{5... | collective-permute-start | bytes 393224 | tf_op jit(solution)/shard_map/ppermute | solution.py:403
  37.4 0.0 collective-permute-done.11.far_a
  37.4 1.3 %collective-permute-done.12.far_b = bf16[256,512]{1,0:T(8,128)(2,1)S(1)} collective-permute-done((bf16[256,512]{1,0:T(8,128)(2,1)S(1)}, bf16[256,512]{1,0:T(8,128)(2,1)S(1)}, u32[]{:S(2)}, u32[]{:S(2)}) %collective-permute-start.12) | collective-permute-done | bytes 262176 | tf_op jit(solution)/shard_map/ppermute | solution.py:403
  38.7 0.1 add_returned.1
  38.8 1.4 %collective-permute-start.13 = (bf16[256,512]{1,0:T(8,128)(2,1)S(1)}, bf16[256,512]{1,0:T(8,128)(2,1)S(1)}, u32[]{:S(2)}, u32[]{:S(2)}) collective-permute-start(bf16[256,512]{1,0:T(8,128)(2,1)S(1)} %add_returned.1), channel_id=1, source_target_pairs={{0,4},{4,0},{8,12},{12,8},{16,20},{20,16},{24,28},{28,24},{1,5},{5... | collective-permute-start | bytes 786440 | tf_op jit(solution)/shard_map/ppermute | solution.py:403
  40.2 0.6 %collective-permute-done.14 = bf16[64,1024]{1,0:T(8,128)(2,1)S(1)} collective-permute-done((bf16[64,1024]{1,0:T(8,128)(2,1)S(1)}, bf16[64,1024]{1,0:T(8,128)(2,1)S(1)}, u32[]{:S(2)}, u32[]{:S(2)}) %collective-permute-start.14) | collective-permute-done | bytes 131104 | tf_op jit(solution)/shard_map/ppermute | solution.py:441
  40.8 1.7 %collective-permute-start.15 = (bf16[32,1024]{1,0:T(8,128)(2,1)S(1)}, bf16[32,1024]{1,0:T(8,128)(2,1)S(1)}, u32[]{:S(2)}, u32[]{:S(2)}) collective-permute-start(bf16[32,1024]{1,0:T(8,128)(2,1)S(1)} %slice.36), channel_id=1, source_target_pairs={{0,16},{4,20},{8,24},{12,28},{16,0},{20,4},{24,8},{28,12},{1,17},{... | collective-permute-start | bytes 196616 | tf_op jit(solution)/shard_map/ppermute | solution.py:441
  42.5 0.0 collective-permute-done.5.att_back
  42.5 2.1 %collective-permute-done.6.dq_back = bf16[128,512]{1,0:T(8,128)(2,1)S(1)} collective-permute-done((bf16[128,512]{1,0:T(8,128)(2,1)S(1)}, bf16[128,512]{1,0:T(8,128)(2,1)S(1)}, u32[]{:S(2)}, u32[]{:S(2)}) %collective-permute-start.6) | collective-permute-done | bytes 131104 | tf_op jit(solution)/shard_map/ppermute | solution.py:403
  44.6 0.0 copy-done
  44.7 1.2 %finish_queries.1 = (bf16[128,1024]{1,0:T(8,128)(2,1)}, bf16[128,1024]{1,0:T(8,128)(2,1)}) custom-call(bf16[128,512]{1,0:T(8,128)(2,1)S(1)} %get-tuple-element.31.att_own, bf16[128,512]{1,0:T(8,128)(2,1)S(1)} %collective-permute-done.5.att_back, bf16[128,512]{1,0:T(8,128)(2,1)S(1)} %get-tuple-element.35.dq_own, ...), custom_call_target="tpu_custom_call" | custom-call | tf_op jit(solution)/shard_map/finish_queries/pallas_call | solution.py:344
  45.9 2.8 %collective-permute-done.13.home = bf16[256,512]{1,0:T(8,128)(2,1)S(1)} collective-permute-done((bf16[256,512]{1,0:T(8,128)(2,1)S(1)}, bf16[256,512]{1,0:T(8,128)(2,1)S(1)}, u32[]{:S(2)}, u32[]{:S(2)}) %collective-permute-start.13) | collective-permute-done | bytes 262176 | tf_op jit(solution)/shard_map/ppermute | solution.py:403
  48.7 0.0 collective-permute-done.15.out
  48.7 0.9 %finish_keys.1 = (bf16[128,1024]{1,0:T(8,128)(2,1)}, bf16[128,1024]{1,0:T(8,128)(2,1)}, f32[32,1024]{1,0:T(8,128)}) custom-call(bf16[256,512]{1,0:T(8,128)(2,1)S(1)} %get-tuple-element.42.own, bf16[256,512]{1,0:T(8,128)(2,1)S(1)} %collective-permute-done.11.far_a, bf16[256,512]{1,0:T(8,128)(2,1)S(1)} %collective-permute-done.12.far_b, ...), custom_call_target="tpu_custom_call" | custom-call | tf_op jit(solution)/shard_map/finish_keys/pallas_call | solution.py:381
  (5 shorter events, 0.1 us)
Async XLA Ops:
  2.0 10.2 %collective-permute-start.1 = (bf16[256,512]{1,0:T(8,128)(2,1)S(1)}, bf16[256,512]{1,0:T(8,128)(2,1)S(1)}, u32[]{:S(2)}, u32[]{:S(2)}) collective-permute-start(bf16[256,512]{1,0:T(8,128)(2,1)S(1)} %get-tuple-element.30), channel_id=1, source_target_pairs={{0,4},{4,0},{8,12},{12,8},{16,20},{20,16},{24,28},{28,24},{1,5},{5... | collective-permute-start | bytes 786440 | tf_op jit(solution)/shard_map/ppermute | solution.py:403
  5.0 12.4 %collective-permute-start.4 = (bf16[128,1024]{1,0:T(8,128)(2,1)}, bf16[128,1024]{1,0:T(8,128)(2,1)S(1)}, u32[]{:S(2)}, u32[]{:S(2)}) collective-permute-start(bf16[128,1024]{1,0:T(8,128)(2,1)} %bitcast.13), channel_id=1, source_target_pairs={{0,4},{4,0},{8,12},{12,8},{16,20},{20,16},{24,28},{28,24},{1,5},{5... | collective-permute-start | bytes 786440 | tf_op jit(solution)/shard_map/ppermute | solution.py:403
  5.1 16.3 %collective-permute-start.3 = (bf16[256,512]{1,0:T(8,128)(2,1)S(1)}, bf16[256,512]{1,0:T(8,128)(2,1)S(1)}, u32[]{:S(2)}, u32[]{:S(2)}) collective-permute-start(bf16[256,512]{1,0:T(8,128)(2,1)S(1)} %get-tuple-element.29.own), channel_id=1, source_target_pairs={{8,0},{16,8},{24,16},{4,12},{12,20},{20,28},{9,1},{17,9},{25,17},{... | collective-permute-start | bytes 786440 | tf_op jit(solution)/shard_map/ppermute | solution.py:403
  12.1 9.2 %collective-permute-start.2 = (bf16[256,512]{1,0:T(8,128)(2,1)S(1)}, bf16[256,512]{1,0:T(8,128)(2,1)S(1)}, u32[]{:S(2)}, u32[]{:S(2)}) collective-permute-start(bf16[256,512]{1,0:T(8,128)(2,1)S(1)} %collective-permute-done.1.par), channel_id=1, source_target_pairs={{0,8},{8,16},{16,24},{12,4},{20,12},{28,20},{1,9},{9,17},{17,25},{... | collective-permute-start | bytes 786440 | tf_op jit(solution)/shard_map/ppermute | solution.py:403
  16.2 5.2 %collective-permute-start = (bf16[144,512]{1,0:T(8,128)(2,1)S(1)}, bf16[144,512]{1,0:T(8,128)(2,1)S(1)}, u32[]{:S(2)}, u32[]{:S(2)}) collective-permute-start(bf16[144,512]{1,0:T(8,128)(2,1)S(1)} %get-tuple-element.28), channel_id=1, source_target_pairs={{0,4},{4,0},{8,12},{12,8},{16,20},{20,16},{24,28},{28,24},{1,5},{5... | collective-permute-start | bytes 442376 | tf_op jit(solution)/shard_map/ppermute | solution.py:403
  16.3 8.2 %collective-permute-start.8 = (bf16[128,1024]{1,0:T(8,128)(2,1)}, bf16[128,1024]{1,0:T(8,128)(2,1)S(1)}, u32[]{:S(2)}, u32[]{:S(2)}) collective-permute-start(bf16[128,1024]{1,0:T(8,128)(2,1)} %bitcast.14), channel_id=1, source_target_pairs={{0,1},{1,0},{2,3},{3,2},{4,5},{5,4},{6,7},{7,6},{8,9},{9,8},{10,11... | collective-permute-start | bytes 786440 | tf_op jit(solution)/shard_map/ppermute | solution.py:404
  17.4 7.0 %collective-permute-start.9 = (bf16[128,1024]{1,0:T(8,128)(2,1)S(1)}, bf16[128,1024]{1,0:T(8,128)(2,1)S(1)}, u32[]{:S(2)}, u32[]{:S(2)}) collective-permute-start(bf16[128,1024]{1,0:T(8,128)(2,1)S(1)} %collective-permute-done.4.cot_par.par), channel_id=1, source_target_pairs={{0,1},{1,0},{2,3},{3,2},{4,5},{5,4},{6,7},{7,6},{8,9},{9,8},{10,11... | collective-permute-start | bytes 786440 | tf_op jit(solution)/shard_map/ppermute | solution.py:404
  21.4 3.1 %copy-start.1 = (bf16[1,128,1024]{2,1,0:T(8,128)(2,1)S(1)}, bf16[1,128,1024]{2,1,0:T(8,128)(2,1)}, u32[]{:S(2)}) copy-start(bf16[1,128,1024]{2,1,0:T(8,128)(2,1)} %param.11) | copy-start | bytes 786436
  23.0 1.5 %collective-permute-start.7 = (bf16[256,256]{1,0:T(8,128)(2,1)S(1)}, bf16[256,256]{1,0:T(8,128)(2,1)S(1)}, u32[]{:S(2)}, u32[]{:S(2)}) collective-permute-start(bf16[256,256]{1,0:T(8,128)(2,1)S(1)} %get-tuple-element.49), channel_id=1, source_target_pairs={{0,1},{1,0},{2,3},{3,2},{4,5},{5,4},{6,7},{7,6},{8,9},{9,8},{10,11... | collective-permute-start | bytes 393224 | tf_op jit(solution)/shard_map/ppermute | solution.py:404
  24.9 8.8 %collective-permute-start.10 = (bf16[128,1024]{1,0:T(8,128)(2,1)S(1)}, bf16[128,1024]{1,0:T(8,128)(2,1)S(1)}, u32[]{:S(2)}, u32[]{:S(2)}) collective-permute-start(bf16[128,1024]{1,0:T(8,128)(2,1)S(1)} %weight_terms_sent.1._after), channel_id=1, source_target_pairs={{0,2},{1,3},{2,0},{3,1},{4,6},{5,7},{6,4},{7,5},{8,10},{9,11},{10,... | collective-permute-start | bytes 786440 | tf_op jit(solution)/shard_map/ppermute | solution.py:441
  26.5 11.0 %collective-permute-start.11 = (bf16[256,512]{1,0:T(8,128)(2,1)S(1)}, bf16[256,512]{1,0:T(8,128)(2,1)S(1)}, u32[]{:S(2)}, u32[]{:S(2)}) collective-permute-start(bf16[256,512]{1,0:T(8,128)(2,1)S(1)} %get-tuple-element.40._after), channel_id=1, source_target_pairs={{8,16},{12,20},{16,8},{20,12},{9,17},{13,21},{17,9},{21,13},{10,18... | collective-permute-start | bytes 786440 | tf_op jit(solution)/shard_map/ppermute | solution.py:403
  27.2 11.6 %collective-permute-start.12 = (bf16[256,512]{1,0:T(8,128)(2,1)S(1)}, bf16[256,512]{1,0:T(8,128)(2,1)S(1)}, u32[]{:S(2)}, u32[]{:S(2)}) collective-permute-start(bf16[256,512]{1,0:T(8,128)(2,1)S(1)} %get-tuple-element.43), channel_id=1, source_target_pairs={{0,8},{4,12},{8,0},{12,4},{16,24},{20,28},{24,16},{28,20},{1,9},{5... | collective-permute-start | bytes 786440 | tf_op jit(solution)/shard_map/ppermute | solution.py:403
  32.7 12.0 %copy-start = (bf16[1024,1024]{1,0:T(8,128)(2,1)S(1)}, bf16[1024,1024]{1,0:T(8,128)(2,1)}, u32[]{:S(2)}) copy-start(bf16[1024,1024]{1,0:T(8,128)(2,1)} %w.3) | copy-start | bytes 6291460
  33.8 7.0 %collective-permute-start.14 = (bf16[64,1024]{1,0:T(8,128)(2,1)S(1)}, bf16[64,1024]{1,0:T(8,128)(2,1)S(1)}, u32[]{:S(2)}, u32[]{:S(2)}) collective-permute-start(bf16[64,1024]{1,0:T(8,128)(2,1)S(1)} %slice.35), channel_id=1, source_target_pairs={{0,8},{4,12},{8,0},{12,4},{16,24},{20,28},{24,16},{28,20},{1,9},{5... | collective-permute-start | bytes 393224 | tf_op jit(solution)/shard_map/ppermute | solution.py:441
  35.4 7.1 %collective-permute-start.5 = (bf16[128,512]{1,0:T(8,128)(2,1)S(1)}, bf16[128,512]{1,0:T(8,128)(2,1)S(1)}, u32[]{:S(2)}, u32[]{:S(2)}) collective-permute-start(bf16[128,512]{1,0:T(8,128)(2,1)S(1)} %get-tuple-element.32), channel_id=1, source_target_pairs={{0,4},{4,0},{8,12},{12,8},{16,20},{20,16},{24,28},{28,24},{1,5},{5... | collective-permute-start | bytes 393224 | tf_op jit(solution)/shard_map/ppermute | solution.py:403
  36.5 8.2 %collective-permute-start.6 = (bf16[128,512]{1,0:T(8,128)(2,1)S(1)}, bf16[128,512]{1,0:T(8,128)(2,1)S(1)}, u32[]{:S(2)}, u32[]{:S(2)}) collective-permute-start(bf16[128,512]{1,0:T(8,128)(2,1)S(1)} %get-tuple-element.36), channel_id=1, source_target_pairs={{0,4},{4,0},{8,12},{12,8},{16,20},{20,16},{24,28},{28,24},{1,5},{5... | collective-permute-start | bytes 393224 | tf_op jit(solution)/shard_map/ppermute | solution.py:403
  38.8 9.9 %collective-permute-start.13 = (bf16[256,512]{1,0:T(8,128)(2,1)S(1)}, bf16[256,512]{1,0:T(8,128)(2,1)S(1)}, u32[]{:S(2)}, u32[]{:S(2)}) collective-permute-start(bf16[256,512]{1,0:T(8,128)(2,1)S(1)} %add_returned.1), channel_id=1, source_target_pairs={{0,4},{4,0},{8,12},{12,8},{16,20},{20,16},{24,28},{28,24},{1,5},{5... | collective-permute-start | bytes 786440 | tf_op jit(solution)/shard_map/ppermute | solution.py:403
  40.8 7.8 %collective-permute-start.15 = (bf16[32,1024]{1,0:T(8,128)(2,1)S(1)}, bf16[32,1024]{1,0:T(8,128)(2,1)S(1)}, u32[]{:S(2)}, u32[]{:S(2)}) collective-permute-start(bf16[32,1024]{1,0:T(8,128)(2,1)S(1)} %slice.36), channel_id=1, source_target_pairs={{0,16},{4,20},{8,24},{12,28},{16,0},{20,4},{24,8},{28,12},{1,17},{... | collective-permute-start | bytes 196616 | tf_op jit(solution)/shard_map/ppermute | solution.py:441

commit v5 on v2

--- a/solution.py
+++ b/solution.py
@@ -184,10 +184,10 @@
         o_t += jnp.concatenate(
             [dot(vfo, low[2][:, :tokens], 0, 0), dot(vfp, low[2][:, tokens:], 0, 0)], axis=1
         )
-        o = o_t.T.astype(BF16)
+        o_low = o_t.astype(BF16)
+        o = o_low.T
         att_own[:, cols] = o[:tokens]
         att_back[:, cols] = o[tokens:]
-        o_low = o_t.astype(BF16)
         if direct:
             rows = HD // n_dp
             place = bit_reversed(j ^ (me >> 1), (pairs - 1).bit_length())

time: 48.1 us -> 48.1 us (level)
  no operation moved by 1% of the time
where the time goes in v5:
time: 48.1 us; the launch traced here: 47.8 us
  starting transfers between devices  21.4 us (44%)
  waiting for transfers between devices  15.1 us (31%)
  Pallas kernels  10.3 us (21%)
  between operations  0.85 us (2%)
    ppermute x10, starting transfers between devices, on_device(): send = lambda x, pairs: lax.ppermute(x, 'seq', pairs)  16.7 us
    ppermute x10, waiting for transfers between devices, on_device(): send = lambda x, pairs: lax.ppermute(x, 'seq', pairs)  14.2 us
    ppermute x3, starting transfers between devices, on_device(): out = lax.ppermute(out, axis, [(i, i ^ bit) for i in range(count)])  4.57 us
    pallas_call x1, Pallas kernels, grad_attended(): call(turn_kernel, (shape_of(2 * tokens, pairs * HD),), [HBM, VMEM, HBM],...  2.32 us
    pallas_call x1, Pallas kernels, forward(): call(functools.partial(forward_kernel, direct, n_dp), (shape_of(pairs, 3...  1.57 us
    pallas_call x1, Pallas kernels, backward(): call(backward_kernel, (shape_of(*probs.shape),) + (shape_of(2 * tokens, h...  1.35 us
    pallas_call x1, Pallas kernels, pack(): call(pack_kernel, (kv, kv) + (shape_of(tokens + FLAG_ROWS, half),) * 2, [...  1.34 us
    pallas_call x1, Pallas kernels, finish_queries(): call(query_kernel, (shape_of(tokens, w.shape[1]), shape_of(tokens, w.shap...  1.19 us
  transfers between devices with their start and end apart: 16, of which 7 were waited for; matrix products, arithmetic and copies ran while one was open for 0% of the time, Pallas kernels for 16%

profile of v5, /device:TPU:0, one launch (start us, length us, event | category | flops | bytes accessed | tf_op | source)
XLA Modules:
  0.0 47.8 jit_solution(8093699527603749299)
XLA Ops:
  0.6 1.3 %pack_heads.1 = (bf16[256,512]{1,0:T(8,128)(2,1)S(1)}, bf16[256,512]{1,0:T(8,128)(2,1)S(1)}, bf16[144,512]{1,0:T(8,128)(2,1)S(1)}, bf16[144,512]{1,0:T(8,128)(2,1)S(1)}) custom-call(s32[1,2]{1,0:T(1,128)} %bitcast.21, bf16[128,1024]{1,0:T(8,128)(2,1)} %bitcast.18, bf16[128,1024]{1,0:T(8,128)(2,1)} %bitcast.19, bf16[128,1024]{1,0:T(8,128)(2,1)} %bitcast.20), custom_call_target="tpu_custom_call" | custom-call | tf_op jit(solution)/shard_map/pack_heads/pallas_call | solution.py:97
  2.0 3.0 %collective-permute-start.1 = (bf16[256,512]{1,0:T(8,128)(2,1)S(1)}, bf16[256,512]{1,0:T(8,128)(2,1)S(1)}, u32[]{:S(2)}, u32[]{:S(2)}) collective-permute-start(bf16[256,512]{1,0:T(8,128)(2,1)S(1)} %get-tuple-element.31), channel_id=1, source_target_pairs={{0,4},{4,0},{8,12},{12,8},{16,20},{20,16},{24,28},{28,24},{1,5},{5... | collective-permute-start | bytes 786440 | tf_op jit(solution)/shard_map/ppermute | solution.py:403
  5.0 0.1 collective-permute-start.4
  5.1 1.3 %collective-permute-start.3 = (bf16[256,512]{1,0:T(8,128)(2,1)S(1)}, bf16[256,512]{1,0:T(8,128)(2,1)S(1)}, u32[]{:S(2)}, u32[]{:S(2)}) collective-permute-start(bf16[256,512]{1,0:T(8,128)(2,1)S(1)} %get-tuple-element.30.own), channel_id=1, source_target_pairs={{8,0},{16,8},{24,16},{4,12},{12,20},{20,28},{9,1},{17,9},{25,17},{... | collective-permute-start | bytes 786440 | tf_op jit(solution)/shard_map/ppermute | solution.py:403
  6.4 5.8 %collective-permute-done.1.par = bf16[256,512]{1,0:T(8,128)(2,1)S(1)} collective-permute-done((bf16[256,512]{1,0:T(8,128)(2,1)S(1)}, bf16[256,512]{1,0:T(8,128)(2,1)S(1)}, u32[]{:S(2)}, u32[]{:S(2)}) %collective-permute-start.1) | collective-permute-done | bytes 262176 | tf_op jit(solution)/shard_map/ppermute | solution.py:403
  12.1 4.0 %collective-permute-start.2 = (bf16[256,512]{1,0:T(8,128)(2,1)S(1)}, bf16[256,512]{1,0:T(8,128)(2,1)S(1)}, u32[]{:S(2)}, u32[]{:S(2)}) collective-permute-start(bf16[256,512]{1,0:T(8,128)(2,1)S(1)} %collective-permute-done.1.par), channel_id=1, source_target_pairs={{0,8},{8,16},{16,24},{12,4},{20,12},{28,20},{1,9},{9,17},{17,25},{... | collective-permute-start | bytes 786440 | tf_op jit(solution)/shard_map/ppermute | solution.py:403
  16.2 0.1 collective-permute-start
  16.3 0.1 collective-permute-start.6
  16.3 1.1 %collective-permute-done.4.cot_par.par = bf16[128,1024]{1,0:T(8,128)(2,1)S(1)} collective-permute-done((bf16[128,1024]{1,0:T(8,128)(2,1)}, bf16[128,1024]{1,0:T(8,128)(2,1)S(1)}, u32[]{:S(2)}, u32[]{:S(2)}) %collective-permute-start.4) | collective-permute-done | bytes 262176 | tf_op jit(solution)/shard_map/ppermute | solution.py:403
  17.4 0.0 collective-permute-start.7
  17.4 2.3 %grad_attended.1.after.ga = bf16[256,512]{1,0:T(8,128)(2,1)S(1)} custom-call(bf16[128,1024]{1,0:T(8,128)(2,1)} %bitcast.15, bf16[128,1024]{1,0:T(8,128)(2,1)S(1)} %collective-permute-done.4.cot_par.par, bf16[1024,1024]{1,0:T(8,128)(2,1)} %w.3), custom_call_target="tpu_custom_call" | custom-call | tf_op jit(solution)/shard_map/grad_attended/pallas_call | solution.py:129
  19.8 1.6 %collective-permute-done.q_par = bf16[144,512]{1,0:T(8,128)(2,1)S(1)} collective-permute-done((bf16[144,512]{1,0:T(8,128)(2,1)S(1)}, bf16[144,512]{1,0:T(8,128)(2,1)S(1)}, u32[]{:S(2)}, u32[]{:S(2)}) %collective-permute-start) | collective-permute-done | bytes 147488 | tf_op jit(solution)/shard_map/ppermute | solution.py:403
  21.4 0.0 collective-permute-done.3.far_par
  21.4 0.0 collective-permute-done.2.far_own
  21.4 0.0 copy-start.1
  21.4 1.6 %patch_forward.1 = (bf16[4,384,256]{2,1,0:T(8,128)(2,1)S(1)}, bf16[128,512]{1,0:T(8,128)(2,1)S(1)}, bf16[128,512]{1,0:T(8,128)(2,1)S(1)}, bf16[2,256,256]{2,1,0:T(8,128)(2,1)S(1)}) custom-call(bf16[144,512]{1,0:T(8,128)(2,1)S(1)} %get-tuple-element.28.q_own, bf16[144,512]{1,0:T(8,128)(2,1)S(1)} %collective-permute-done.q_par, ...), custom_call_target="tpu_custom_call" | custom-call | tf_op jit(solution)/shard_map/patch_forward/pallas_call | solution.py:209
  23.0 0.1 collective-permute-start.5
  23.1 1.4 %patch_backward.1 = (bf16[4,384,256]{2,1,0:T(8,128)(2,1)S(1)}, bf16[256,512]{1,0:T(8,128)(2,1)S(1)}, bf16[256,512]{1,0:T(8,128)(2,1)S(1)}) custom-call(bf16[144,512]{1,0:T(8,128)(2,1)S(1)} %get-tuple-element.28.q_own, bf16[144,512]{1,0:T(8,128)(2,1)S(1)} %collective-permute-done.q_par, bf16[256,512]{1,0:T(8,128)(2,1)S(1)} %get-tuple-element.30.own, ...), custom_call_target="tpu_custom_call" | custom-call | tf_op jit(solution)/shard_map/patch_backward/pallas_call | solution.py:269
  24.4 0.0 collective-permute-done.6.core_own
  24.5 0.0 collective-permute-done.7.core_par
  24.5 0.0 collective-permute-done.5.att_core
  24.5 0.0 copy-done.1
  24.5 0.4 weight_terms_sent.1._after
  24.9 1.6 %collective-permute-start.8 = (bf16[128,1024]{1,0:T(8,128)(2,1)S(1)}, bf16[128,1024]{1,0:T(8,128)(2,1)S(1)}, u32[]{:S(2)}, u32[]{:S(2)}) collective-permute-start(bf16[128,1024]{1,0:T(8,128)(2,1)S(1)} %weight_terms_sent.1._after), channel_id=1, source_target_pairs={{0,2},{1,3},{2,0},{3,1},{4,6},{5,7},{6,4},{7,5},{8,10},{9,11},{10,... | collective-permute-start | bytes 786440 | tf_op jit(solution)/shard_map/ppermute | solution.py:441
  26.5 1.3 %collective-permute-start.9 = (bf16[128,512]{1,0:T(8,128)(2,1)S(1)}, bf16[128,512]{1,0:T(8,128)(2,1)S(1)}, u32[]{:S(2)}, u32[]{:S(2)}) collective-permute-start(bf16[128,512]{1,0:T(8,128)(2,1)S(1)} %get-tuple-element.38), channel_id=1, source_target_pairs={{0,4},{4,0},{8,12},{12,8},{16,20},{20,16},{24,28},{28,24},{1,5},{5... | collective-permute-start | bytes 393224 | tf_op jit(solution)/shard_map/ppermute | solution.py:403
  27.7 0.7 %collective-permute-start.11 = (bf16[256,512]{1,0:T(8,128)(2,1)S(1)}, bf16[256,512]{1,0:T(8,128)(2,1)S(1)}, u32[]{:S(2)}, u32[]{:S(2)}) collective-permute-start(bf16[256,512]{1,0:T(8,128)(2,1)S(1)} %get-tuple-element.35._after), channel_id=1, source_target_pairs={{8,16},{12,20},{16,8},{20,12},{9,17},{13,21},{17,9},{21,13},{10,18... | collective-permute-start | bytes 786440 | tf_op jit(solution)/shard_map/ppermute | solution.py:403
  28.4 4.5 %collective-permute-start.12 = (bf16[256,512]{1,0:T(8,128)(2,1)S(1)}, bf16[256,512]{1,0:T(8,128)(2,1)S(1)}, u32[]{:S(2)}, u32[]{:S(2)}) collective-permute-start(bf16[256,512]{1,0:T(8,128)(2,1)S(1)} %get-tuple-element.45), channel_id=1, source_target_pairs={{0,8},{4,12},{8,0},{12,4},{16,24},{20,28},{24,16},{28,20},{1,9},{5... | collective-permute-start | bytes 786440 | tf_op jit(solution)/shard_map/ppermute | solution.py:403
  32.9 0.7 %patch_gradients.1 = (bf16[128,512]{1,0:T(8,128)(2,1)S(1)}, bf16[128,512]{1,0:T(8,128)(2,1)S(1)}, bf16[256,512]{1,0:T(8,128)(2,1)S(1)}, bf16[256,512]{1,0:T(8,128)(2,1)S(1)}) custom-call(bf16[144,512]{1,0:T(8,128)(2,1)S(1)} %get-tuple-element.28.q_own, bf16[144,512]{1,0:T(8,128)(2,1)S(1)} %collective-permute-done.q_par, ...), custom_call_target="tpu_custom_call" | custom-call | tf_op jit(solution)/shard_map/patch_gradients/pallas_call | solution.py:305
  33.5 0.4 weight_terms_kept.1
  34.0 0.0 copy-start
  34.0 0.0 collective-permute-done.9.att_back
  34.0 0.0 collective-permute-done.8
  34.0 0.1 convert_add_fusion
  34.1 1.3 %collective-permute-start.14 = (bf16[64,1024]{1,0:T(8,128)(2,1)S(1)}, bf16[64,1024]{1,0:T(8,128)(2,1)S(1)}, u32[]{:S(2)}, u32[]{:S(2)}) collective-permute-start(bf16[64,1024]{1,0:T(8,128)(2,1)S(1)} %slice.35), channel_id=1, source_target_pairs={{0,8},{4,12},{8,0},{12,4},{16,24},{20,28},{24,16},{28,20},{1,9},{5... | collective-permute-start | bytes 393224 | tf_op jit(solution)/shard_map/ppermute | solution.py:441
  35.4 1.1 %collective-permute-start.10 = (bf16[128,512]{1,0:T(8,128)(2,1)S(1)}, bf16[128,512]{1,0:T(8,128)(2,1)S(1)}, u32[]{:S(2)}, u32[]{:S(2)}) collective-permute-start(bf16[128,512]{1,0:T(8,128)(2,1)S(1)} %get-tuple-element.41), channel_id=1, source_target_pairs={{0,4},{4,0},{8,12},{12,8},{16,20},{20,16},{24,28},{28,24},{1,5},{5... | collective-permute-start | bytes 393224 | tf_op jit(solution)/shard_map/ppermute | solution.py:403
  36.5 3.6 %collective-permute-done.12.far_b = bf16[256,512]{1,0:T(8,128)(2,1)S(1)} collective-permute-done((bf16[256,512]{1,0:T(8,128)(2,1)S(1)}, bf16[256,512]{1,0:T(8,128)(2,1)S(1)}, u32[]{:S(2)}, u32[]{:S(2)}) %collective-permute-start.12) | collective-permute-done | bytes 262176 | tf_op jit(solution)/shard_map/ppermute | solution.py:403
  40.1 0.0 collective-permute-done.11.far_a
  40.1 0.1 add_returned.1
  40.2 0.8 %collective-permute-start.13 = (bf16[256,512]{1,0:T(8,128)(2,1)S(1)}, bf16[256,512]{1,0:T(8,128)(2,1)S(1)}, u32[]{:S(2)}, u32[]{:S(2)}) collective-permute-start(bf16[256,512]{1,0:T(8,128)(2,1)S(1)} %add_returned.1), channel_id=1, source_target_pairs={{0,4},{4,0},{8,12},{12,8},{16,20},{20,16},{24,28},{28,24},{1,5},{5... | collective-permute-start | bytes 786440 | tf_op jit(solution)/shard_map/ppermute | solution.py:403
  41.0 0.6 %collective-permute-done.14 = bf16[64,1024]{1,0:T(8,128)(2,1)S(1)} collective-permute-done((bf16[64,1024]{1,0:T(8,128)(2,1)S(1)}, bf16[64,1024]{1,0:T(8,128)(2,1)S(1)}, u32[]{:S(2)}, u32[]{:S(2)}) %collective-permute-start.14) | collective-permute-done | bytes 131104 | tf_op jit(solution)/shard_map/ppermute | solution.py:441
  41.6 1.7 %collective-permute-start.15 = (bf16[32,1024]{1,0:T(8,128)(2,1)S(1)}, bf16[32,1024]{1,0:T(8,128)(2,1)S(1)}, u32[]{:S(2)}, u32[]{:S(2)}) collective-permute-start(bf16[32,1024]{1,0:T(8,128)(2,1)S(1)} %slice.36), channel_id=1, source_target_pairs={{0,16},{4,20},{8,24},{12,28},{16,0},{20,4},{24,8},{28,12},{1,17},{... | collective-permute-start | bytes 196616 | tf_op jit(solution)/shard_map/ppermute | solution.py:441
  43.3 0.0 collective-permute-done.10.dq_back
  43.3 0.0 copy-done
  43.3 1.2 %finish_queries.1 = (bf16[128,1024]{1,0:T(8,128)(2,1)}, bf16[128,1024]{1,0:T(8,128)(2,1)}) custom-call(bf16[128,512]{1,0:T(8,128)(2,1)S(1)} %get-tuple-element.32.att_own, bf16[128,512]{1,0:T(8,128)(2,1)S(1)} %collective-permute-done.9.att_back, bf16[128,512]{1,0:T(8,128)(2,1)S(1)} %get-tuple-element.40.dq_own, ...), custom_call_target="tpu_custom_call" | custom-call | tf_op jit(solution)/shard_map/finish_queries/pallas_call | solution.py:344
  44.5 2.1 %collective-permute-done.13.home = bf16[256,512]{1,0:T(8,128)(2,1)S(1)} collective-permute-done((bf16[256,512]{1,0:T(8,128)(2,1)S(1)}, bf16[256,512]{1,0:T(8,128)(2,1)S(1)}, u32[]{:S(2)}, u32[]{:S(2)}) %collective-permute-start.13) | collective-permute-done | bytes 262176 | tf_op jit(solution)/shard_map/ppermute | solution.py:403
  46.6 0.2 collective-permute-done.15.out
  46.9 0.9 %finish_keys.1 = (bf16[128,1024]{1,0:T(8,128)(2,1)}, bf16[128,1024]{1,0:T(8,128)(2,1)}, f32[32,1024]{1,0:T(8,128)}) custom-call(bf16[256,512]{1,0:T(8,128)(2,1)S(1)} %get-tuple-element.44.own, bf16[256,512]{1,0:T(8,128)(2,1)S(1)} %collective-permute-done.11.far_a, bf16[256,512]{1,0:T(8,128)(2,1)S(1)} %collective-permute-done.12.far_b, ...), custom_call_target="tpu_custom_call" | custom-call | tf_op jit(solution)/shard_map/finish_keys/pallas_call | solution.py:381
  (5 shorter events, 0.1 us)
Async XLA Ops:
  2.0 10.2 %collective-permute-start.1 = (bf16[256,512]{1,0:T(8,128)(2,1)S(1)}, bf16[256,512]{1,0:T(8,128)(2,1)S(1)}, u32[]{:S(2)}, u32[]{:S(2)}) collective-permute-start(bf16[256,512]{1,0:T(8,128)(2,1)S(1)} %get-tuple-element.31), channel_id=1, source_target_pairs={{0,4},{4,0},{8,12},{12,8},{16,20},{20,16},{24,28},{28,24},{1,5},{5... | collective-permute-start | bytes 786440 | tf_op jit(solution)/shard_map/ppermute | solution.py:403
  5.0 12.4 %collective-permute-start.4 = (bf16[128,1024]{1,0:T(8,128)(2,1)}, bf16[128,1024]{1,0:T(8,128)(2,1)S(1)}, u32[]{:S(2)}, u32[]{:S(2)}) collective-permute-start(bf16[128,1024]{1,0:T(8,128)(2,1)} %bitcast.13), channel_id=1, source_target_pairs={{0,4},{4,0},{8,12},{12,8},{16,20},{20,16},{24,28},{28,24},{1,5},{5... | collective-permute-start | bytes 786440 | tf_op jit(solution)/shard_map/ppermute | solution.py:403
  5.1 16.3 %collective-permute-start.3 = (bf16[256,512]{1,0:T(8,128)(2,1)S(1)}, bf16[256,512]{1,0:T(8,128)(2,1)S(1)}, u32[]{:S(2)}, u32[]{:S(2)}) collective-permute-start(bf16[256,512]{1,0:T(8,128)(2,1)S(1)} %get-tuple-element.30.own), channel_id=1, source_target_pairs={{8,0},{16,8},{24,16},{4,12},{12,20},{20,28},{9,1},{17,9},{25,17},{... | collective-permute-start | bytes 786440 | tf_op jit(solution)/shard_map/ppermute | solution.py:403
  12.1 9.2 %collective-permute-start.2 = (bf16[256,512]{1,0:T(8,128)(2,1)S(1)}, bf16[256,512]{1,0:T(8,128)(2,1)S(1)}, u32[]{:S(2)}, u32[]{:S(2)}) collective-permute-start(bf16[256,512]{1,0:T(8,128)(2,1)S(1)} %collective-permute-done.1.par), channel_id=1, source_target_pairs={{0,8},{8,16},{16,24},{12,4},{20,12},{28,20},{1,9},{9,17},{17,25},{... | collective-permute-start | bytes 786440 | tf_op jit(solution)/shard_map/ppermute | solution.py:403
  16.2 5.2 %collective-permute-start = (bf16[144,512]{1,0:T(8,128)(2,1)S(1)}, bf16[144,512]{1,0:T(8,128)(2,1)S(1)}, u32[]{:S(2)}, u32[]{:S(2)}) collective-permute-start(bf16[144,512]{1,0:T(8,128)(2,1)S(1)} %get-tuple-element.29), channel_id=1, source_target_pairs={{0,4},{4,0},{8,12},{12,8},{16,20},{20,16},{24,28},{28,24},{1,5},{5... | collective-permute-start | bytes 442376 | tf_op jit(solution)/shard_map/ppermute | solution.py:403
  16.3 8.2 %collective-permute-start.6 = (bf16[128,1024]{1,0:T(8,128)(2,1)}, bf16[128,1024]{1,0:T(8,128)(2,1)S(1)}, u32[]{:S(2)}, u32[]{:S(2)}) collective-permute-start(bf16[128,1024]{1,0:T(8,128)(2,1)} %bitcast.14), channel_id=1, source_target_pairs={{0,1},{1,0},{2,3},{3,2},{4,5},{5,4},{6,7},{7,6},{8,9},{9,8},{10,11... | collective-permute-start | bytes 786440 | tf_op jit(solution)/shard_map/ppermute | solution.py:404
  17.4 7.0 %collective-permute-start.7 = (bf16[128,1024]{1,0:T(8,128)(2,1)S(1)}, bf16[128,1024]{1,0:T(8,128)(2,1)S(1)}, u32[]{:S(2)}, u32[]{:S(2)}) collective-permute-start(bf16[128,1024]{1,0:T(8,128)(2,1)S(1)} %collective-permute-done.4.cot_par.par), channel_id=1, source_target_pairs={{0,1},{1,0},{2,3},{3,2},{4,5},{5,4},{6,7},{7,6},{8,9},{9,8},{10,11... | collective-permute-start | bytes 786440 | tf_op jit(solution)/shard_map/ppermute | solution.py:404
  21.4 3.1 %copy-start.1 = (bf16[1,128,1024]{2,1,0:T(8,128)(2,1)S(1)}, bf16[1,128,1024]{2,1,0:T(8,128)(2,1)}, u32[]{:S(2)}) copy-start(bf16[1,128,1024]{2,1,0:T(8,128)(2,1)} %param.11) | copy-start | bytes 786436
  23.0 1.5 %collective-permute-start.5 = (bf16[256,256]{1,0:T(8,128)(2,1)S(1)}, bf16[256,256]{1,0:T(8,128)(2,1)S(1)}, u32[]{:S(2)}, u32[]{:S(2)}) collective-permute-start(bf16[256,256]{1,0:T(8,128)(2,1)S(1)} %get-tuple-element.51), channel_id=1, source_target_pairs={{0,1},{1,0},{2,3},{3,2},{4,5},{5,4},{6,7},{7,6},{8,9},{9,8},{10,11... | collective-permute-start | bytes 393224 | tf_op jit(solution)/shard_map/ppermute | solution.py:404
  24.9 9.1 %collective-permute-start.8 = (bf16[128,1024]{1,0:T(8,128)(2,1)S(1)}, bf16[128,1024]{1,0:T(8,128)(2,1)S(1)}, u32[]{:S(2)}, u32[]{:S(2)}) collective-permute-start(bf16[128,1024]{1,0:T(8,128)(2,1)S(1)} %weight_terms_sent.1._after), channel_id=1, source_target_pairs={{0,2},{1,3},{2,0},{3,1},{4,6},{5,7},{6,4},{7,5},{8,10},{9,11},{10,... | collective-permute-start | bytes 786440 | tf_op jit(solution)/shard_map/ppermute | solution.py:441
  26.5 7.5 %collective-permute-start.9 = (bf16[128,512]{1,0:T(8,128)(2,1)S(1)}, bf16[128,512]{1,0:T(8,128)(2,1)S(1)}, u32[]{:S(2)}, u32[]{:S(2)}) collective-permute-start(bf16[128,512]{1,0:T(8,128)(2,1)S(1)} %get-tuple-element.38), channel_id=1, source_target_pairs={{0,4},{4,0},{8,12},{12,8},{16,20},{20,16},{24,28},{28,24},{1,5},{5... | collective-permute-start | bytes 393224 | tf_op jit(solution)/shard_map/ppermute | solution.py:403
  27.7 12.3 %collective-permute-start.11 = (bf16[256,512]{1,0:T(8,128)(2,1)S(1)}, bf16[256,512]{1,0:T(8,128)(2,1)S(1)}, u32[]{:S(2)}, u32[]{:S(2)}) collective-permute-start(bf16[256,512]{1,0:T(8,128)(2,1)S(1)} %get-tuple-element.35._after), channel_id=1, source_target_pairs={{8,16},{12,20},{16,8},{20,12},{9,17},{13,21},{17,9},{21,13},{10,18... | collective-permute-start | bytes 786440 | tf_op jit(solution)/shard_map/ppermute | solution.py:403
  28.4 11.6 %collective-permute-start.12 = (bf16[256,512]{1,0:T(8,128)(2,1)S(1)}, bf16[256,512]{1,0:T(8,128)(2,1)S(1)}, u32[]{:S(2)}, u32[]{:S(2)}) collective-permute-start(bf16[256,512]{1,0:T(8,128)(2,1)S(1)} %get-tuple-element.45), channel_id=1, source_target_pairs={{0,8},{4,12},{8,0},{12,4},{16,24},{20,28},{24,16},{28,20},{1,9},{5... | collective-permute-start | bytes 786440 | tf_op jit(solution)/shard_map/ppermute | solution.py:403
  34.0 9.4 %copy-start = (bf16[1024,1024]{1,0:T(8,128)(2,1)S(1)}, bf16[1024,1024]{1,0:T(8,128)(2,1)}, u32[]{:S(2)}) copy-start(bf16[1024,1024]{1,0:T(8,128)(2,1)} %w.3) | copy-start | bytes 6291460
  34.1 7.5 %collective-permute-start.14 = (bf16[64,1024]{1,0:T(8,128)(2,1)S(1)}, bf16[64,1024]{1,0:T(8,128)(2,1)S(1)}, u32[]{:S(2)}, u32[]{:S(2)}) collective-permute-start(bf16[64,1024]{1,0:T(8,128)(2,1)S(1)} %slice.35), channel_id=1, source_target_pairs={{0,8},{4,12},{8,0},{12,4},{16,24},{20,28},{24,16},{28,20},{1,9},{5... | collective-permute-start | bytes 393224 | tf_op jit(solution)/shard_map/ppermute | solution.py:441
  35.4 7.9 %collective-permute-start.10 = (bf16[128,512]{1,0:T(8,128)(2,1)S(1)}, bf16[128,512]{1,0:T(8,128)(2,1)S(1)}, u32[]{:S(2)}, u32[]{:S(2)}) collective-permute-start(bf16[128,512]{1,0:T(8,128)(2,1)S(1)} %get-tuple-element.41), channel_id=1, source_target_pairs={{0,4},{4,0},{8,12},{12,8},{16,20},{20,16},{24,28},{28,24},{1,5},{5... | collective-permute-start | bytes 393224 | tf_op jit(solution)/shard_map/ppermute | solution.py:403
  40.2 6.4 %collective-permute-start.13 = (bf16[256,512]{1,0:T(8,128)(2,1)S(1)}, bf16[256,512]{1,0:T(8,128)(2,1)S(1)}, u32[]{:S(2)}, u32[]{:S(2)}) collective-permute-start(bf16[256,512]{1,0:T(8,128)(2,1)S(1)} %add_returned.1), channel_id=1, source_target_pairs={{0,4},{4,0},{8,12},{12,8},{16,20},{20,16},{24,28},{28,24},{1,5},{5... | collective-permute-start | bytes 786440 | tf_op jit(solution)/shard_map/ppermute | solution.py:403
  41.6 5.2 %collective-permute-start.15 = (bf16[32,1024]{1,0:T(8,128)(2,1)S(1)}, bf16[32,1024]{1,0:T(8,128)(2,1)S(1)}, u32[]{:S(2)}, u32[]{:S(2)}) collective-permute-start(bf16[32,1024]{1,0:T(8,128)(2,1)S(1)} %slice.36), channel_id=1, source_target_pairs={{0,16},{4,20},{8,24},{12,28},{16,0},{20,4},{24,8},{28,12},{1,17},{... | collective-permute-start | bytes 196616 | tf_op jit(solution)/shard_map/ppermute | solution.py:441

commit v6 on v5

--- a/solution.py
+++ b/solution.py
@@ -440,7 +440,7 @@
     for place, (axis, count, bit) in enumerate(hops):
         out = lax.ppermute(out, axis, [(i, i ^ bit) for i in range(count)])
         if place == 0:
-            out, d_own, att_back = lax.optimization_barrier((out, d_own, att_back))
+            out, att_back = lax.optimization_barrier((out, att_back))
         if place + 1 < len(hops):
             total = keep + out.astype(F32)
             rows = total.shape[0] // 2

time: 48.1 us -> 48.1 us (level)
    ppermute x10, waiting for transfers between devices: 14.2 us -> 13.6 us  [on_device(): send = lambda x, pairs: lax.ppermute(x, 'seq', pairs)]
  transfers between devices with their start and end apart: 16 -> 16, of which waited for: 7 -> 8; matrix products, arithmetic and copies ran while one was open for 0% -> 0% of each run, Pallas kernels for 16% -> 16%
where the time goes in v6:
time: 48.1 us; the launch traced here: 47.8 us
  starting transfers between devices  21.8 us (45%)
  waiting for transfers between devices  14.7 us (31%)
  Pallas kernels  10.3 us (21%)
  between operations  0.83 us (2%)
    ppermute x10, starting transfers between devices, on_device(): send = lambda x, pairs: lax.ppermute(x, 'seq', pairs)  16.8 us
    ppermute x10, waiting for transfers between devices, on_device(): send = lambda x, pairs: lax.ppermute(x, 'seq', pairs)  13.6 us
    ppermute x3, starting transfers between devices, on_device(): out = lax.ppermute(out, axis, [(i, i ^ bit) for i in range(count)])  4.89 us
    pallas_call x1, Pallas kernels, grad_attended(): call(turn_kernel, (shape_of(2 * tokens, pairs * HD),), [HBM, VMEM, HBM],...  2.32 us
    pallas_call x1, Pallas kernels, forward(): call(functools.partial(forward_kernel, direct, n_dp), (shape_of(pairs, 3...  1.57 us
    pallas_call x1, Pallas kernels, backward(): call(backward_kernel, (shape_of(*probs.shape),) + (shape_of(2 * tokens, h...  1.35 us
    pallas_call x1, Pallas kernels, pack(): call(pack_kernel, (kv, kv) + (shape_of(tokens + FLAG_ROWS, half),) * 2, [...  1.34 us
    pallas_call x1, Pallas kernels, finish_queries(): call(query_kernel, (shape_of(tokens, w.shape[1]), shape_of(tokens, w.shap...  1.19 us
  transfers between devices with their start and end apart: 16, of which 8 were waited for; matrix products, arithmetic and copies ran while one was open for 0% of the time, Pallas kernels for 16%

profile of v6, /device:TPU:0, one launch (start us, length us, event | category | flops | bytes accessed | tf_op | source)
XLA Modules:
  0.0 47.8 jit_solution(8235925361394887429)
XLA Ops:
  0.6 1.3 %pack_heads.1 = (bf16[256,512]{1,0:T(8,128)(2,1)S(1)}, bf16[256,512]{1,0:T(8,128)(2,1)S(1)}, bf16[144,512]{1,0:T(8,128)(2,1)S(1)}, bf16[144,512]{1,0:T(8,128)(2,1)S(1)}) custom-call(s32[1,2]{1,0:T(1,128)} %bitcast.21, bf16[128,1024]{1,0:T(8,128)(2,1)} %bitcast.18, bf16[128,1024]{1,0:T(8,128)(2,1)} %bitcast.19, bf16[128,1024]{1,0:T(8,128)(2,1)} %bitcast.20), custom_call_target="tpu_custom_call" | custom-call | tf_op jit(solution)/shard_map/pack_heads/pallas_call | solution.py:97
  2.0 3.0 %collective-permute-start.1 = (bf16[256,512]{1,0:T(8,128)(2,1)S(1)}, bf16[256,512]{1,0:T(8,128)(2,1)S(1)}, u32[]{:S(2)}, u32[]{:S(2)}) collective-permute-start(bf16[256,512]{1,0:T(8,128)(2,1)S(1)} %get-tuple-element.30), channel_id=1, source_target_pairs={{0,4},{4,0},{8,12},{12,8},{16,20},{20,16},{24,28},{28,24},{1,5},{5... | collective-permute-start | bytes 786440 | tf_op jit(solution)/shard_map/ppermute | solution.py:403
  5.0 0.1 collective-permute-start.4
  5.1 1.3 %collective-permute-start.3 = (bf16[256,512]{1,0:T(8,128)(2,1)S(1)}, bf16[256,512]{1,0:T(8,128)(2,1)S(1)}, u32[]{:S(2)}, u32[]{:S(2)}) collective-permute-start(bf16[256,512]{1,0:T(8,128)(2,1)S(1)} %get-tuple-element.29.own), channel_id=1, source_target_pairs={{8,0},{16,8},{24,16},{4,12},{12,20},{20,28},{9,1},{17,9},{25,17},{... | collective-permute-start | bytes 786440 | tf_op jit(solution)/shard_map/ppermute | solution.py:403
  6.4 5.8 %collective-permute-done.1.par = bf16[256,512]{1,0:T(8,128)(2,1)S(1)} collective-permute-done((bf16[256,512]{1,0:T(8,128)(2,1)S(1)}, bf16[256,512]{1,0:T(8,128)(2,1)S(1)}, u32[]{:S(2)}, u32[]{:S(2)}) %collective-permute-start.1) | collective-permute-done | bytes 262176 | tf_op jit(solution)/shard_map/ppermute | solution.py:403
  12.1 4.0 %collective-permute-start.2 = (bf16[256,512]{1,0:T(8,128)(2,1)S(1)}, bf16[256,512]{1,0:T(8,128)(2,1)S(1)}, u32[]{:S(2)}, u32[]{:S(2)}) collective-permute-start(bf16[256,512]{1,0:T(8,128)(2,1)S(1)} %collective-permute-done.1.par), channel_id=1, source_target_pairs={{0,8},{8,16},{16,24},{12,4},{20,12},{28,20},{1,9},{9,17},{17,25},{... | collective-permute-start | bytes 786440 | tf_op jit(solution)/shard_map/ppermute | solution.py:403
  16.2 0.1 collective-permute-start
  16.3 0.1 collective-permute-start.6
  16.3 1.1 %collective-permute-done.4.cot_par.par = bf16[128,1024]{1,0:T(8,128)(2,1)S(1)} collective-permute-done((bf16[128,1024]{1,0:T(8,128)(2,1)}, bf16[128,1024]{1,0:T(8,128)(2,1)S(1)}, u32[]{:S(2)}, u32[]{:S(2)}) %collective-permute-start.4) | collective-permute-done | bytes 262176 | tf_op jit(solution)/shard_map/ppermute | solution.py:403
  17.4 0.0 collective-permute-start.7
  17.4 2.3 %grad_attended.1.after.ga = bf16[256,512]{1,0:T(8,128)(2,1)S(1)} custom-call(bf16[128,1024]{1,0:T(8,128)(2,1)} %bitcast.15, bf16[128,1024]{1,0:T(8,128)(2,1)S(1)} %collective-permute-done.4.cot_par.par, bf16[1024,1024]{1,0:T(8,128)(2,1)} %w.3), custom_call_target="tpu_custom_call" | custom-call | tf_op jit(solution)/shard_map/grad_attended/pallas_call | solution.py:129
  19.8 1.6 %collective-permute-done.q_par = bf16[144,512]{1,0:T(8,128)(2,1)S(1)} collective-permute-done((bf16[144,512]{1,0:T(8,128)(2,1)S(1)}, bf16[144,512]{1,0:T(8,128)(2,1)S(1)}, u32[]{:S(2)}, u32[]{:S(2)}) %collective-permute-start) | collective-permute-done | bytes 147488 | tf_op jit(solution)/shard_map/ppermute | solution.py:403
  21.4 0.0 collective-permute-done.3.far_par
  21.4 0.0 collective-permute-done.2.far_own
  21.4 0.0 copy-start.1
  21.4 1.6 %patch_forward.1 = (bf16[4,384,256]{2,1,0:T(8,128)(2,1)S(1)}, bf16[128,512]{1,0:T(8,128)(2,1)S(1)}, bf16[128,512]{1,0:T(8,128)(2,1)S(1)}, bf16[2,256,256]{2,1,0:T(8,128)(2,1)S(1)}) custom-call(bf16[144,512]{1,0:T(8,128)(2,1)S(1)} %get-tuple-element.27.q_own, bf16[144,512]{1,0:T(8,128)(2,1)S(1)} %collective-permute-done.q_par, ...), custom_call_target="tpu_custom_call" | custom-call | tf_op jit(solution)/shard_map/patch_forward/pallas_call | solution.py:209
  23.0 0.1 collective-permute-start.5
  23.1 1.3 %patch_backward.1 = (bf16[4,384,256]{2,1,0:T(8,128)(2,1)S(1)}, bf16[256,512]{1,0:T(8,128)(2,1)S(1)}, bf16[256,512]{1,0:T(8,128)(2,1)S(1)}) custom-call(bf16[144,512]{1,0:T(8,128)(2,1)S(1)} %get-tuple-element.27.q_own, bf16[144,512]{1,0:T(8,128)(2,1)S(1)} %collective-permute-done.q_par, bf16[256,512]{1,0:T(8,128)(2,1)S(1)} %get-tuple-element.29.own, ...), custom_call_target="tpu_custom_call" | custom-call | tf_op jit(solution)/shard_map/patch_backward/pallas_call | solution.py:269
  24.4 0.0 collective-permute-done.6.core_own
  24.4 0.0 collective-permute-done.7.core_par
  24.5 0.0 collective-permute-done.5.att_core
  24.5 0.0 copy-done.1
  24.5 0.4 weight_terms_sent.1._after
  24.9 1.6 %collective-permute-start.8 = (bf16[128,1024]{1,0:T(8,128)(2,1)S(1)}, bf16[128,1024]{1,0:T(8,128)(2,1)S(1)}, u32[]{:S(2)}, u32[]{:S(2)}) collective-permute-start(bf16[128,1024]{1,0:T(8,128)(2,1)S(1)} %weight_terms_sent.1._after), channel_id=1, source_target_pairs={{0,2},{1,3},{2,0},{3,1},{4,6},{5,7},{6,4},{7,5},{8,10},{9,11},{10,... | collective-permute-start | bytes 786440 | tf_op jit(solution)/shard_map/ppermute | solution.py:441
  26.5 1.3 %collective-permute-start.9 = (bf16[128,512]{1,0:T(8,128)(2,1)S(1)}, bf16[128,512]{1,0:T(8,128)(2,1)S(1)}, u32[]{:S(2)}, u32[]{:S(2)}) collective-permute-start(bf16[128,512]{1,0:T(8,128)(2,1)S(1)} %get-tuple-element.35), channel_id=1, source_target_pairs={{0,4},{4,0},{8,12},{12,8},{16,20},{20,16},{24,28},{28,24},{1,5},{5... | collective-permute-start | bytes 393224 | tf_op jit(solution)/shard_map/ppermute | solution.py:403
  27.8 0.7 %collective-permute-start.11 = (bf16[256,512]{1,0:T(8,128)(2,1)S(1)}, bf16[256,512]{1,0:T(8,128)(2,1)S(1)}, u32[]{:S(2)}, u32[]{:S(2)}) collective-permute-start(bf16[256,512]{1,0:T(8,128)(2,1)S(1)} %get-tuple-element.34._after), channel_id=1, source_target_pairs={{8,16},{12,20},{16,8},{20,12},{9,17},{13,21},{17,9},{21,13},{10,18... | collective-permute-start | bytes 786440 | tf_op jit(solution)/shard_map/ppermute | solution.py:403
  28.4 4.5 %collective-permute-start.12 = (bf16[256,512]{1,0:T(8,128)(2,1)S(1)}, bf16[256,512]{1,0:T(8,128)(2,1)S(1)}, u32[]{:S(2)}, u32[]{:S(2)}) collective-permute-start(bf16[256,512]{1,0:T(8,128)(2,1)S(1)} %get-tuple-element.43), channel_id=1, source_target_pairs={{0,8},{4,12},{8,0},{12,4},{16,24},{20,28},{24,16},{28,20},{1,9},{5... | collective-permute-start | bytes 786440 | tf_op jit(solution)/shard_map/ppermute | solution.py:403
  32.9 0.4 weight_terms_kept.1
  33.3 0.0 collective-permute-done.9.att_back
  33.3 0.4 collective-permute-done.8
  33.7 0.1 convert_add_fusion
  33.8 1.6 %collective-permute-start.14 = (bf16[64,1024]{1,0:T(8,128)(2,1)S(1)}, bf16[64,1024]{1,0:T(8,128)(2,1)S(1)}, u32[]{:S(2)}, u32[]{:S(2)}) collective-permute-start(bf16[64,1024]{1,0:T(8,128)(2,1)S(1)} %slice.35), channel_id=1, source_target_pairs={{0,8},{4,12},{8,0},{12,4},{16,24},{20,28},{24,16},{28,20},{1,9},{5... | collective-permute-start | bytes 393224 | tf_op jit(solution)/shard_map/ppermute | solution.py:441
  35.4 0.0 copy-start
  35.4 0.7 %patch_gradients.1 = (bf16[128,512]{1,0:T(8,128)(2,1)S(1)}, bf16[128,512]{1,0:T(8,128)(2,1)S(1)}, bf16[256,512]{1,0:T(8,128)(2,1)S(1)}, bf16[256,512]{1,0:T(8,128)(2,1)S(1)}) custom-call(bf16[144,512]{1,0:T(8,128)(2,1)S(1)} %get-tuple-element.27.q_own, bf16[144,512]{1,0:T(8,128)(2,1)S(1)} %collective-permute-done.q_par, ...), custom_call_target="tpu_custom_call" | custom-call | tf_op jit(solution)/shard_map/patch_gradients/pallas_call | solution.py:305
  36.1 1.1 %collective-permute-start.10 = (bf16[128,512]{1,0:T(8,128)(2,1)S(1)}, bf16[128,512]{1,0:T(8,128)(2,1)S(1)}, u32[]{:S(2)}, u32[]{:S(2)}) collective-permute-start(bf16[128,512]{1,0:T(8,128)(2,1)S(1)} %get-tuple-element.39), channel_id=1, source_target_pairs={{0,4},{4,0},{8,12},{12,8},{16,20},{20,16},{24,28},{28,24},{1,5},{5... | collective-permute-start | bytes 393224 | tf_op jit(solution)/shard_map/ppermute | solution.py:403
  37.2 2.9 %collective-permute-done.12.far_b = bf16[256,512]{1,0:T(8,128)(2,1)S(1)} collective-permute-done((bf16[256,512]{1,0:T(8,128)(2,1)S(1)}, bf16[256,512]{1,0:T(8,128)(2,1)S(1)}, u32[]{:S(2)}, u32[]{:S(2)}) %collective-permute-start.12) | collective-permute-done | bytes 262176 | tf_op jit(solution)/shard_map/ppermute | solution.py:403
  40.1 0.0 collective-permute-done.11.far_a
  40.1 0.1 add_returned.1
  40.2 0.8 %collective-permute-start.13 = (bf16[256,512]{1,0:T(8,128)(2,1)S(1)}, bf16[256,512]{1,0:T(8,128)(2,1)S(1)}, u32[]{:S(2)}, u32[]{:S(2)}) collective-permute-start(bf16[256,512]{1,0:T(8,128)(2,1)S(1)} %add_returned.1), channel_id=1, source_target_pairs={{0,4},{4,0},{8,12},{12,8},{16,20},{20,16},{24,28},{28,24},{1,5},{5... | collective-permute-start | bytes 786440 | tf_op jit(solution)/shard_map/ppermute | solution.py:403
  41.0 0.6 %collective-permute-done.14 = bf16[64,1024]{1,0:T(8,128)(2,1)S(1)} collective-permute-done((bf16[64,1024]{1,0:T(8,128)(2,1)S(1)}, bf16[64,1024]{1,0:T(8,128)(2,1)S(1)}, u32[]{:S(2)}, u32[]{:S(2)}) %collective-permute-start.14) | collective-permute-done | bytes 131104 | tf_op jit(solution)/shard_map/ppermute | solution.py:441
  41.6 1.7 %collective-permute-start.15 = (bf16[32,1024]{1,0:T(8,128)(2,1)S(1)}, bf16[32,1024]{1,0:T(8,128)(2,1)S(1)}, u32[]{:S(2)}, u32[]{:S(2)}) collective-permute-start(bf16[32,1024]{1,0:T(8,128)(2,1)S(1)} %slice.36), channel_id=1, source_target_pairs={{0,16},{4,20},{8,24},{12,28},{16,0},{20,4},{24,8},{28,12},{1,17},{... | collective-permute-start | bytes 196616 | tf_op jit(solution)/shard_map/ppermute | solution.py:441
  43.3 0.0 collective-permute-done.10.dq_back
  43.3 0.0 copy-done
  43.3 1.2 %finish_queries.1 = (bf16[128,1024]{1,0:T(8,128)(2,1)}, bf16[128,1024]{1,0:T(8,128)(2,1)}) custom-call(bf16[128,512]{1,0:T(8,128)(2,1)S(1)} %get-tuple-element.31.att_own, bf16[128,512]{1,0:T(8,128)(2,1)S(1)} %collective-permute-done.9.att_back, bf16[128,512]{1,0:T(8,128)(2,1)S(1)} %get-tuple-element.38.dq_own, ...), custom_call_target="tpu_custom_call" | custom-call | tf_op jit(solution)/shard_map/finish_queries/pallas_call | solution.py:344
  44.5 2.2 %collective-permute-done.13.home = bf16[256,512]{1,0:T(8,128)(2,1)S(1)} collective-permute-done((bf16[256,512]{1,0:T(8,128)(2,1)S(1)}, bf16[256,512]{1,0:T(8,128)(2,1)S(1)}, u32[]{:S(2)}, u32[]{:S(2)}) %collective-permute-start.13) | collective-permute-done | bytes 262176 | tf_op jit(solution)/shard_map/ppermute | solution.py:403
  46.7 0.2 collective-permute-done.15.out
  46.9 0.9 %finish_keys.1 = (bf16[128,1024]{1,0:T(8,128)(2,1)}, bf16[128,1024]{1,0:T(8,128)(2,1)}, f32[32,1024]{1,0:T(8,128)}) custom-call(bf16[256,512]{1,0:T(8,128)(2,1)S(1)} %get-tuple-element.42.own, bf16[256,512]{1,0:T(8,128)(2,1)S(1)} %collective-permute-done.11.far_a, bf16[256,512]{1,0:T(8,128)(2,1)S(1)} %collective-permute-done.12.far_b, ...), custom_call_target="tpu_custom_call" | custom-call | tf_op jit(solution)/shard_map/finish_keys/pallas_call | solution.py:381
  (5 shorter events, 0.1 us)
Async XLA Ops:
  2.0 10.2 %collective-permute-start.1 = (bf16[256,512]{1,0:T(8,128)(2,1)S(1)}, bf16[256,512]{1,0:T(8,128)(2,1)S(1)}, u32[]{:S(2)}, u32[]{:S(2)}) collective-permute-start(bf16[256,512]{1,0:T(8,128)(2,1)S(1)} %get-tuple-element.30), channel_id=1, source_target_pairs={{0,4},{4,0},{8,12},{12,8},{16,20},{20,16},{24,28},{28,24},{1,5},{5... | collective-permute-start | bytes 786440 | tf_op jit(solution)/shard_map/ppermute | solution.py:403
  5.0 12.4 %collective-permute-start.4 = (bf16[128,1024]{1,0:T(8,128)(2,1)}, bf16[128,1024]{1,0:T(8,128)(2,1)S(1)}, u32[]{:S(2)}, u32[]{:S(2)}) collective-permute-start(bf16[128,1024]{1,0:T(8,128)(2,1)} %bitcast.13), channel_id=1, source_target_pairs={{0,4},{4,0},{8,12},{12,8},{16,20},{20,16},{24,28},{28,24},{1,5},{5... | collective-permute-start | bytes 786440 | tf_op jit(solution)/shard_map/ppermute | solution.py:403
  5.1 16.3 %collective-permute-start.3 = (bf16[256,512]{1,0:T(8,128)(2,1)S(1)}, bf16[256,512]{1,0:T(8,128)(2,1)S(1)}, u32[]{:S(2)}, u32[]{:S(2)}) collective-permute-start(bf16[256,512]{1,0:T(8,128)(2,1)S(1)} %get-tuple-element.29.own), channel_id=1, source_target_pairs={{8,0},{16,8},{24,16},{4,12},{12,20},{20,28},{9,1},{17,9},{25,17},{... | collective-permute-start | bytes 786440 | tf_op jit(solution)/shard_map/ppermute | solution.py:403
  12.1 9.2 %collective-permute-start.2 = (bf16[256,512]{1,0:T(8,128)(2,1)S(1)}, bf16[256,512]{1,0:T(8,128)(2,1)S(1)}, u32[]{:S(2)}, u32[]{:S(2)}) collective-permute-start(bf16[256,512]{1,0:T(8,128)(2,1)S(1)} %collective-permute-done.1.par), channel_id=1, source_target_pairs={{0,8},{8,16},{16,24},{12,4},{20,12},{28,20},{1,9},{9,17},{17,25},{... | collective-permute-start | bytes 786440 | tf_op jit(solution)/shard_map/ppermute | solution.py:403
  16.2 5.2 %collective-permute-start = (bf16[144,512]{1,0:T(8,128)(2,1)S(1)}, bf16[144,512]{1,0:T(8,128)(2,1)S(1)}, u32[]{:S(2)}, u32[]{:S(2)}) collective-permute-start(bf16[144,512]{1,0:T(8,128)(2,1)S(1)} %get-tuple-element.28), channel_id=1, source_target_pairs={{0,4},{4,0},{8,12},{12,8},{16,20},{20,16},{24,28},{28,24},{1,5},{5... | collective-permute-start | bytes 442376 | tf_op jit(solution)/shard_map/ppermute | solution.py:403
  16.3 8.2 %collective-permute-start.6 = (bf16[128,1024]{1,0:T(8,128)(2,1)}, bf16[128,1024]{1,0:T(8,128)(2,1)S(1)}, u32[]{:S(2)}, u32[]{:S(2)}) collective-permute-start(bf16[128,1024]{1,0:T(8,128)(2,1)} %bitcast.14), channel_id=1, source_target_pairs={{0,1},{1,0},{2,3},{3,2},{4,5},{5,4},{6,7},{7,6},{8,9},{9,8},{10,11... | collective-permute-start | bytes 786440 | tf_op jit(solution)/shard_map/ppermute | solution.py:404
  17.4 7.0 %collective-permute-start.7 = (bf16[128,1024]{1,0:T(8,128)(2,1)S(1)}, bf16[128,1024]{1,0:T(8,128)(2,1)S(1)}, u32[]{:S(2)}, u32[]{:S(2)}) collective-permute-start(bf16[128,1024]{1,0:T(8,128)(2,1)S(1)} %collective-permute-done.4.cot_par.par), channel_id=1, source_target_pairs={{0,1},{1,0},{2,3},{3,2},{4,5},{5,4},{6,7},{7,6},{8,9},{9,8},{10,11... | collective-permute-start | bytes 786440 | tf_op jit(solution)/shard_map/ppermute | solution.py:404
  21.4 3.1 %copy-start.1 = (bf16[1,128,1024]{2,1,0:T(8,128)(2,1)S(1)}, bf16[1,128,1024]{2,1,0:T(8,128)(2,1)}, u32[]{:S(2)}) copy-start(bf16[1,128,1024]{2,1,0:T(8,128)(2,1)} %param.11) | copy-start | bytes 786436
  23.0 1.5 %collective-permute-start.5 = (bf16[256,256]{1,0:T(8,128)(2,1)S(1)}, bf16[256,256]{1,0:T(8,128)(2,1)S(1)}, u32[]{:S(2)}, u32[]{:S(2)}) collective-permute-start(bf16[256,256]{1,0:T(8,128)(2,1)S(1)} %get-tuple-element.49), channel_id=1, source_target_pairs={{0,1},{1,0},{2,3},{3,2},{4,5},{5,4},{6,7},{7,6},{8,9},{9,8},{10,11... | collective-permute-start | bytes 393224 | tf_op jit(solution)/shard_map/ppermute | solution.py:404
  24.9 8.8 %collective-permute-start.8 = (bf16[128,1024]{1,0:T(8,128)(2,1)S(1)}, bf16[128,1024]{1,0:T(8,128)(2,1)S(1)}, u32[]{:S(2)}, u32[]{:S(2)}) collective-permute-start(bf16[128,1024]{1,0:T(8,128)(2,1)S(1)} %weight_terms_sent.1._after), channel_id=1, source_target_pairs={{0,2},{1,3},{2,0},{3,1},{4,6},{5,7},{6,4},{7,5},{8,10},{9,11},{10,... | collective-permute-start | bytes 786440 | tf_op jit(solution)/shard_map/ppermute | solution.py:441
  26.5 6.8 %collective-permute-start.9 = (bf16[128,512]{1,0:T(8,128)(2,1)S(1)}, bf16[128,512]{1,0:T(8,128)(2,1)S(1)}, u32[]{:S(2)}, u32[]{:S(2)}) collective-permute-start(bf16[128,512]{1,0:T(8,128)(2,1)S(1)} %get-tuple-element.35), channel_id=1, source_target_pairs={{0,4},{4,0},{8,12},{12,8},{16,20},{20,16},{24,28},{28,24},{1,5},{5... | collective-permute-start | bytes 393224 | tf_op jit(solution)/shard_map/ppermute | solution.py:403
  27.8 12.3 %collective-permute-start.11 = (bf16[256,512]{1,0:T(8,128)(2,1)S(1)}, bf16[256,512]{1,0:T(8,128)(2,1)S(1)}, u32[]{:S(2)}, u32[]{:S(2)}) collective-permute-start(bf16[256,512]{1,0:T(8,128)(2,1)S(1)} %get-tuple-element.34._after), channel_id=1, source_target_pairs={{8,16},{12,20},{16,8},{20,12},{9,17},{13,21},{17,9},{21,13},{10,18... | collective-permute-start | bytes 786440 | tf_op jit(solution)/shard_map/ppermute | solution.py:403
  28.4 11.6 %collective-permute-start.12 = (bf16[256,512]{1,0:T(8,128)(2,1)S(1)}, bf16[256,512]{1,0:T(8,128)(2,1)S(1)}, u32[]{:S(2)}, u32[]{:S(2)}) collective-permute-start(bf16[256,512]{1,0:T(8,128)(2,1)S(1)} %get-tuple-element.43), channel_id=1, source_target_pairs={{0,8},{4,12},{8,0},{12,4},{16,24},{20,28},{24,16},{28,20},{1,9},{5... | collective-permute-start | bytes 786440 | tf_op jit(solution)/shard_map/ppermute | solution.py:403
  33.8 7.8 %collective-permute-start.14 = (bf16[64,1024]{1,0:T(8,128)(2,1)S(1)}, bf16[64,1024]{1,0:T(8,128)(2,1)S(1)}, u32[]{:S(2)}, u32[]{:S(2)}) collective-permute-start(bf16[64,1024]{1,0:T(8,128)(2,1)S(1)} %slice.35), channel_id=1, source_target_pairs={{0,8},{4,12},{8,0},{12,4},{16,24},{20,28},{24,16},{28,20},{1,9},{5... | collective-permute-start | bytes 393224 | tf_op jit(solution)/shard_map/ppermute | solution.py:441
  35.4 7.9 %copy-start = (bf16[1024,1024]{1,0:T(8,128)(2,1)S(1)}, bf16[1024,1024]{1,0:T(8,128)(2,1)}, u32[]{:S(2)}) copy-start(bf16[1024,1024]{1,0:T(8,128)(2,1)} %w.3) | copy-start | bytes 6291460
  36.1 7.3 %collective-permute-start.10 = (bf16[128,512]{1,0:T(8,128)(2,1)S(1)}, bf16[128,512]{1,0:T(8,128)(2,1)S(1)}, u32[]{:S(2)}, u32[]{:S(2)}) collective-permute-start(bf16[128,512]{1,0:T(8,128)(2,1)S(1)} %get-tuple-element.39), channel_id=1, source_target_pairs={{0,4},{4,0},{8,12},{12,8},{16,20},{20,16},{24,28},{28,24},{1,5},{5... | collective-permute-start | bytes 393224 | tf_op jit(solution)/shard_map/ppermute | solution.py:403
  40.2 6.5 %collective-permute-start.13 = (bf16[256,512]{1,0:T(8,128)(2,1)S(1)}, bf16[256,512]{1,0:T(8,128)(2,1)S(1)}, u32[]{:S(2)}, u32[]{:S(2)}) collective-permute-start(bf16[256,512]{1,0:T(8,128)(2,1)S(1)} %add_returned.1), channel_id=1, source_target_pairs={{0,4},{4,0},{8,12},{12,8},{16,20},{20,16},{24,28},{28,24},{1,5},{5... | collective-permute-start | bytes 786440 | tf_op jit(solution)/shard_map/ppermute | solution.py:403
  41.6 5.2 %collective-permute-start.15 = (bf16[32,1024]{1,0:T(8,128)(2,1)S(1)}, bf16[32,1024]{1,0:T(8,128)(2,1)S(1)}, u32[]{:S(2)}, u32[]{:S(2)}) collective-permute-start(bf16[32,1024]{1,0:T(8,128)(2,1)S(1)} %slice.36), channel_id=1, source_target_pairs={{0,16},{4,20},{8,24},{12,28},{16,0},{20,4},{24,8},{28,12},{1,17},{... | collective-permute-start | bytes 196616 | tf_op jit(solution)/shard_map/ppermute | solution.py:441

commit v7 on v6

--- a/solution.py
+++ b/solution.py
@@ -352,7 +352,7 @@
 
 def returned_kernel(d_par, far_a, far_b, total):
     slot = far_slot(lax.axis_index("seq"))
-    returned = jnp.where(slot == 0, far_b[...].astype(F32), far_a[...].astype(F32))
+    returned = jnp.where(slot == 0, far_b[...], far_a[...]).astype(F32)
     total[...] = (d_par[...].astype(F32) + returned).astype(BF16)
 
 
@@ -370,7 +370,7 @@
         rows = slice(i * tokens, (i + 1) * tokens)
         for j in range(own.shape[1] // HD):
             cols = slice(j * HD, (j + 1) * HD)
-            far = jnp.where(slot == 0, far_a[rows, cols].astype(F32), far_b[rows, cols].astype(F32))
+            far = jnp.where(slot == 0, far_a[rows, cols], far_b[rows, cols]).astype(F32)
             target[:, head_cols(j, mine)] = (own[rows, cols].astype(F32) + far).astype(BF16)
             target[:, head_cols(j, 1 - mine)] = home[rows, cols]
     total[...] = keep[...] + out[...].astype(F32)

time: 48.1 us -> 48.1 us (level)
  no operation moved by 1% of the time
where the time goes in v7:
time: 48.1 us; the launch traced here: 47.8 us
  starting transfers between devices  21.8 us (45%)
  waiting for transfers between devices  14.7 us (31%)
  Pallas kernels  10.3 us (21%)
  between operations  0.83 us (2%)
    ppermute x10, starting transfers between devices, on_device(): send = lambda x, pairs: lax.ppermute(x, 'seq', pairs)  16.8 us
    ppermute x10, waiting for transfers between devices, on_device(): send = lambda x, pairs: lax.ppermute(x, 'seq', pairs)  13.6 us
    ppermute x3, starting transfers between devices, on_device(): out = lax.ppermute(out, axis, [(i, i ^ bit) for i in range(count)])  4.89 us
    pallas_call x1, Pallas kernels, grad_attended(): call(turn_kernel, (shape_of(2 * tokens, pairs * HD),), [HBM, VMEM, HBM],...  2.32 us
    pallas_call x1, Pallas kernels, forward(): call(functools.partial(forward_kernel, direct, n_dp), (shape_of(pairs, 3...  1.57 us
    pallas_call x1, Pallas kernels, backward(): call(backward_kernel, (shape_of(*probs.shape),) + (shape_of(2 * tokens, h...  1.35 us
    pallas_call x1, Pallas kernels, pack(): call(pack_kernel, (kv, kv) + (shape_of(tokens + FLAG_ROWS, half),) * 2, [...  1.34 us
    pallas_call x1, Pallas kernels, finish_queries(): call(query_kernel, (shape_of(tokens, w.shape[1]), shape_of(tokens, w.shap...  1.19 us
  transfers between devices with their start and end apart: 16, of which 8 were waited for; matrix products, arithmetic and copies ran while one was open for 0% of the time, Pallas kernels for 16%

profile of v7, /device:TPU:0, one launch (start us, length us, event | category | flops | bytes accessed | tf_op | source)
XLA Modules:
  0.0 47.8 jit_solution(13834396922593987734)
XLA Ops:
  0.6 1.3 %pack_heads.1 = (bf16[256,512]{1,0:T(8,128)(2,1)S(1)}, bf16[256,512]{1,0:T(8,128)(2,1)S(1)}, bf16[144,512]{1,0:T(8,128)(2,1)S(1)}, bf16[144,512]{1,0:T(8,128)(2,1)S(1)}) custom-call(s32[1,2]{1,0:T(1,128)} %bitcast.21, bf16[128,1024]{1,0:T(8,128)(2,1)} %bitcast.18, bf16[128,1024]{1,0:T(8,128)(2,1)} %bitcast.19, bf16[128,1024]{1,0:T(8,128)(2,1)} %bitcast.20), custom_call_target="tpu_custom_call" | custom-call | tf_op jit(solution)/shard_map/pack_heads/pallas_call | solution.py:97
  2.0 3.0 %collective-permute-start.1 = (bf16[256,512]{1,0:T(8,128)(2,1)S(1)}, bf16[256,512]{1,0:T(8,128)(2,1)S(1)}, u32[]{:S(2)}, u32[]{:S(2)}) collective-permute-start(bf16[256,512]{1,0:T(8,128)(2,1)S(1)} %get-tuple-element.30), channel_id=1, source_target_pairs={{0,4},{4,0},{8,12},{12,8},{16,20},{20,16},{24,28},{28,24},{1,5},{5... | collective-permute-start | bytes 786440 | tf_op jit(solution)/shard_map/ppermute | solution.py:403
  5.0 0.1 collective-permute-start.4
  5.1 1.3 %collective-permute-start.3 = (bf16[256,512]{1,0:T(8,128)(2,1)S(1)}, bf16[256,512]{1,0:T(8,128)(2,1)S(1)}, u32[]{:S(2)}, u32[]{:S(2)}) collective-permute-start(bf16[256,512]{1,0:T(8,128)(2,1)S(1)} %get-tuple-element.29.own), channel_id=1, source_target_pairs={{8,0},{16,8},{24,16},{4,12},{12,20},{20,28},{9,1},{17,9},{25,17},{... | collective-permute-start | bytes 786440 | tf_op jit(solution)/shard_map/ppermute | solution.py:403
  6.4 5.8 %collective-permute-done.1.par = bf16[256,512]{1,0:T(8,128)(2,1)S(1)} collective-permute-done((bf16[256,512]{1,0:T(8,128)(2,1)S(1)}, bf16[256,512]{1,0:T(8,128)(2,1)S(1)}, u32[]{:S(2)}, u32[]{:S(2)}) %collective-permute-start.1) | collective-permute-done | bytes 262176 | tf_op jit(solution)/shard_map/ppermute | solution.py:403
  12.1 4.0 %collective-permute-start.2 = (bf16[256,512]{1,0:T(8,128)(2,1)S(1)}, bf16[256,512]{1,0:T(8,128)(2,1)S(1)}, u32[]{:S(2)}, u32[]{:S(2)}) collective-permute-start(bf16[256,512]{1,0:T(8,128)(2,1)S(1)} %collective-permute-done.1.par), channel_id=1, source_target_pairs={{0,8},{8,16},{16,24},{12,4},{20,12},{28,20},{1,9},{9,17},{17,25},{... | collective-permute-start | bytes 786440 | tf_op jit(solution)/shard_map/ppermute | solution.py:403
  16.2 0.1 collective-permute-start
  16.3 0.1 collective-permute-start.6
  16.3 1.1 %collective-permute-done.4.cot_par.par = bf16[128,1024]{1,0:T(8,128)(2,1)S(1)} collective-permute-done((bf16[128,1024]{1,0:T(8,128)(2,1)}, bf16[128,1024]{1,0:T(8,128)(2,1)S(1)}, u32[]{:S(2)}, u32[]{:S(2)}) %collective-permute-start.4) | collective-permute-done | bytes 262176 | tf_op jit(solution)/shard_map/ppermute | solution.py:403
  17.4 0.0 collective-permute-start.7
  17.4 2.3 %grad_attended.1.after.ga = bf16[256,512]{1,0:T(8,128)(2,1)S(1)} custom-call(bf16[128,1024]{1,0:T(8,128)(2,1)} %bitcast.15, bf16[128,1024]{1,0:T(8,128)(2,1)S(1)} %collective-permute-done.4.cot_par.par, bf16[1024,1024]{1,0:T(8,128)(2,1)} %w.3), custom_call_target="tpu_custom_call" | custom-call | tf_op jit(solution)/shard_map/grad_attended/pallas_call | solution.py:129
  19.8 1.6 %collective-permute-done.q_par = bf16[144,512]{1,0:T(8,128)(2,1)S(1)} collective-permute-done((bf16[144,512]{1,0:T(8,128)(2,1)S(1)}, bf16[144,512]{1,0:T(8,128)(2,1)S(1)}, u32[]{:S(2)}, u32[]{:S(2)}) %collective-permute-start) | collective-permute-done | bytes 147488 | tf_op jit(solution)/shard_map/ppermute | solution.py:403
  21.4 0.0 collective-permute-done.3.far_par
  21.4 0.0 collective-permute-done.2.far_own
  21.4 0.0 copy-start.1
  21.4 1.6 %patch_forward.1 = (bf16[4,384,256]{2,1,0:T(8,128)(2,1)S(1)}, bf16[128,512]{1,0:T(8,128)(2,1)S(1)}, bf16[128,512]{1,0:T(8,128)(2,1)S(1)}, bf16[2,256,256]{2,1,0:T(8,128)(2,1)S(1)}) custom-call(bf16[144,512]{1,0:T(8,128)(2,1)S(1)} %get-tuple-element.27.q_own, bf16[144,512]{1,0:T(8,128)(2,1)S(1)} %collective-permute-done.q_par, ...), custom_call_target="tpu_custom_call" | custom-call | tf_op jit(solution)/shard_map/patch_forward/pallas_call | solution.py:209
  23.0 0.1 collective-permute-start.5
  23.1 1.3 %patch_backward.1 = (bf16[4,384,256]{2,1,0:T(8,128)(2,1)S(1)}, bf16[256,512]{1,0:T(8,128)(2,1)S(1)}, bf16[256,512]{1,0:T(8,128)(2,1)S(1)}) custom-call(bf16[144,512]{1,0:T(8,128)(2,1)S(1)} %get-tuple-element.27.q_own, bf16[144,512]{1,0:T(8,128)(2,1)S(1)} %collective-permute-done.q_par, bf16[256,512]{1,0:T(8,128)(2,1)S(1)} %get-tuple-element.29.own, ...), custom_call_target="tpu_custom_call" | custom-call | tf_op jit(solution)/shard_map/patch_backward/pallas_call | solution.py:269
  24.4 0.0 collective-permute-done.6.core_own
  24.4 0.0 collective-permute-done.7.core_par
  24.5 0.0 collective-permute-done.5.att_core
  24.5 0.0 copy-done.1
  24.5 0.4 weight_terms_sent.1._after
  24.9 1.6 %collective-permute-start.8 = (bf16[128,1024]{1,0:T(8,128)(2,1)S(1)}, bf16[128,1024]{1,0:T(8,128)(2,1)S(1)}, u32[]{:S(2)}, u32[]{:S(2)}) collective-permute-start(bf16[128,1024]{1,0:T(8,128)(2,1)S(1)} %weight_terms_sent.1._after), channel_id=1, source_target_pairs={{0,2},{1,3},{2,0},{3,1},{4,6},{5,7},{6,4},{7,5},{8,10},{9,11},{10,... | collective-permute-start | bytes 786440 | tf_op jit(solution)/shard_map/ppermute | solution.py:441
  26.5 1.3 %collective-permute-start.9 = (bf16[128,512]{1,0:T(8,128)(2,1)S(1)}, bf16[128,512]{1,0:T(8,128)(2,1)S(1)}, u32[]{:S(2)}, u32[]{:S(2)}) collective-permute-start(bf16[128,512]{1,0:T(8,128)(2,1)S(1)} %get-tuple-element.35), channel_id=1, source_target_pairs={{0,4},{4,0},{8,12},{12,8},{16,20},{20,16},{24,28},{28,24},{1,5},{5... | collective-permute-start | bytes 393224 | tf_op jit(solution)/shard_map/ppermute | solution.py:403
  27.8 0.7 %collective-permute-start.11 = (bf16[256,512]{1,0:T(8,128)(2,1)S(1)}, bf16[256,512]{1,0:T(8,128)(2,1)S(1)}, u32[]{:S(2)}, u32[]{:S(2)}) collective-permute-start(bf16[256,512]{1,0:T(8,128)(2,1)S(1)} %get-tuple-element.34._after), channel_id=1, source_target_pairs={{8,16},{12,20},{16,8},{20,12},{9,17},{13,21},{17,9},{21,13},{10,18... | collective-permute-start | bytes 786440 | tf_op jit(solution)/shard_map/ppermute | solution.py:403
  28.4 4.5 %collective-permute-start.12 = (bf16[256,512]{1,0:T(8,128)(2,1)S(1)}, bf16[256,512]{1,0:T(8,128)(2,1)S(1)}, u32[]{:S(2)}, u32[]{:S(2)}) collective-permute-start(bf16[256,512]{1,0:T(8,128)(2,1)S(1)} %get-tuple-element.43), channel_id=1, source_target_pairs={{0,8},{4,12},{8,0},{12,4},{16,24},{20,28},{24,16},{28,20},{1,9},{5... | collective-permute-start | bytes 786440 | tf_op jit(solution)/shard_map/ppermute | solution.py:403
  32.9 0.4 weight_terms_kept.1
  33.3 0.0 collective-permute-done.9.att_back
  33.3 0.4 collective-permute-done.8
  33.7 0.1 convert_add_fusion
  33.8 1.6 %collective-permute-start.14 = (bf16[64,1024]{1,0:T(8,128)(2,1)S(1)}, bf16[64,1024]{1,0:T(8,128)(2,1)S(1)}, u32[]{:S(2)}, u32[]{:S(2)}) collective-permute-start(bf16[64,1024]{1,0:T(8,128)(2,1)S(1)} %slice.35), channel_id=1, source_target_pairs={{0,8},{4,12},{8,0},{12,4},{16,24},{20,28},{24,16},{28,20},{1,9},{5... | collective-permute-start | bytes 393224 | tf_op jit(solution)/shard_map/ppermute | solution.py:441
  35.4 0.0 copy-start
  35.4 0.7 %patch_gradients.1 = (bf16[128,512]{1,0:T(8,128)(2,1)S(1)}, bf16[128,512]{1,0:T(8,128)(2,1)S(1)}, bf16[256,512]{1,0:T(8,128)(2,1)S(1)}, bf16[256,512]{1,0:T(8,128)(2,1)S(1)}) custom-call(bf16[144,512]{1,0:T(8,128)(2,1)S(1)} %get-tuple-element.27.q_own, bf16[144,512]{1,0:T(8,128)(2,1)S(1)} %collective-permute-done.q_par, ...), custom_call_target="tpu_custom_call" | custom-call | tf_op jit(solution)/shard_map/patch_gradients/pallas_call | solution.py:305
  36.1 1.1 %collective-permute-start.10 = (bf16[128,512]{1,0:T(8,128)(2,1)S(1)}, bf16[128,512]{1,0:T(8,128)(2,1)S(1)}, u32[]{:S(2)}, u32[]{:S(2)}) collective-permute-start(bf16[128,512]{1,0:T(8,128)(2,1)S(1)} %get-tuple-element.39), channel_id=1, source_target_pairs={{0,4},{4,0},{8,12},{12,8},{16,20},{20,16},{24,28},{28,24},{1,5},{5... | collective-permute-start | bytes 393224 | tf_op jit(solution)/shard_map/ppermute | solution.py:403
  37.2 2.9 %collective-permute-done.12.far_b = bf16[256,512]{1,0:T(8,128)(2,1)S(1)} collective-permute-done((bf16[256,512]{1,0:T(8,128)(2,1)S(1)}, bf16[256,512]{1,0:T(8,128)(2,1)S(1)}, u32[]{:S(2)}, u32[]{:S(2)}) %collective-permute-start.12) | collective-permute-done | bytes 262176 | tf_op jit(solution)/shard_map/ppermute | solution.py:403
  40.1 0.0 collective-permute-done.11.far_a
  40.1 0.1 add_returned.1
  40.2 0.8 %collective-permute-start.13 = (bf16[256,512]{1,0:T(8,128)(2,1)S(1)}, bf16[256,512]{1,0:T(8,128)(2,1)S(1)}, u32[]{:S(2)}, u32[]{:S(2)}) collective-permute-start(bf16[256,512]{1,0:T(8,128)(2,1)S(1)} %add_returned.1), channel_id=1, source_target_pairs={{0,4},{4,0},{8,12},{12,8},{16,20},{20,16},{24,28},{28,24},{1,5},{5... | collective-permute-start | bytes 786440 | tf_op jit(solution)/shard_map/ppermute | solution.py:403
  40.9 0.7 %collective-permute-done.14 = bf16[64,1024]{1,0:T(8,128)(2,1)S(1)} collective-permute-done((bf16[64,1024]{1,0:T(8,128)(2,1)S(1)}, bf16[64,1024]{1,0:T(8,128)(2,1)S(1)}, u32[]{:S(2)}, u32[]{:S(2)}) %collective-permute-start.14) | collective-permute-done | bytes 131104 | tf_op jit(solution)/shard_map/ppermute | solution.py:441
  41.6 1.7 %collective-permute-start.15 = (bf16[32,1024]{1,0:T(8,128)(2,1)S(1)}, bf16[32,1024]{1,0:T(8,128)(2,1)S(1)}, u32[]{:S(2)}, u32[]{:S(2)}) collective-permute-start(bf16[32,1024]{1,0:T(8,128)(2,1)S(1)} %slice.36), channel_id=1, source_target_pairs={{0,16},{4,20},{8,24},{12,28},{16,0},{20,4},{24,8},{28,12},{1,17},{... | collective-permute-start | bytes 196616 | tf_op jit(solution)/shard_map/ppermute | solution.py:441
  43.3 0.0 collective-permute-done.10.dq_back
  43.3 0.0 copy-done
  43.3 1.2 %finish_queries.1 = (bf16[128,1024]{1,0:T(8,128)(2,1)}, bf16[128,1024]{1,0:T(8,128)(2,1)}) custom-call(bf16[128,512]{1,0:T(8,128)(2,1)S(1)} %get-tuple-element.31.att_own, bf16[128,512]{1,0:T(8,128)(2,1)S(1)} %collective-permute-done.9.att_back, bf16[128,512]{1,0:T(8,128)(2,1)S(1)} %get-tuple-element.38.dq_own, ...), custom_call_target="tpu_custom_call" | custom-call | tf_op jit(solution)/shard_map/finish_queries/pallas_call | solution.py:344
  44.5 2.2 %collective-permute-done.13.home = bf16[256,512]{1,0:T(8,128)(2,1)S(1)} collective-permute-done((bf16[256,512]{1,0:T(8,128)(2,1)S(1)}, bf16[256,512]{1,0:T(8,128)(2,1)S(1)}, u32[]{:S(2)}, u32[]{:S(2)}) %collective-permute-start.13) | collective-permute-done | bytes 262176 | tf_op jit(solution)/shard_map/ppermute | solution.py:403
  46.7 0.2 collective-permute-done.15.out
  46.9 1.0 %finish_keys.1 = (bf16[128,1024]{1,0:T(8,128)(2,1)}, bf16[128,1024]{1,0:T(8,128)(2,1)}, f32[32,1024]{1,0:T(8,128)}) custom-call(bf16[256,512]{1,0:T(8,128)(2,1)S(1)} %get-tuple-element.42.own, bf16[256,512]{1,0:T(8,128)(2,1)S(1)} %collective-permute-done.11.far_a, bf16[256,512]{1,0:T(8,128)(2,1)S(1)} %collective-permute-done.12.far_b, ...), custom_call_target="tpu_custom_call" | custom-call | tf_op jit(solution)/shard_map/finish_keys/pallas_call | solution.py:381
  (5 shorter events, 0.1 us)
Async XLA Ops:
  2.0 10.2 %collective-permute-start.1 = (bf16[256,512]{1,0:T(8,128)(2,1)S(1)}, bf16[256,512]{1,0:T(8,128)(2,1)S(1)}, u32[]{:S(2)}, u32[]{:S(2)}) collective-permute-start(bf16[256,512]{1,0:T(8,128)(2,1)S(1)} %get-tuple-element.30), channel_id=1, source_target_pairs={{0,4},{4,0},{8,12},{12,8},{16,20},{20,16},{24,28},{28,24},{1,5},{5... | collective-permute-start | bytes 786440 | tf_op jit(solution)/shard_map/ppermute | solution.py:403
  5.0 12.4 %collective-permute-start.4 = (bf16[128,1024]{1,0:T(8,128)(2,1)}, bf16[128,1024]{1,0:T(8,128)(2,1)S(1)}, u32[]{:S(2)}, u32[]{:S(2)}) collective-permute-start(bf16[128,1024]{1,0:T(8,128)(2,1)} %bitcast.13), channel_id=1, source_target_pairs={{0,4},{4,0},{8,12},{12,8},{16,20},{20,16},{24,28},{28,24},{1,5},{5... | collective-permute-start | bytes 786440 | tf_op jit(solution)/shard_map/ppermute | solution.py:403
  5.1 16.3 %collective-permute-start.3 = (bf16[256,512]{1,0:T(8,128)(2,1)S(1)}, bf16[256,512]{1,0:T(8,128)(2,1)S(1)}, u32[]{:S(2)}, u32[]{:S(2)}) collective-permute-start(bf16[256,512]{1,0:T(8,128)(2,1)S(1)} %get-tuple-element.29.own), channel_id=1, source_target_pairs={{8,0},{16,8},{24,16},{4,12},{12,20},{20,28},{9,1},{17,9},{25,17},{... | collective-permute-start | bytes 786440 | tf_op jit(solution)/shard_map/ppermute | solution.py:403
  12.1 9.2 %collective-permute-start.2 = (bf16[256,512]{1,0:T(8,128)(2,1)S(1)}, bf16[256,512]{1,0:T(8,128)(2,1)S(1)}, u32[]{:S(2)}, u32[]{:S(2)}) collective-permute-start(bf16[256,512]{1,0:T(8,128)(2,1)S(1)} %collective-permute-done.1.par), channel_id=1, source_target_pairs={{0,8},{8,16},{16,24},{12,4},{20,12},{28,20},{1,9},{9,17},{17,25},{... | collective-permute-start | bytes 786440 | tf_op jit(solution)/shard_map/ppermute | solution.py:403
  16.2 5.2 %collective-permute-start = (bf16[144,512]{1,0:T(8,128)(2,1)S(1)}, bf16[144,512]{1,0:T(8,128)(2,1)S(1)}, u32[]{:S(2)}, u32[]{:S(2)}) collective-permute-start(bf16[144,512]{1,0:T(8,128)(2,1)S(1)} %get-tuple-element.28), channel_id=1, source_target_pairs={{0,4},{4,0},{8,12},{12,8},{16,20},{20,16},{24,28},{28,24},{1,5},{5... | collective-permute-start | bytes 442376 | tf_op jit(solution)/shard_map/ppermute | solution.py:403
  16.3 8.2 %collective-permute-start.6 = (bf16[128,1024]{1,0:T(8,128)(2,1)}, bf16[128,1024]{1,0:T(8,128)(2,1)S(1)}, u32[]{:S(2)}, u32[]{:S(2)}) collective-permute-start(bf16[128,1024]{1,0:T(8,128)(2,1)} %bitcast.14), channel_id=1, source_target_pairs={{0,1},{1,0},{2,3},{3,2},{4,5},{5,4},{6,7},{7,6},{8,9},{9,8},{10,11... | collective-permute-start | bytes 786440 | tf_op jit(solution)/shard_map/ppermute | solution.py:404
  17.4 7.0 %collective-permute-start.7 = (bf16[128,1024]{1,0:T(8,128)(2,1)S(1)}, bf16[128,1024]{1,0:T(8,128)(2,1)S(1)}, u32[]{:S(2)}, u32[]{:S(2)}) collective-permute-start(bf16[128,1024]{1,0:T(8,128)(2,1)S(1)} %collective-permute-done.4.cot_par.par), channel_id=1, source_target_pairs={{0,1},{1,0},{2,3},{3,2},{4,5},{5,4},{6,7},{7,6},{8,9},{9,8},{10,11... | collective-permute-start | bytes 786440 | tf_op jit(solution)/shard_map/ppermute | solution.py:404
  21.4 3.1 %copy-start.1 = (bf16[1,128,1024]{2,1,0:T(8,128)(2,1)S(1)}, bf16[1,128,1024]{2,1,0:T(8,128)(2,1)}, u32[]{:S(2)}) copy-start(bf16[1,128,1024]{2,1,0:T(8,128)(2,1)} %param.11) | copy-start | bytes 786436
  23.0 1.5 %collective-permute-start.5 = (bf16[256,256]{1,0:T(8,128)(2,1)S(1)}, bf16[256,256]{1,0:T(8,128)(2,1)S(1)}, u32[]{:S(2)}, u32[]{:S(2)}) collective-permute-start(bf16[256,256]{1,0:T(8,128)(2,1)S(1)} %get-tuple-element.49), channel_id=1, source_target_pairs={{0,1},{1,0},{2,3},{3,2},{4,5},{5,4},{6,7},{7,6},{8,9},{9,8},{10,11... | collective-permute-start | bytes 393224 | tf_op jit(solution)/shard_map/ppermute | solution.py:404
  24.9 8.8 %collective-permute-start.8 = (bf16[128,1024]{1,0:T(8,128)(2,1)S(1)}, bf16[128,1024]{1,0:T(8,128)(2,1)S(1)}, u32[]{:S(2)}, u32[]{:S(2)}) collective-permute-start(bf16[128,1024]{1,0:T(8,128)(2,1)S(1)} %weight_terms_sent.1._after), channel_id=1, source_target_pairs={{0,2},{1,3},{2,0},{3,1},{4,6},{5,7},{6,4},{7,5},{8,10},{9,11},{10,... | collective-permute-start | bytes 786440 | tf_op jit(solution)/shard_map/ppermute | solution.py:441
  26.5 6.8 %collective-permute-start.9 = (bf16[128,512]{1,0:T(8,128)(2,1)S(1)}, bf16[128,512]{1,0:T(8,128)(2,1)S(1)}, u32[]{:S(2)}, u32[]{:S(2)}) collective-permute-start(bf16[128,512]{1,0:T(8,128)(2,1)S(1)} %get-tuple-element.35), channel_id=1, source_target_pairs={{0,4},{4,0},{8,12},{12,8},{16,20},{20,16},{24,28},{28,24},{1,5},{5... | collective-permute-start | bytes 393224 | tf_op jit(solution)/shard_map/ppermute | solution.py:403
  27.8 12.3 %collective-permute-start.11 = (bf16[256,512]{1,0:T(8,128)(2,1)S(1)}, bf16[256,512]{1,0:T(8,128)(2,1)S(1)}, u32[]{:S(2)}, u32[]{:S(2)}) collective-permute-start(bf16[256,512]{1,0:T(8,128)(2,1)S(1)} %get-tuple-element.34._after), channel_id=1, source_target_pairs={{8,16},{12,20},{16,8},{20,12},{9,17},{13,21},{17,9},{21,13},{10,18... | collective-permute-start | bytes 786440 | tf_op jit(solution)/shard_map/ppermute | solution.py:403
  28.4 11.6 %collective-permute-start.12 = (bf16[256,512]{1,0:T(8,128)(2,1)S(1)}, bf16[256,512]{1,0:T(8,128)(2,1)S(1)}, u32[]{:S(2)}, u32[]{:S(2)}) collective-permute-start(bf16[256,512]{1,0:T(8,128)(2,1)S(1)} %get-tuple-element.43), channel_id=1, source_target_pairs={{0,8},{4,12},{8,0},{12,4},{16,24},{20,28},{24,16},{28,20},{1,9},{5... | collective-permute-start | bytes 786440 | tf_op jit(solution)/shard_map/ppermute | solution.py:403
  33.8 7.8 %collective-permute-start.14 = (bf16[64,1024]{1,0:T(8,128)(2,1)S(1)}, bf16[64,1024]{1,0:T(8,128)(2,1)S(1)}, u32[]{:S(2)}, u32[]{:S(2)}) collective-permute-start(bf16[64,1024]{1,0:T(8,128)(2,1)S(1)} %slice.35), channel_id=1, source_target_pairs={{0,8},{4,12},{8,0},{12,4},{16,24},{20,28},{24,16},{28,20},{1,9},{5... | collective-permute-start | bytes 393224 | tf_op jit(solution)/shard_map/ppermute | solution.py:441
  35.4 7.9 %copy-start = (bf16[1024,1024]{1,0:T(8,128)(2,1)S(1)}, bf16[1024,1024]{1,0:T(8,128)(2,1)}, u32[]{:S(2)}) copy-start(bf16[1024,1024]{1,0:T(8,128)(2,1)} %w.3) | copy-start | bytes 6291460
  36.1 7.3 %collective-permute-start.10 = (bf16[128,512]{1,0:T(8,128)(2,1)S(1)}, bf16[128,512]{1,0:T(8,128)(2,1)S(1)}, u32[]{:S(2)}, u32[]{:S(2)}) collective-permute-start(bf16[128,512]{1,0:T(8,128)(2,1)S(1)} %get-tuple-element.39), channel_id=1, source_target_pairs={{0,4},{4,0},{8,12},{12,8},{16,20},{20,16},{24,28},{28,24},{1,5},{5... | collective-permute-start | bytes 393224 | tf_op jit(solution)/shard_map/ppermute | solution.py:403
  40.2 6.6 %collective-permute-start.13 = (bf16[256,512]{1,0:T(8,128)(2,1)S(1)}, bf16[256,512]{1,0:T(8,128)(2,1)S(1)}, u32[]{:S(2)}, u32[]{:S(2)}) collective-permute-start(bf16[256,512]{1,0:T(8,128)(2,1)S(1)} %add_returned.1), channel_id=1, source_target_pairs={{0,4},{4,0},{8,12},{12,8},{16,20},{20,16},{24,28},{28,24},{1,5},{5... | collective-permute-start | bytes 786440 | tf_op jit(solution)/shard_map/ppermute | solution.py:403
  41.6 5.2 %collective-permute-start.15 = (bf16[32,1024]{1,0:T(8,128)(2,1)S(1)}, bf16[32,1024]{1,0:T(8,128)(2,1)S(1)}, u32[]{:S(2)}, u32[]{:S(2)}) collective-permute-start(bf16[32,1024]{1,0:T(8,128)(2,1)S(1)} %slice.36), channel_id=1, source_target_pairs={{0,16},{4,20},{8,24},{12,28},{16,0},{20,4},{24,8},{28,12},{1,17},{... | collective-permute-start | bytes 196616 | tf_op jit(solution)/shard_map/ppermute | solution.py:441
